TPU v7x, 32 devices: a whole 2x2x4 slice. The times are simulated.
32 devices in a mesh: ka: 8 (over z, core), row: 4 (over y, x).
Axes of the slice: x: 2, y: 2, z: 4, core: 2. Of those that a mesh axis runs over, the one named last changes fastest.
Arguments:
- frames: bfloat16 [2, 1024, 64, 256], P(None, 'ka', 'row'), may hold values from -16 to 16
Outputs:
- decorrelation: float32 [512, 64, 256], P('ka', 'row')
All inputs are finite; a program needn't handle non-finite values.
Results may differ from a plain program's by a relative error of at most 0.002.
Values may be sent and summed in bfloat16 or wider, within the bound.
No kernel may reach another device: no remote copies, remote signals or barrier semaphores. Data moves between devices by JAX's collectives and lax.ppermute only.
A program may use at most 128 MiB of HBM per device.

v0:
```python
import math

import jax
import jax.numpy as jnp
from jax import lax
from jax.sharding import PartitionSpec as P

K = 1024
DEPTH = 512


def with_halo(x, sides, width):
    for axis, dim in sides:
        count, length = (lax.axis_size(axis), x.shape[dim])
        up = [(i, (i + 1) % count) for i in range(count - 1)]
        down = [(j, i) for i, j in up]
        last = lax.slice_in_dim(x, length - width, length, axis=dim)
        first = lax.slice_in_dim(x, 0, width, axis=dim)
        before = lax.ppermute(last, axis, up)
        after = lax.ppermute(first, axis, down)
        x = jnp.concatenate([before, x, after], axis=dim)
    return x


def dft_tables(kpos, zpos, size):
    phase = kpos[:, None] * zpos[None, :] % size
    angle = phase.astype(jnp.float32) * (2.0 * math.pi / size)
    return (jnp.cos(angle).astype(jnp.bfloat16), jnp.sin(angle).astype(jnp.bfloat16))


def transform(samples, cos_table, sin_table):
    real = jnp.einsum("kz,pk...->zp...", cos_table, samples, preferred_element_type=jnp.float32)
    imag = -jnp.einsum("kz,pk...->zp...", sin_table, samples, preferred_element_type=jnp.float32)
    both = jnp.stack((real, imag), axis=2)
    return both.reshape((both.shape[0], both.shape[1] * 2) + both.shape[3:])


def products(spectrum):
    wide = spectrum.astype(jnp.float32)
    a_one, b_one = (wide[:, 0], wide[:, 1])
    a_two, b_two = (wide[:, 2], wide[:, 3])
    cross_re = a_one * a_two + b_one * b_two
    cross_im = b_one * a_two - a_one * b_two
    power = (a_one * a_one + b_one * b_one + a_two * a_two + b_two * b_two) / 2.0
    return jnp.stack((cross_re, cross_im, power), axis=0)


def body(frames):
    scale = float(K) ** (-0.5)
    local_k = frames.shape[1]
    kpos = lax.axis_index("ka") * local_k + jnp.arange(local_k, dtype=jnp.int32)
    zpos = jnp.arange(DEPTH // lax.axis_size("ka") * lax.axis_size("ka"), dtype=jnp.int32)
    cos_table, sin_table = dft_tables(kpos, zpos, K)
    summed = lax.psum_scatter(
        transform(frames, cos_table, sin_table), "ka", scatter_dimension=0, tiled=True
    )
    spectrum = (summed * scale).astype(jnp.bfloat16)
    padded = with_halo(products(spectrum), (("ka", 1), ("row", 2)), 1)
    summed = padded[:, :-2] + padded[:, 1:-1] + padded[:, 2:]
    summed = summed[:, :, :-2] + summed[:, :, 1:-1] + summed[:, :, 2:]
    widened = jnp.pad(summed, ((0, 0), (0, 0), (0, 0), (1, 1)))
    summed = widened[:, :, :, :-2] + widened[:, :, :, 1:-1] + widened[:, :, :, 2:]
    magnitude = jnp.sqrt(summed[0] * summed[0] + summed[1] * summed[1])
    return 1.0 - magnitude / (summed[2] + 1e-05)


def solution(mesh):
    in_specs = (P(None, "ka", "row", None),)
    out_specs = P("ka", "row", None)
    return jax.shard_map(body, mesh=mesh, in_specs=in_specs, out_specs=out_specs, check_vma=False)
```

profile of v0, /device:TPU:1, one launch (start us, length us, event | category | flops | bytes accessed | tf_op | source)
XLA Modules:
  0.0 440.4 jit_solution(12222323758243000887)
XLA Ops:
  6.5 0.0 copy-start
  6.5 0.0 reduce-scatter.2.cloned.1.call-start
  6.5 1.6 copy-done
  8.1 9.0 %negate_bitcast_fusion = f32[512,2,1,16,256]{4,0,3,1,2:T(8,128)} fusion(bf16[2,128,16,256]{3,2,1,0:T(8,128)(2,1)S(1)} %copy-done, s32[128]{0:T(128)S(1)} %iota_add_fusion), kind=kOutput, calls=%fused_computation.1 | convolution fusion | flops 1078919168 | bytes 18874880 | tf_op jit(solution)/shard_map/kz,pk...->zp.../dot_general | solution.py:33
  17.1 9.0 %convolution_bitcast_fusion = f32[512,2,1,16,256]{4,0,3,1,2:T(8,128)} fusion(bf16[2,128,16,256]{3,2,1,0:T(8,128)(2,1)S(1)} %copy-done, s32[128]{0:T(128)S(1)} %iota_add_fusion), kind=kOutput, calls=%fused_computation.2 | convolution fusion | flops 1074724864 | bytes 18874880 | tf_op jit(solution)/shard_map/kz,pk...->zp.../dot_general | solution.py:32
  26.1 12.4 %pad_maximum_fusion = f32[512,2,2,16,256]{4,0,3,1,2:T(8,128)S(1)} fusion(f32[512,2,1,16,256]{4,0,3,1,2:T(8,128)} %negate_bitcast_fusion, f32[512,2,1,16,256]{4,0,3,1,2:T(8,128)} %convolution_bitcast_fusion), kind=kLoop, calls=%fused_computation | loop fusion | flops 8388608 | bytes 67108864 | tf_op jit(solution)/shard_map/stack | solution.py:34
  38.5 38.1 %copy.6 = f32[512,2,2,16,256]{4,3,2,1,0:T(8,128)} copy(f32[512,2,2,16,256]{4,0,3,1,2:T(8,128)S(1)} %pad_maximum_fusion) | data formatting | bytes 67108864 | tf_op jit(solution)/shard_map/stack | solution.py:34
  76.6 0.0 reduce-scatter.2.cloned.1.call-update
  76.6 325.6 %reduce-scatter.2.cloned.1.call-done = f32[64,4,16,256]{3,2,1,0:T(8,128)} async-done(((f32[512,4,16,256]{3,2,1,0:T(8,128)}), f32[64,4,16,256]{3,2,1,0:T(8,128)}) %reduce-scatter.2.cloned.1.call-update) | async-done | bytes 4194320 | tf_op jit(solution)/shard_map/reduce_scatter | solution.py:54
  402.2 2.8 fusion.2
  405.0 0.5 fusion.11
  405.5 0.5 fusion.13
  406.0 2.9 collective-permute-start
  408.9 3.1 collective-permute-start.1
  412.0 0.0 collective-permute-done
  412.1 2.3 collective-permute-done.1
  414.4 0.4 pad_maximum_fusion.6
  414.7 3.2 collective-permute-start.2
  417.9 1.3 collective-permute-start.3
  419.2 2.8 collective-permute-done.2
  422.0 6.0 %collective-permute-done.3 = f32[3,66,1,256]{3,2,1,0:T(1,128)S(1)} collective-permute-done((f32[3,66,1,256]{3,2,1,0:T(1,128)S(1)}, f32[3,66,1,256]{3,2,1,0:T(1,128)S(1)}, u32[]{:S(2)}, u32[]{:S(2)}) %collective-permute-start.3) | collective-permute-done | bytes 202784 | tf_op jit(solution)/shard_map/ppermute | solution.py:20
  428.0 1.2 pad_maximum_fusion.1
  429.2 0.5 slice_add_fusion
  429.7 0.0 copy-start.1
  429.7 0.7 slice_add_fusion.2
  430.4 1.7 fusion.1
  432.1 1.5 fusion.7
  433.5 0.0 copy-done.1
  (2 shorter events, 0.0 us)
Async XLA Ops:
  6.5 1.6 copy-start
  6.5 395.7 %reduce-scatter.2.cloned.1.call-start = ((), (), s32[]{:S(2)}) async-start(), calls=%async_computation.1 | async-start | bytes 37748736 | tf_op jit(solution)/shard_map/reduce_scatter | solution.py:54
  406.0 6.0 %collective-permute-start = (f32[3,1,16,256]{3,2,1,0:T(8,128)S(1)}, f32[3,1,16,256]{3,2,1,0:T(8,128)S(1)}, u32[]{:S(2)}, u32[]{:S(2)}) collective-permute-start(f32[3,1,16,256]{3,2,1,0:T(8,128)S(1)} %get-tuple-element.9), channel_id=1, source_target_pairs={{0,4},{4,8},{8,12},{12,16},{16,20},{20,24},{24,28},{1,5},{5,9},{9,... | collective-permute-start | bytes 147464 | tf_op jit(solution)/shard_map/ppermute | solution.py:19
  408.9 5.4 %collective-permute-start.1 = (f32[3,1,16,256]{3,2,1,0:T(8,128)S(1)}, f32[3,1,16,256]{3,2,1,0:T(8,128)S(1)}, u32[]{:S(2)}, u32[]{:S(2)}) collective-permute-start(f32[3,1,16,256]{3,2,1,0:T(8,128)S(1)} %get-tuple-element.10), channel_id=1, source_target_pairs={{4,0},{8,4},{12,8},{16,12},{20,16},{24,20},{28,24},{5,1},{9,5},{13... | collective-permute-start | bytes 147464 | tf_op jit(solution)/shard_map/ppermute | solution.py:20
  414.7 7.3 %collective-permute-start.2 = (f32[3,66,1,256]{3,2,1,0:T(1,128)S(1)}, f32[3,66,1,256]{3,2,1,0:T(1,128)S(1)}, u32[]{:S(2)}, u32[]{:S(2)}) collective-permute-start(f32[3,66,1,256]{3,2,1,0:T(1,128)S(1)} %get-tuple-element.7), channel_id=1, source_target_pairs={{0,1},{1,2},{2,3},{4,5},{5,6},{6,7},{8,9},{9,10},{10,11},{12,13},{... | collective-permute-start | bytes 608264 | tf_op jit(solution)/shard_map/ppermute | solution.py:19
  417.9 10.1 %collective-permute-start.3 = (f32[3,66,1,256]{3,2,1,0:T(1,128)S(1)}, f32[3,66,1,256]{3,2,1,0:T(1,128)S(1)}, u32[]{:S(2)}, u32[]{:S(2)}) collective-permute-start(f32[3,66,1,256]{3,2,1,0:T(1,128)S(1)} %get-tuple-element.8), channel_id=1, source_target_pairs={{1,0},{2,1},{3,2},{5,4},{6,5},{7,6},{9,8},{10,9},{11,10},{13,12},{... | collective-permute-start | bytes 608264 | tf_op jit(solution)/shard_map/ppermute | solution.py:20
  429.7 3.9 copy-start.1
Sparse Core Ops, SparseCore 0:
  76.7 325.4 reduce-scatter.1
where the time goes:
time: 441 us; the launch traced here: 440 us
  waiting for transfers between devices  337 us (76%)
  local copies, waits for them, and re-layouts  39.7 us (9%)
  other arithmetic  22 us (5%)
  matrix products  18 us (4%)
  between operations  13.5 us (3%)
  starting transfers between devices  10.5 us (2%)
    reduce_scatter x1, waiting for transfers between devices, body(): lax.psum_scatter(transform(frames, cos_table, sin_table), 'ka', scatter_d...  326 us
    another operation x1, local copies, waits for them, and re-layouts, transform(): both = jnp.stack((real, imag), axis=2)  38.1 us
    another operation x1, other arithmetic, transform(): both = jnp.stack((real, imag), axis=2)  12.4 us
    dot_general x1, matrix products, transform(): jnp.einsum('kz,pk...->zp...', sin_table, samples, preferred_element_type=...  9.01 us
    dot_general x1, matrix products, transform(): jnp.einsum('kz,pk...->zp...', cos_table, samples, preferred_element_type=...  8.96 us
  transfers between devices with their start and end apart: 5, of which 4 were waited for; matrix products, arithmetic and copies ran while one was open for 0% of the time, Pallas kernels for 0%

commit v1 on v0

v1 whole, which is shorter than its diff:
```python
import functools
import math

import jax
import jax.numpy as jnp
import numpy as np
from jax import lax
from jax.experimental import pallas as pl
from jax.experimental.pallas import tpu as pltpu
from jax.sharding import PartitionSpec as P

K = 1024
DEPTH = 512
LANES = 128
EDGE = 16
F32 = jnp.float32
BF16 = jnp.bfloat16


def table():
    phase = (np.arange(K)[None, :] * np.arange(DEPTH)[:, None]) % K
    angle = phase.astype(np.float32) * np.float32(2.0 * math.pi / K)
    both = np.concatenate([np.cos(angle), np.sin(angle)], axis=0)
    return both.astype(jnp.bfloat16)


def place(dest, half, rb, mirrored):
    h = dest // half
    q = dest % half
    q = jnp.where(mirrored, half - 1 - q, q)
    return h, q * rb


def params(mib=48):
    return pltpu.CompilerParams(vmem_limit_bytes=mib * 1024 * 1024)


def split_kernel(n, rows, kl, rb, first, rest, x_ref, *refs):
    half = n // 2
    a_refs, b_refs = refs[:n], refs[n : n + (n if rest else 0)]
    x32, e_scr, e16 = refs[-3:]
    me = lax.axis_index("ka")
    mirrored = lax.axis_index("row") % 2 == 1
    x32[0] = x_ref[:, :LANES].astype(F32)
    x32[1] = x_ref[:, LANES:].astype(F32)
    lane = lax.broadcasted_iota(jnp.int32, (kl, LANES), 1)
    for h in range(2):
        m = jnp.zeros((kl, LANES), F32)
        for p in range(2):
            for r in range(rows):
                at = p * rows + r
                y = x32[1 - h, pl.ds(p * kl * rows + r, kl, stride=rows), :]
                m = jnp.where(lane == at, pltpu.roll(y, (at + h) % LANES, 1), m)
        if kl < LANES:
            m = jnp.concatenate([m, jnp.zeros((LANES - kl, LANES), F32)], axis=0)
        e_scr[h] = m.T
    e16[...] = jnp.zeros_like(e16)
    for s in range(n):
        h, row = place(me ^ s, half, rb, mirrored)
        for out, group in ((a_refs, first), (b_refs, rest)):
            for slot, j in enumerate(group):
                for p in range(2):
                    y = x32[h, pl.ds(p * kl * rows + row + j, kl, stride=rows), :]
                    out[s][pl.ds((slot * 2 + p) * kl, kl), :] = y.astype(BF16)
        for p in range(2):
            e16[pl.ds(p * 8 + 1, rb), :] = e_scr[h, pl.ds(p * rows + row, rb), :]
        a_refs[s][pl.ds(len(first) * 2 * kl, EDGE), :] = e16[...].astype(BF16)


def split(x, n, rows, kl, rb, first, rest):
    a_shape = jax.ShapeDtypeStruct((len(first) * 2 * kl + EDGE, LANES), BF16)
    b_shape = jax.ShapeDtypeStruct((len(rest) * 2 * kl, LANES), BF16)
    out = pl.pallas_call(
        functools.partial(split_kernel, n, rows, kl, rb, first, rest),
        out_shape=[a_shape] * n + ([b_shape] * n if rest else []),
        scratch_shapes=[
            pltpu.VMEM((2, 2 * kl * rows, LANES), F32),
            pltpu.VMEM((2, LANES, LANES), F32),
            pltpu.VMEM((EDGE, LANES), F32),
        ],
        compiler_params=params(),
        cost_estimate=pl.CostEstimate(flops=10**6, bytes_accessed=4 * 2**20, transcendentals=0),
        name="split",
    )(x)
    return out[:n], out[n:]


def gather(n, refs, held, sem):
    me = lax.axis_index("ka")
    copies = [
        pltpu.make_async_copy(refs[s], held.at[me ^ s], sem.at[s]) for s in range(n)
    ]
    for c in copies:
        c.start()
    for c in copies:
        c.wait()


def samples(held, n, kl, slot):
    return jnp.concatenate(
        [
            held[:, (slot * 2 + p) * kl : (slot * 2 + p + 1) * kl, :].reshape(n * kl, LANES)
            for p in range(2)
        ],
        axis=1,
    )


def rounded(x):
    return (x * (float(K) ** -0.5)).astype(BF16)


def outer_kernel(n, kl, first, *refs):
    pieces, t_ref = refs[:n], refs[n]
    outs = refs[n + 1 : n + 1 + len(first)]
    held, sem = refs[-2:]
    gather(n, pieces, held, sem)
    base = len(first) * 2 * kl
    e = jnp.concatenate([held[j, base : base + EDGE, :kl] for j in range(n)], axis=1)
    e = jnp.concatenate([e, jnp.zeros((LANES - EDGE, K), BF16)], axis=0)
    se = lax.dot_general(t_ref[...], e, (((1,), (1,)), ((), ())), preferred_element_type=F32)
    se = rounded(se).astype(F32)
    packed = se[:LANES]
    for b in range(1, 2 * DEPTH // LANES):
        packed = packed + pltpu.roll(se[b * LANES : (b + 1) * LANES], EDGE * b, 1)
    packed = packed.astype(BF16)
    for slot in range(len(first)):
        s = rounded(jnp.dot(t_ref[...], samples(held, n, kl, slot), preferred_element_type=F32))
        outs[slot][: 2 * DEPTH, :] = s[:, :LANES]
        outs[slot][2 * DEPTH : 4 * DEPTH, :] = s[:, LANES:]
        outs[slot][4 * DEPTH :, :] = packed


def outer(pieces, t, n, kl, first):
    return pl.pallas_call(
        functools.partial(outer_kernel, n, kl, first),
        out_shape=[jax.ShapeDtypeStruct((4 * DEPTH + LANES, LANES), BF16)] * len(first),
        in_specs=[pl.BlockSpec(memory_space=pl.ANY)] * n + [pl.BlockSpec(memory_space=pltpu.VMEM)],
        scratch_shapes=[
            pltpu.VMEM((n, len(first) * 2 * kl + EDGE, LANES), BF16),
            pltpu.SemaphoreType.DMA((n,)),
        ],
        compiler_params=params(),
        cost_estimate=pl.CostEstimate(
            flops=2 * 2 * DEPTH * K * 256 * 3, bytes_accessed=4 * 2**20, transcendentals=0
        ),
        name="outer",
    )(*pieces, t)


def terms(a1, b1, a2, b2):
    re = a1 * a2 + b1 * b2
    im = b1 * a2 - a1 * b2
    pw = (a1 * a1 + b1 * b1 + a2 * a2 + b2 * b2) * 0.5
    return re, im, pw


def inner_kernel(n, kl, rb, rest, *refs):
    nb = n if rest else 0
    pieces = refs[:nb]
    t_ref, top, bottom, above, below = refs[nb : nb + 5]
    outs = refs[nb + 5 : nb + 5 + n]
    held, sem, prod, edge, zpad, dec = refs[-6:]
    half = n // 2
    me = lax.axis_index("ka")
    h = me // half
    dl = DEPTH // n
    if rest:
        gather(n, pieces, held, sem)

    for at, ref in ((0, above), (1, top), (rb, bottom), (rb + 1, below)):
        @pl.loop(0, DEPTH // 64)
        def _(i):
            z = pl.multiple_of(i * 64, 64)
            parts = [
                ref[pl.ds(z + off, 64), :].astype(F32)
                for off in (0, DEPTH, 2 * DEPTH, 3 * DEPTH)
            ]
            for t, v in enumerate(terms(*parts)):
                prod[at, t, pl.ds(z, 64), :] = v
    for slot, r in enumerate(rest):
        s = rounded(
            jnp.dot(t_ref[...], samples(held, n, kl, slot), preferred_element_type=F32)
        ).astype(F32)
        a, b = s[:DEPTH], s[DEPTH:]
        for t, v in enumerate(terms(a[:, :LANES], b[:, :LANES], a[:, LANES:], b[:, LANES:])):
            prod[r + 1, t] = v

    lane = lax.broadcasted_iota(jnp.int32, (LANES, LANES), 1)
    mine = top[4 * DEPTH :, :].astype(F32)
    up = pltpu.roll(above[4 * DEPTH :, :].astype(F32), LANES - rb, 1)
    down = pltpu.roll(below[4 * DEPTH :, :].astype(F32), rb, 1)
    mine = jnp.where(lane % 8 == 0, up, jnp.where(lane % 8 == rb + 1, down, mine))
    blocks = DEPTH // LANES
    for b in range(blocks):
        c = mine if b == 0 else pltpu.roll(mine, LANES - EDGE * b, 1)
        s = pltpu.roll(mine, LANES - EDGE * (b + blocks), 1)
        c2, s2 = pltpu.roll(c, LANES - 8, 1), pltpu.roll(s, LANES - 8, 1)
        for t, v in enumerate(terms(c, s, c2, s2)):
            v = v + pltpu.roll(v, 1, 1) + pltpu.roll(v, LANES - 1, 1)
            edge[t, pl.ds(b * LANES, LANES), :] = v

    zero8 = jnp.zeros((8, LANES), F32)
    for t in range(3):
        zpad[t, pl.ds(0, 8), :] = zero8
        zpad[t, pl.ds(DEPTH + 8, 8), :] = zero8
    lane = lax.broadcasted_iota(jnp.int32, (64, LANES), 1)
    not_first, not_last = lane > 0, lane < LANES - 1
    at_edge = lane == jnp.where(h == 0, LANES - 1, 0)
    for r in range(rb):
        shift = LANES - 2 - r + h

        @pl.loop(0, DEPTH // 64)
        def _(i):
            z = pl.multiple_of(i * 64, 64)
            for t in range(3):
                v = (
                    prod[r, t, pl.ds(z, 64), :]
                    + prod[r + 1, t, pl.ds(z, 64), :]
                    + prod[r + 2, t, pl.ds(z, 64), :]
                )
                left = jnp.where(not_first, pltpu.roll(v, 1, 1), 0.0)
                right = jnp.where(not_last, pltpu.roll(v, LANES - 1, 1), 0.0)
                e = jnp.where(at_edge, pltpu.roll(edge[t, pl.ds(z, 64), :], shift, 1), 0.0)
                zpad[t, pl.ds(z + 8, 64), :] = v + left + right + e

        @pl.loop(0, DEPTH // 64)
        def _(i):
            z = pl.multiple_of(i * 64, 64)
            box = [
                zpad[t, pl.ds(z + 7, 64), :]
                + zpad[t, pl.ds(z + 8, 64), :]
                + zpad[t, pl.ds(z + 9, 64), :]
                for t in range(3)
            ]
            magnitude = jnp.sqrt(box[0] * box[0] + box[1] * box[1])
            dec[r, pl.ds(z, 64), :] = 1.0 - magnitude / (box[2] + 1e-05)

    for s in range(n):
        z = pl.multiple_of((me ^ s) * dl, dl)
        for r in range(rb):
            outs[s][pl.ds(r * dl, dl), :] = dec[r, pl.ds(z, dl), :].astype(BF16)


def inner(pieces, t, halos, n, kl, rb, rest):
    nb = n if rest else 0
    return pl.pallas_call(
        functools.partial(inner_kernel, n, kl, rb, rest),
        out_shape=[jax.ShapeDtypeStruct((rb * (DEPTH // n), LANES), BF16)] * n,
        in_specs=[pl.BlockSpec(memory_space=pl.ANY)] * nb
        + [pl.BlockSpec(memory_space=pltpu.VMEM)] * 5,
        scratch_shapes=[
            pltpu.VMEM((n, max(len(rest) * 2 * kl, 16), LANES), BF16),
            pltpu.SemaphoreType.DMA((n,)),
            pltpu.VMEM((rb + 2, 3, DEPTH, LANES), F32),
            pltpu.VMEM((3, DEPTH, LANES), F32),
            pltpu.VMEM((3, DEPTH + 16, LANES), F32),
            pltpu.VMEM((rb, DEPTH, LANES), F32),
        ],
        compiler_params=params(),
        cost_estimate=pl.CostEstimate(
            flops=2 * 2 * DEPTH * K * 256 * len(rest) + 10**7,
            bytes_accessed=6 * 2**20,
            transcendentals=0,
        ),
        name="inner",
    )(*pieces, t, *halos)


def join_kernel(n, rows, rb, *refs):
    half = n // 2
    pieces, out, held = refs[:n], refs[n], refs[n + 1]
    me = lax.axis_index("ka")
    mirrored = lax.axis_index("row") % 2 == 1
    dl = DEPTH // n
    for s in range(n):
        h, row = place(me ^ s, half, rb, mirrored)
        for r in range(rb):
            d = pieces[s][pl.ds(r * dl, dl), :].astype(F32)
            held[h, pl.ds(row + r, dl, stride=rows), :] = d
    out[:, :LANES] = held[0]
    out[:, LANES:] = held[1]


def join(pieces, n, rows, rb):
    return pl.pallas_call(
        functools.partial(join_kernel, n, rows, rb),
        out_shape=jax.ShapeDtypeStruct((DEPTH // n * rows, 2 * LANES), F32),
        scratch_shapes=[pltpu.VMEM((2, DEPTH // n * rows, LANES), F32)],
        compiler_params=params(),
        cost_estimate=pl.CostEstimate(flops=10**6, bytes_accessed=2 * 2**20, transcendentals=0),
        name="join",
    )(*pieces)


def body(frames):
    n, groups = lax.axis_size("ka"), lax.axis_size("row")
    _, kl, rows, cols = frames.shape
    half = n // 2
    rb = rows // half
    first, rest = (0, rb - 1), tuple(range(1, rb - 1))
    t = jnp.asarray(table())

    order = sorted(range(1, n), key=lambda s: (s & half) == 0)

    def exchange(pieces):
        out = list(pieces)
        for s in order:
            out[s] = lax.ppermute(pieces[s], "ka", [(i, i ^ s) for i in range(n)])
        return out

    a, b = split(frames.reshape(2 * kl * rows, cols), n, rows, kl, rb, first, rest)
    a = exchange(a)
    b = exchange(b) if rest else []
    top, bottom = outer(a, t, n, kl, first)

    def where(h, block):
        g, q = block // half, block % half
        q = q if g % 2 == 0 else half - 1 - q
        return (h * half + q) * groups + g

    steps = [(h, block) for h in range(2) for block in range(groups * half - 1)]
    down = [(where(h, block), where(h, block + 1)) for h, block in steps]
    above = lax.ppermute(bottom, ("ka", "row"), down)
    below = lax.ppermute(top, ("ka", "row"), [(j, i) for i, j in down])
    pieces = inner(b, t, (top, bottom, above, below), n, kl, rb, rest)
    out = join(exchange(pieces), n, rows, rb)
    return out.reshape(DEPTH // n, rows, cols)


def solution(mesh):
    in_specs = (P(None, "ka", "row", None),)
    out_specs = P("ka", "row", None)
    return jax.shard_map(body, mesh=mesh, in_specs=in_specs, out_specs=out_specs, check_vma=False)
```

time: 441 us -> 104 us (0.24)
  the two profiles are of different devices: /device:TPU:1 before, /device:TPU:19 now
where the time goes in v1:
time: 104 us
  waiting for transfers between devices  49.9 us (48%)
  starting transfers between devices  34.1 us (33%)
  Pallas kernels  18.5 us (18%)
  local copies, waits for them, and re-layouts  1.59 us (2%)
    ppermute x21, waiting for transfers between devices, exchange(): out[s] = lax.ppermute(pieces[s], 'ka', [(i, i ^ s) for i in range(n)])  49.9 us
    ppermute x21, starting transfers between devices, exchange(): out[s] = lax.ppermute(pieces[s], 'ka', [(i, i ^ s) for i in range(n)])  29.7 us
    pallas_call x1, Pallas kernels, inner(): pl.pallas_call(functools.partial(inner_kernel, n, kl, rb, rest), out_shap...  9.66 us
    pallas_call x1, Pallas kernels, split(): pl.pallas_call(functools.partial(split_kernel, n, rows, kl, rb, first, re...  4.01 us
    pallas_call x1, Pallas kernels, outer(): pl.pallas_call(functools.partial(outer_kernel, n, kl, first), out_shape=[...  3.22 us
    ppermute x1, starting transfers between devices, body(): above = lax.ppermute(bottom, ('ka', 'row'), down)  2.41 us
  transfers between devices with their start and end apart: 23, of which 14 were waited for; matrix products, arithmetic and copies ran while one was open for 0% of the time, Pallas kernels for 0%

profile of v1, /device:TPU:19, one launch (start us, length us, event | category | flops | bytes accessed | tf_op | source)
XLA Modules:
  0.0 104.1 jit_solution(3421102616546143212)
XLA Ops:
  0.0 0.0 copy-start
  0.0 1.6 %copy-done = bf16[2,128,16,256]{3,2,1,0:T(8,128)(2,1)S(1)} copy-done((bf16[2,128,16,256]{3,2,1,0:T(8,128)(2,1)S(1)}, bf16[2,128,16,256]{3,2,1,0:T(8,128)(2,1)}, u32[]{:S(2)}) %copy-start) | copy-done | bytes 2097176
  1.6 0.0 copy-start.1
  1.6 4.0 %split.1 = (bf16[528,128]{1,0:T(8,128)(2,1)S(1)}, bf16[528,128]{1,0:T(8,128)(2,1)S(1)}, bf16[528,128]{1,0:T(8,128)(2,1)S(1)}, bf16[528,128]{1,0:T(8,128)(2,1)S(1...) custom-call(bf16[4096,256]{1,0:T(8,128)(2,1)S(1)} %bitcast.2), custom_call_target="tpu_custom_call" | custom-call | flops 1000000 | bytes 4194304 | tf_op jit(solution)/shard_map/split/pallas_call | solution.py:73
  5.6 0.7 collective-permute-start.7
  6.3 1.3 %collective-permute-start.8 = (bf16[528,128]{1,0:T(8,128)(2,1)S(1)}, bf16[528,128]{1,0:T(8,128)(2,1)S(1)}, u32[]{:S(2)}, u32[]{:S(2)}) collective-permute-start(bf16[528,128]{1,0:T(8,128)(2,1)S(1)} %get-tuple-element.41), channel_id=1, source_target_pairs={{0,8},{4,12},{8,0},{12,4},{16,24},{20,28},{24,16},{28,20},{1,9},{5... | collective-permute-start | bytes 405512 | tf_op jit(solution)/shard_map/ppermute | solution.py:309
  7.6 0.4 collective-permute-start.9
  8.0 0.1 collective-permute-start.10
  8.1 2.6 %collective-permute-start.11 = (bf16[528,128]{1,0:T(8,128)(2,1)S(1)}, bf16[528,128]{1,0:T(8,128)(2,1)S(1)}, u32[]{:S(2)}, u32[]{:S(2)}) collective-permute-start(bf16[528,128]{1,0:T(8,128)(2,1)S(1)} %get-tuple-element.44), channel_id=1, source_target_pairs={{0,20},{4,16},{8,28},{12,24},{16,4},{20,0},{24,12},{28,8},{1,21},{... | collective-permute-start | bytes 405512 | tf_op jit(solution)/shard_map/ppermute | solution.py:309
  10.7 0.0 collective-permute-done.7.refs_1_
  10.7 0.2 collective-permute-start.12
  10.9 0.6 collective-permute-done.8.refs_2_
  11.5 4.3 %collective-permute-start.13 = (bf16[528,128]{1,0:T(8,128)(2,1)S(1)}, bf16[528,128]{1,0:T(8,128)(2,1)S(1)}, u32[]{:S(2)}, u32[]{:S(2)}) collective-permute-start(bf16[528,128]{1,0:T(8,128)(2,1)S(1)} %get-tuple-element.46), channel_id=1, source_target_pairs={{0,28},{4,24},{8,20},{12,16},{16,12},{20,8},{24,4},{28,0},{1,29},{... | collective-permute-start | bytes 405512 | tf_op jit(solution)/shard_map/ppermute | solution.py:309
  15.8 0.8 collective-permute-done.9.refs_3_
  16.5 0.7 collective-permute-done.10.refs_4_
  17.2 3.6 %collective-permute-done.11.refs_5_ = bf16[528,128]{1,0:T(8,128)(2,1)S(1)} collective-permute-done((bf16[528,128]{1,0:T(8,128)(2,1)S(1)}, bf16[528,128]{1,0:T(8,128)(2,1)S(1)}, u32[]{:S(2)}, u32[]{:S(2)}) %collective-permute-start.11) | collective-permute-done | bytes 135200 | tf_op jit(solution)/shard_map/ppermute | solution.py:309
  20.8 10.7 %collective-permute-done.12.refs_6_ = bf16[528,128]{1,0:T(8,128)(2,1)S(1)} collective-permute-done((bf16[528,128]{1,0:T(8,128)(2,1)S(1)}, bf16[528,128]{1,0:T(8,128)(2,1)S(1)}, u32[]{:S(2)}, u32[]{:S(2)}) %collective-permute-start.12) | collective-permute-done | bytes 135200 | tf_op jit(solution)/shard_map/ppermute | solution.py:309
  31.5 3.2 %collective-permute-done.13.refs_7_ = bf16[528,128]{1,0:T(8,128)(2,1)S(1)} collective-permute-done((bf16[528,128]{1,0:T(8,128)(2,1)S(1)}, bf16[528,128]{1,0:T(8,128)(2,1)S(1)}, u32[]{:S(2)}, u32[]{:S(2)}) %collective-permute-start.13) | collective-permute-done | bytes 135200 | tf_op jit(solution)/shard_map/ppermute | solution.py:309
  34.7 0.0 copy-done.1
  34.7 3.2 %outer.1 = (bf16[2176,128]{1,0:T(8,128)(2,1)S(1)}, bf16[2176,128]{1,0:T(8,128)(2,1)S(1)}) custom-call(bf16[528,128]{1,0:T(8,128)(2,1)S(1)} %get-tuple-element.39.refs_0_, bf16[528,128]{1,0:T(8,128)(2,1)S(1)} %collective-permute-done.7.refs_1_, bf16[528,128]{1,0:T(8,128)(2,1)S(1)} %collective-permute-done.8.refs_2_, ...), custom_call_target="tpu_custom_call" | custom-call | flops 1610612736 | bytes 4194304 | tf_op jit(solution)/shard_map/outer/pallas_call | solution.py:135
  37.9 1.9 %collective-permute-start.15 = (bf16[2176,128]{1,0:T(8,128)(2,1)S(1)}, bf16[2176,128]{1,0:T(8,128)(2,1)S(1)}, u32[]{:S(2)}, u32[]{:S(2)}) collective-permute-start(bf16[2176,128]{1,0:T(8,128)(2,1)S(1)} %get-tuple-element.47.refs_9_), channel_id=1, source_target_pairs={{4,0},{8,4},{12,8},{13,12},{9,13},{5,9},{1,5},{2,1},{6,2},{10,6},{... | collective-permute-start | bytes 1671176 | tf_op jit(solution)/shard_map/ppermute | solution.py:325
  39.8 2.4 %collective-permute-start.14 = (bf16[2176,128]{1,0:T(8,128)(2,1)S(1)}, bf16[2176,128]{1,0:T(8,128)(2,1)S(1)}, u32[]{:S(2)}, u32[]{:S(2)}) collective-permute-start(bf16[2176,128]{1,0:T(8,128)(2,1)S(1)} %get-tuple-element.48.refs_10_), channel_id=1, source_target_pairs={{0,4},{4,8},{8,12},{12,13},{13,9},{9,5},{5,1},{1,2},{2,6},{6,10},{... | collective-permute-start | bytes 1671176 | tf_op jit(solution)/shard_map/ppermute | solution.py:324
  42.3 2.6 %collective-permute-start = (bf16[512,128]{1,0:T(8,128)(2,1)S(1)}, bf16[512,128]{1,0:T(8,128)(2,1)S(1)}, u32[]{:S(2)}, u32[]{:S(2)}) collective-permute-start(bf16[512,128]{1,0:T(8,128)(2,1)S(1)} %get-tuple-element.32), channel_id=1, source_target_pairs={{0,4},{4,0},{8,12},{12,8},{16,20},{20,16},{24,28},{28,24},{1,5},{5... | collective-permute-start | bytes 393224 | tf_op jit(solution)/shard_map/ppermute | solution.py:309
  44.9 0.0 collective-permute-start.1
  44.9 1.7 %collective-permute-start.2 = (bf16[512,128]{1,0:T(8,128)(2,1)S(1)}, bf16[512,128]{1,0:T(8,128)(2,1)S(1)}, u32[]{:S(2)}, u32[]{:S(2)}) collective-permute-start(bf16[512,128]{1,0:T(8,128)(2,1)S(1)} %get-tuple-element.34), channel_id=1, source_target_pairs={{0,12},{4,8},{8,4},{12,0},{16,28},{20,24},{24,20},{28,16},{1,13},{... | collective-permute-start | bytes 393224 | tf_op jit(solution)/shard_map/ppermute | solution.py:309
  46.6 0.0 collective-permute-done.refs_1_
  46.6 0.0 collective-permute-start.3
  46.6 5.9 %collective-permute-done.1.refs_2_ = bf16[512,128]{1,0:T(8,128)(2,1)S(1)} collective-permute-done((bf16[512,128]{1,0:T(8,128)(2,1)S(1)}, bf16[512,128]{1,0:T(8,128)(2,1)S(1)}, u32[]{:S(2)}, u32[]{:S(2)}) %collective-permute-start.1) | collective-permute-done | bytes 131104 | tf_op jit(solution)/shard_map/ppermute | solution.py:309
  52.5 6.7 %collective-permute-start.4 = (bf16[512,128]{1,0:T(8,128)(2,1)S(1)}, bf16[512,128]{1,0:T(8,128)(2,1)S(1)}, u32[]{:S(2)}, u32[]{:S(2)}) collective-permute-start(bf16[512,128]{1,0:T(8,128)(2,1)S(1)} %get-tuple-element.36), channel_id=1, source_target_pairs={{0,20},{4,16},{8,28},{12,24},{16,4},{20,0},{24,12},{28,8},{1,21},{... | collective-permute-start | bytes 393224 | tf_op jit(solution)/shard_map/ppermute | solution.py:309
  59.2 0.0 collective-permute-done.2.refs_3_
  59.2 0.0 collective-permute-start.5
  59.2 0.0 collective-permute-done.3.refs_4_
  59.2 1.7 %collective-permute-start.6 = (bf16[512,128]{1,0:T(8,128)(2,1)S(1)}, bf16[512,128]{1,0:T(8,128)(2,1)S(1)}, u32[]{:S(2)}, u32[]{:S(2)}) collective-permute-start(bf16[512,128]{1,0:T(8,128)(2,1)S(1)} %get-tuple-element.38), channel_id=1, source_target_pairs={{0,28},{4,24},{8,20},{12,16},{16,12},{20,8},{24,4},{28,0},{1,29},{... | collective-permute-start | bytes 393224 | tf_op jit(solution)/shard_map/ppermute | solution.py:309
  61.0 8.8 %collective-permute-done.4.refs_5_ = bf16[512,128]{1,0:T(8,128)(2,1)S(1)} collective-permute-done((bf16[512,128]{1,0:T(8,128)(2,1)S(1)}, bf16[512,128]{1,0:T(8,128)(2,1)S(1)}, u32[]{:S(2)}, u32[]{:S(2)}) %collective-permute-start.4) | collective-permute-done | bytes 131104 | tf_op jit(solution)/shard_map/ppermute | solution.py:309
  69.7 2.8 %collective-permute-done.5.refs_6_ = bf16[512,128]{1,0:T(8,128)(2,1)S(1)} collective-permute-done((bf16[512,128]{1,0:T(8,128)(2,1)S(1)}, bf16[512,128]{1,0:T(8,128)(2,1)S(1)}, u32[]{:S(2)}, u32[]{:S(2)}) %collective-permute-start.5) | collective-permute-done | bytes 131104 | tf_op jit(solution)/shard_map/ppermute | solution.py:309
  72.5 2.8 %collective-permute-done.6.refs_7_ = bf16[512,128]{1,0:T(8,128)(2,1)S(1)} collective-permute-done((bf16[512,128]{1,0:T(8,128)(2,1)S(1)}, bf16[512,128]{1,0:T(8,128)(2,1)S(1)}, u32[]{:S(2)}, u32[]{:S(2)}) %collective-permute-start.6) | collective-permute-done | bytes 131104 | tf_op jit(solution)/shard_map/ppermute | solution.py:309
  75.3 0.0 collective-permute-done.15.refs_12_
  75.4 0.0 collective-permute-done.14.refs_11_
  75.4 9.7 %inner.1 = (bf16[256,128]{1,0:T(8,128)(2,1)S(1)}, bf16[256,128]{1,0:T(8,128)(2,1)S(1)}, bf16[256,128]{1,0:T(8,128)(2,1)S(1)}, bf16[256,128]{1,0:T(8,128)(2,1)S(1...) custom-call(bf16[512,128]{1,0:T(8,128)(2,1)S(1)} %get-tuple-element., ...), custom_call_target="tpu_custom_call" | custom-call | flops 1083741824 | bytes 6291456 | tf_op jit(solution)/shard_map/inner/pallas_call | solution.py:247
  85.0 0.3 collective-permute-start.16
  85.3 0.0 collective-permute-start.17
  85.3 1.9 %collective-permute-start.18 = (bf16[256,128]{1,0:T(8,128)(2,1)S(1)}, bf16[256,128]{1,0:T(8,128)(2,1)S(1)}, u32[]{:S(2)}, u32[]{:S(2)}) collective-permute-start(bf16[256,128]{1,0:T(8,128)(2,1)S(1)} %get-tuple-element.52), channel_id=1, source_target_pairs={{0,12},{4,8},{8,4},{12,0},{16,28},{20,24},{24,20},{28,16},{1,13},{... | collective-permute-start | bytes 196616 | tf_op jit(solution)/shard_map/ppermute | solution.py:309
  87.2 1.6 %collective-permute-start.19 = (bf16[256,128]{1,0:T(8,128)(2,1)S(1)}, bf16[256,128]{1,0:T(8,128)(2,1)S(1)}, u32[]{:S(2)}, u32[]{:S(2)}) collective-permute-start(bf16[256,128]{1,0:T(8,128)(2,1)S(1)} %get-tuple-element.53), channel_id=1, source_target_pairs={{0,16},{4,20},{8,24},{12,28},{16,0},{20,4},{24,8},{28,12},{1,17},{... | collective-permute-start | bytes 196616 | tf_op jit(solution)/shard_map/ppermute | solution.py:309
  88.8 0.8 collective-permute-start.20
  89.7 0.0 collective-permute-done.16.refs_1_
  89.7 2.3 %collective-permute-start.21 = (bf16[256,128]{1,0:T(8,128)(2,1)S(1)}, bf16[256,128]{1,0:T(8,128)(2,1)S(1)}, u32[]{:S(2)}, u32[]{:S(2)}) collective-permute-start(bf16[256,128]{1,0:T(8,128)(2,1)S(1)} %get-tuple-element.55), channel_id=1, source_target_pairs={{0,24},{4,28},{8,16},{12,20},{16,8},{20,12},{24,0},{28,4},{1,25},{... | collective-permute-start | bytes 196616 | tf_op jit(solution)/shard_map/ppermute | solution.py:309
  92.0 0.0 collective-permute-done.17.refs_2_
  92.0 0.4 collective-permute-start.22
  92.5 0.0 collective-permute-done.18.refs_3_
  92.5 1.3 %collective-permute-done.19.refs_4_ = bf16[256,128]{1,0:T(8,128)(2,1)S(1)} collective-permute-done((bf16[256,128]{1,0:T(8,128)(2,1)S(1)}, bf16[256,128]{1,0:T(8,128)(2,1)S(1)}, u32[]{:S(2)}, u32[]{:S(2)}) %collective-permute-start.19) | collective-permute-done | bytes 65568 | tf_op jit(solution)/shard_map/ppermute | solution.py:309
  93.8 3.4 %collective-permute-done.20.refs_5_ = bf16[256,128]{1,0:T(8,128)(2,1)S(1)} collective-permute-done((bf16[256,128]{1,0:T(8,128)(2,1)S(1)}, bf16[256,128]{1,0:T(8,128)(2,1)S(1)}, u32[]{:S(2)}, u32[]{:S(2)}) %collective-permute-start.20) | collective-permute-done | bytes 65568 | tf_op jit(solution)/shard_map/ppermute | solution.py:309
  97.2 3.9 %collective-permute-done.21.refs_6_ = bf16[256,128]{1,0:T(8,128)(2,1)S(1)} collective-permute-done((bf16[256,128]{1,0:T(8,128)(2,1)S(1)}, bf16[256,128]{1,0:T(8,128)(2,1)S(1)}, u32[]{:S(2)}, u32[]{:S(2)}) %collective-permute-start.21) | collective-permute-done | bytes 65568 | tf_op jit(solution)/shard_map/ppermute | solution.py:309
  101.1 1.4 %collective-permute-done.22.refs_7_ = bf16[256,128]{1,0:T(8,128)(2,1)S(1)} collective-permute-done((bf16[256,128]{1,0:T(8,128)(2,1)S(1)}, bf16[256,128]{1,0:T(8,128)(2,1)S(1)}, u32[]{:S(2)}, u32[]{:S(2)}) %collective-permute-start.22) | collective-permute-done | bytes 65568 | tf_op jit(solution)/shard_map/ppermute | solution.py:309
  102.5 1.6 %join.1 = f32[1024,256]{1,0:T(8,128)} custom-call(bf16[256,128]{1,0:T(8,128)(2,1)S(1)} %get-tuple-element.49.refs_0_, bf16[256,128]{1,0:T(8,128)(2,1)S(1)} %collective-permute-done.16.refs_1_, bf16[256,128]{1,0:T(8,128)(2,1)S(1)} %collective-permute-done.17.refs_2_, bf16[256,128]{1,0:T(8,128)(2,1)S(1)} %collective-permute-done.18.refs_3_, ...), custom_call_target="tpu_custom_call" | custom-call | flops 1000000 | bytes 2097152 | tf_op jit(solution)/shard_map/join/pallas_call | solution.py:286
Async XLA Ops:
  0.0 1.6 %copy-start = (bf16[2,128,16,256]{3,2,1,0:T(8,128)(2,1)S(1)}, bf16[2,128,16,256]{3,2,1,0:T(8,128)(2,1)}, u32[]{:S(2)}) copy-start(bf16[2,128,16,256]{3,2,1,0:T(8,128)(2,1)} %param.2) | copy-start | bytes 6291460
  1.6 33.1 %copy-start.1 = (bf16[1024,1024]{1,0:T(8,128)(2,1)S(1)}, bf16[1024,1024]{1,0:T(8,128)(2,1)}, u32[]{:S(2)}) copy-start(bf16[1024,1024]{1,0:T(8,128)(2,1)} %constant.2.clone.refs_8_) | copy-start | bytes 6291460
  5.6 5.1 %collective-permute-start.7 = (bf16[528,128]{1,0:T(8,128)(2,1)S(1)}, bf16[528,128]{1,0:T(8,128)(2,1)S(1)}, u32[]{:S(2)}, u32[]{:S(2)}) collective-permute-start(bf16[528,128]{1,0:T(8,128)(2,1)S(1)} %get-tuple-element.40), channel_id=1, source_target_pairs={{0,4},{4,0},{8,12},{12,8},{16,20},{20,16},{24,28},{28,24},{1,5},{5... | collective-permute-start | bytes 405512 | tf_op jit(solution)/shard_map/ppermute | solution.py:309
  6.3 5.2 %collective-permute-start.8 = (bf16[528,128]{1,0:T(8,128)(2,1)S(1)}, bf16[528,128]{1,0:T(8,128)(2,1)S(1)}, u32[]{:S(2)}, u32[]{:S(2)}) collective-permute-start(bf16[528,128]{1,0:T(8,128)(2,1)S(1)} %get-tuple-element.41), channel_id=1, source_target_pairs={{0,8},{4,12},{8,0},{12,4},{16,24},{20,28},{24,16},{28,20},{1,9},{5... | collective-permute-start | bytes 405512 | tf_op jit(solution)/shard_map/ppermute | solution.py:309
  7.6 8.9 %collective-permute-start.9 = (bf16[528,128]{1,0:T(8,128)(2,1)S(1)}, bf16[528,128]{1,0:T(8,128)(2,1)S(1)}, u32[]{:S(2)}, u32[]{:S(2)}) collective-permute-start(bf16[528,128]{1,0:T(8,128)(2,1)S(1)} %get-tuple-element.42), channel_id=1, source_target_pairs={{0,12},{4,8},{8,4},{12,0},{16,28},{20,24},{24,20},{28,16},{1,13},{... | collective-permute-start | bytes 405512 | tf_op jit(solution)/shard_map/ppermute | solution.py:309
  8.0 9.2 %collective-permute-start.10 = (bf16[528,128]{1,0:T(8,128)(2,1)S(1)}, bf16[528,128]{1,0:T(8,128)(2,1)S(1)}, u32[]{:S(2)}, u32[]{:S(2)}) collective-permute-start(bf16[528,128]{1,0:T(8,128)(2,1)S(1)} %get-tuple-element.43), channel_id=1, source_target_pairs={{0,16},{4,20},{8,24},{12,28},{16,0},{20,4},{24,8},{28,12},{1,17},{... | collective-permute-start | bytes 405512 | tf_op jit(solution)/shard_map/ppermute | solution.py:309
  8.1 12.7 %collective-permute-start.11 = (bf16[528,128]{1,0:T(8,128)(2,1)S(1)}, bf16[528,128]{1,0:T(8,128)(2,1)S(1)}, u32[]{:S(2)}, u32[]{:S(2)}) collective-permute-start(bf16[528,128]{1,0:T(8,128)(2,1)S(1)} %get-tuple-element.44), channel_id=1, source_target_pairs={{0,20},{4,16},{8,28},{12,24},{16,4},{20,0},{24,12},{28,8},{1,21},{... | collective-permute-start | bytes 405512 | tf_op jit(solution)/shard_map/ppermute | solution.py:309
  10.7 20.8 %collective-permute-start.12 = (bf16[528,128]{1,0:T(8,128)(2,1)S(1)}, bf16[528,128]{1,0:T(8,128)(2,1)S(1)}, u32[]{:S(2)}, u32[]{:S(2)}) collective-permute-start(bf16[528,128]{1,0:T(8,128)(2,1)S(1)} %get-tuple-element.45), channel_id=1, source_target_pairs={{0,24},{4,28},{8,16},{12,20},{16,8},{20,12},{24,0},{28,4},{1,25},{... | collective-permute-start | bytes 405512 | tf_op jit(solution)/shard_map/ppermute | solution.py:309
  11.5 23.2 %collective-permute-start.13 = (bf16[528,128]{1,0:T(8,128)(2,1)S(1)}, bf16[528,128]{1,0:T(8,128)(2,1)S(1)}, u32[]{:S(2)}, u32[]{:S(2)}) collective-permute-start(bf16[528,128]{1,0:T(8,128)(2,1)S(1)} %get-tuple-element.46), channel_id=1, source_target_pairs={{0,28},{4,24},{8,20},{12,16},{16,12},{20,8},{24,4},{28,0},{1,29},{... | collective-permute-start | bytes 405512 | tf_op jit(solution)/shard_map/ppermute | solution.py:309
  37.9 37.4 %collective-permute-start.15 = (bf16[2176,128]{1,0:T(8,128)(2,1)S(1)}, bf16[2176,128]{1,0:T(8,128)(2,1)S(1)}, u32[]{:S(2)}, u32[]{:S(2)}) collective-permute-start(bf16[2176,128]{1,0:T(8,128)(2,1)S(1)} %get-tuple-element.47.refs_9_), channel_id=1, source_target_pairs={{4,0},{8,4},{12,8},{13,12},{9,13},{5,9},{1,5},{2,1},{6,2},{10,6},{... | collective-permute-start | bytes 1671176 | tf_op jit(solution)/shard_map/ppermute | solution.py:325
  39.8 35.5 %collective-permute-start.14 = (bf16[2176,128]{1,0:T(8,128)(2,1)S(1)}, bf16[2176,128]{1,0:T(8,128)(2,1)S(1)}, u32[]{:S(2)}, u32[]{:S(2)}) collective-permute-start(bf16[2176,128]{1,0:T(8,128)(2,1)S(1)} %get-tuple-element.48.refs_10_), channel_id=1, source_target_pairs={{0,4},{4,8},{8,12},{12,13},{13,9},{9,5},{5,1},{1,2},{2,6},{6,10},{... | collective-permute-start | bytes 1671176 | tf_op jit(solution)/shard_map/ppermute | solution.py:324
  42.3 4.3 %collective-permute-start = (bf16[512,128]{1,0:T(8,128)(2,1)S(1)}, bf16[512,128]{1,0:T(8,128)(2,1)S(1)}, u32[]{:S(2)}, u32[]{:S(2)}) collective-permute-start(bf16[512,128]{1,0:T(8,128)(2,1)S(1)} %get-tuple-element.32), channel_id=1, source_target_pairs={{0,4},{4,0},{8,12},{12,8},{16,20},{20,16},{24,28},{28,24},{1,5},{5... | collective-permute-start | bytes 393224 | tf_op jit(solution)/shard_map/ppermute | solution.py:309
  44.9 7.7 %collective-permute-start.1 = (bf16[512,128]{1,0:T(8,128)(2,1)S(1)}, bf16[512,128]{1,0:T(8,128)(2,1)S(1)}, u32[]{:S(2)}, u32[]{:S(2)}) collective-permute-start(bf16[512,128]{1,0:T(8,128)(2,1)S(1)} %get-tuple-element.33), channel_id=1, source_target_pairs={{0,8},{4,12},{8,0},{12,4},{16,24},{20,28},{24,16},{28,20},{1,9},{5... | collective-permute-start | bytes 393224 | tf_op jit(solution)/shard_map/ppermute | solution.py:309
  44.9 14.4 %collective-permute-start.2 = (bf16[512,128]{1,0:T(8,128)(2,1)S(1)}, bf16[512,128]{1,0:T(8,128)(2,1)S(1)}, u32[]{:S(2)}, u32[]{:S(2)}) collective-permute-start(bf16[512,128]{1,0:T(8,128)(2,1)S(1)} %get-tuple-element.34), channel_id=1, source_target_pairs={{0,12},{4,8},{8,4},{12,0},{16,28},{20,24},{24,20},{28,16},{1,13},{... | collective-permute-start | bytes 393224 | tf_op jit(solution)/shard_map/ppermute | solution.py:309
  46.6 12.6 %collective-permute-start.3 = (bf16[512,128]{1,0:T(8,128)(2,1)S(1)}, bf16[512,128]{1,0:T(8,128)(2,1)S(1)}, u32[]{:S(2)}, u32[]{:S(2)}) collective-permute-start(bf16[512,128]{1,0:T(8,128)(2,1)S(1)} %get-tuple-element.35), channel_id=1, source_target_pairs={{0,16},{4,20},{8,24},{12,28},{16,0},{20,4},{24,8},{28,12},{1,17},{... | collective-permute-start | bytes 393224 | tf_op jit(solution)/shard_map/ppermute | solution.py:309
  52.5 17.2 %collective-permute-start.4 = (bf16[512,128]{1,0:T(8,128)(2,1)S(1)}, bf16[512,128]{1,0:T(8,128)(2,1)S(1)}, u32[]{:S(2)}, u32[]{:S(2)}) collective-permute-start(bf16[512,128]{1,0:T(8,128)(2,1)S(1)} %get-tuple-element.36), channel_id=1, source_target_pairs={{0,20},{4,16},{8,28},{12,24},{16,4},{20,0},{24,12},{28,8},{1,21},{... | collective-permute-start | bytes 393224 | tf_op jit(solution)/shard_map/ppermute | solution.py:309
  59.2 13.3 %collective-permute-start.5 = (bf16[512,128]{1,0:T(8,128)(2,1)S(1)}, bf16[512,128]{1,0:T(8,128)(2,1)S(1)}, u32[]{:S(2)}, u32[]{:S(2)}) collective-permute-start(bf16[512,128]{1,0:T(8,128)(2,1)S(1)} %get-tuple-element.37), channel_id=1, source_target_pairs={{0,24},{4,28},{8,16},{12,20},{16,8},{20,12},{24,0},{28,4},{1,25},{... | collective-permute-start | bytes 393224 | tf_op jit(solution)/shard_map/ppermute | solution.py:309
  59.2 16.1 %collective-permute-start.6 = (bf16[512,128]{1,0:T(8,128)(2,1)S(1)}, bf16[512,128]{1,0:T(8,128)(2,1)S(1)}, u32[]{:S(2)}, u32[]{:S(2)}) collective-permute-start(bf16[512,128]{1,0:T(8,128)(2,1)S(1)} %get-tuple-element.38), channel_id=1, source_target_pairs={{0,28},{4,24},{8,20},{12,16},{16,12},{20,8},{24,4},{28,0},{1,29},{... | collective-permute-start | bytes 393224 | tf_op jit(solution)/shard_map/ppermute | solution.py:309
  85.0 4.7 %collective-permute-start.16 = (bf16[256,128]{1,0:T(8,128)(2,1)S(1)}, bf16[256,128]{1,0:T(8,128)(2,1)S(1)}, u32[]{:S(2)}, u32[]{:S(2)}) collective-permute-start(bf16[256,128]{1,0:T(8,128)(2,1)S(1)} %get-tuple-element.50), channel_id=1, source_target_pairs={{0,4},{4,0},{8,12},{12,8},{16,20},{20,16},{24,28},{28,24},{1,5},{5... | collective-permute-start | bytes 196616 | tf_op jit(solution)/shard_map/ppermute | solution.py:309
  85.3 6.7 %collective-permute-start.17 = (bf16[256,128]{1,0:T(8,128)(2,1)S(1)}, bf16[256,128]{1,0:T(8,128)(2,1)S(1)}, u32[]{:S(2)}, u32[]{:S(2)}) collective-permute-start(bf16[256,128]{1,0:T(8,128)(2,1)S(1)} %get-tuple-element.51), channel_id=1, source_target_pairs={{0,8},{4,12},{8,0},{12,4},{16,24},{20,28},{24,16},{28,20},{1,9},{5... | collective-permute-start | bytes 196616 | tf_op jit(solution)/shard_map/ppermute | solution.py:309
  85.3 7.2 %collective-permute-start.18 = (bf16[256,128]{1,0:T(8,128)(2,1)S(1)}, bf16[256,128]{1,0:T(8,128)(2,1)S(1)}, u32[]{:S(2)}, u32[]{:S(2)}) collective-permute-start(bf16[256,128]{1,0:T(8,128)(2,1)S(1)} %get-tuple-element.52), channel_id=1, source_target_pairs={{0,12},{4,8},{8,4},{12,0},{16,28},{20,24},{24,20},{28,16},{1,13},{... | collective-permute-start | bytes 196616 | tf_op jit(solution)/shard_map/ppermute | solution.py:309
  87.2 6.6 %collective-permute-start.19 = (bf16[256,128]{1,0:T(8,128)(2,1)S(1)}, bf16[256,128]{1,0:T(8,128)(2,1)S(1)}, u32[]{:S(2)}, u32[]{:S(2)}) collective-permute-start(bf16[256,128]{1,0:T(8,128)(2,1)S(1)} %get-tuple-element.53), channel_id=1, source_target_pairs={{0,16},{4,20},{8,24},{12,28},{16,0},{20,4},{24,8},{28,12},{1,17},{... | collective-permute-start | bytes 196616 | tf_op jit(solution)/shard_map/ppermute | solution.py:309
  88.8 8.4 %collective-permute-start.20 = (bf16[256,128]{1,0:T(8,128)(2,1)S(1)}, bf16[256,128]{1,0:T(8,128)(2,1)S(1)}, u32[]{:S(2)}, u32[]{:S(2)}) collective-permute-start(bf16[256,128]{1,0:T(8,128)(2,1)S(1)} %get-tuple-element.54), channel_id=1, source_target_pairs={{0,20},{4,16},{8,28},{12,24},{16,4},{20,0},{24,12},{28,8},{1,21},{... | collective-permute-start | bytes 196616 | tf_op jit(solution)/shard_map/ppermute | solution.py:309
  89.7 11.4 %collective-permute-start.21 = (bf16[256,128]{1,0:T(8,128)(2,1)S(1)}, bf16[256,128]{1,0:T(8,128)(2,1)S(1)}, u32[]{:S(2)}, u32[]{:S(2)}) collective-permute-start(bf16[256,128]{1,0:T(8,128)(2,1)S(1)} %get-tuple-element.55), channel_id=1, source_target_pairs={{0,24},{4,28},{8,16},{12,20},{16,8},{20,12},{24,0},{28,4},{1,25},{... | collective-permute-start | bytes 196616 | tf_op jit(solution)/shard_map/ppermute | solution.py:309
  92.0 10.5 %collective-permute-start.22 = (bf16[256,128]{1,0:T(8,128)(2,1)S(1)}, bf16[256,128]{1,0:T(8,128)(2,1)S(1)}, u32[]{:S(2)}, u32[]{:S(2)}) collective-permute-start(bf16[256,128]{1,0:T(8,128)(2,1)S(1)} %get-tuple-element.56), channel_id=1, source_target_pairs={{0,28},{4,24},{8,20},{12,16},{16,12},{20,8},{24,4},{28,0},{1,29},{... | collective-permute-start | bytes 196616 | tf_op jit(solution)/shard_map/ppermute | solution.py:309

commit v2 on v1

v2 whole, which is shorter than its diff:
```python
import functools
import math

import jax
import jax.numpy as jnp
import numpy as np
from jax import lax
from jax.experimental import pallas as pl
from jax.experimental.pallas import tpu as pltpu
from jax.sharding import PartitionSpec as P

K = 1024
DEPTH = 512
LANES = 128
EDGE = 16
F32 = jnp.float32
BF16 = jnp.bfloat16


def table():
    phase = (np.arange(K)[None, :] * np.arange(DEPTH)[:, None]) % K
    angle = phase.astype(np.float32) * np.float32(2.0 * math.pi / K)
    both = np.concatenate([np.cos(angle), np.sin(angle)], axis=0)
    return both.astype(jnp.bfloat16)


def place(dest, half, rb, mirrored):
    h = dest // half
    q = dest % half
    q = jnp.where(mirrored, half - 1 - q, q)
    return h, q * rb


def params(mib=48):
    return pltpu.CompilerParams(vmem_limit_bytes=mib * 1024 * 1024)


def split_kernel(n, rows, kl, rb, first, rest, x_ref, *refs):
    half = n // 2
    a_refs, b_refs, x32 = refs[:n], refs[n:-1], refs[-1]
    me = lax.axis_index("ka")
    mirrored = lax.axis_index("row") % 2 == 1
    x32[0] = x_ref[:, :LANES].astype(F32)
    x32[1] = x_ref[:, LANES:].astype(F32)
    lane = lax.broadcasted_iota(jnp.int32, (kl, LANES), 1)
    edges = [jnp.zeros((kl, LANES), F32) for _ in range(n * EDGE // LANES)]
    for s in range(n):
        h, row = place(me ^ s, half, rb, mirrored)
        for refs_of, group in ((a_refs, first), (b_refs, rest)):
            for slot, j in enumerate(group):
                for p in range(2):
                    y = x32[h, pl.ds(p * kl * rows + row + j, kl, stride=rows), :]
                    refs_of[s][pl.ds((slot * 2 + p) * kl, kl), :] = y.astype(BF16)
                    at, m = divmod(s * EDGE + p * 8 + 1 + j, LANES)[::-1]
                    y = pltpu.roll(y, (at + 1 - h) % LANES, 1)
                    edges[m] = jnp.where(lane == at, y, edges[m])
    for m, e in enumerate(edges):
        if kl < LANES:
            e = jnp.concatenate([e, jnp.zeros((LANES - kl, LANES), F32)], axis=0)
        e = e.T.astype(BF16)
        for i in range(LANES // EDGE):
            s = (m * LANES // EDGE + i) ^ half
            a_refs[s][pl.ds(len(first) * 2 * kl, EDGE), :] = e[i * EDGE : (i + 1) * EDGE]


def split(x, n, rows, kl, rb, first, rest):
    a_shape = jax.ShapeDtypeStruct((len(first) * 2 * kl + EDGE, LANES), BF16)
    b_shape = jax.ShapeDtypeStruct((len(rest) * 2 * kl, LANES), BF16)
    out = pl.pallas_call(
        functools.partial(split_kernel, n, rows, kl, rb, first, rest),
        out_shape=[a_shape] * n + ([b_shape] * n if rest else []),
        scratch_shapes=[pltpu.VMEM((2, 2 * kl * rows, LANES), F32)],
        compiler_params=params(),
        cost_estimate=pl.CostEstimate(flops=10**6, bytes_accessed=4 * 2**20, transcendentals=0),
        name="split",
    )(x)
    return out[:n], out[n:]


def transform(t_ref, pieces, kl, slot):
    n = len(pieces)
    me = lax.axis_index("ka")
    t = jnp.concatenate([t_ref[me ^ s] for s in range(n)], axis=1)
    x = jnp.concatenate(
        [
            jnp.concatenate([p[pl.ds((slot * 2 + q) * kl, kl), :] for p in pieces], axis=0)
            for q in range(2)
        ],
        axis=1,
    )
    return rounded(jnp.dot(t, x, preferred_element_type=F32))


def rounded(x):
    return (x * (float(K) ** -0.5)).astype(BF16)


def terms(a1, b1, a2, b2):
    re = a1 * a2 + b1 * b2
    im = b1 * a2 - a1 * b2
    pw = (a1 * a1 + b1 * b1 + a2 * a2 + b2 * b2) * 0.5
    return re, im, pw


def outer_kernel(n, kl, first, *refs):
    pieces, t_ref, outs = refs[:n], refs[n], refs[n + 1 :]
    for slot in range(len(first)):
        s = transform(t_ref, pieces, kl, slot)
        outs[slot][: 2 * DEPTH, :] = s[:, :LANES]
        outs[slot][2 * DEPTH : 4 * DEPTH, :] = s[:, LANES:]
    me = lax.axis_index("ka")
    t = jnp.concatenate([t_ref[me ^ s] for s in range(n)], axis=1)
    e = jnp.concatenate([p[len(first) * 2 * kl :, :kl] for p in pieces], axis=1)
    e = jnp.concatenate([e, jnp.zeros((LANES - EDGE, K), BF16)], axis=0)
    se = lax.dot_general(t, e, (((1,), (1,)), ((), ())), preferred_element_type=F32)
    se = rounded(se).astype(F32)
    packed = se[:LANES]
    for b in range(1, 2 * DEPTH // LANES):
        packed = packed + pltpu.roll(se[b * LANES : (b + 1) * LANES], EDGE * b, 1)
    packed = packed.astype(BF16)
    for slot in range(len(first)):
        outs[slot][4 * DEPTH :, :] = packed


def outer(pieces, t, n, kl, first):
    return pl.pallas_call(
        functools.partial(outer_kernel, n, kl, first),
        out_shape=[jax.ShapeDtypeStruct((4 * DEPTH + LANES, LANES), BF16)] * len(first),
        compiler_params=params(),
        cost_estimate=pl.CostEstimate(
            flops=2 * 2 * DEPTH * K * 256 * 3, bytes_accessed=4 * 2**20, transcendentals=0
        ),
        name="outer",
    )(*pieces, t)


def inner_kernel(n, kl, rest, *refs):
    pieces, t_ref, out = refs[:n], refs[n], refs[n + 1]
    for slot in range(len(rest)):
        s = transform(t_ref, pieces, kl, slot)
        out[slot, : 2 * DEPTH, :] = s[:, :LANES]
        out[slot, 2 * DEPTH :, :] = s[:, LANES:]


def inner(pieces, t, n, kl, rest):
    return pl.pallas_call(
        functools.partial(inner_kernel, n, kl, rest),
        out_shape=jax.ShapeDtypeStruct((len(rest), 4 * DEPTH, LANES), BF16),
        compiler_params=params(),
        cost_estimate=pl.CostEstimate(flops=3 * 10**10, bytes_accessed=6 * 2**20, transcendentals=0),
        name="inner",
    )(*pieces, t)


STEP = 16


def box_kernel(n, rb, *refs):
    above, top = refs[0], refs[1]
    inside = refs[2] if rb > 2 else None
    bottom, below = refs[2 + (rb > 2)], refs[3 + (rb > 2)]
    outs = refs[4 + (rb > 2) :][:n]
    edge, total, dec = refs[-3:]
    me = lax.axis_index("ka")
    h = me // (n // 2)
    dl = DEPTH // n

    def spectrum(r, z):
        ref = {-1: above, 0: top, rb - 1: bottom, rb: below}.get(r)
        where = [pl.ds(z + j * DEPTH, STEP) for j in range(4)]
        rows = [ref[w, :] for w in where] if ref is not None else [inside[r - 1, w, :] for w in where]
        return [x.astype(F32) for x in rows]

    lane = lax.broadcasted_iota(jnp.int32, (LANES, LANES), 1)
    packed = top[4 * DEPTH :, :].astype(F32)
    up = pltpu.roll(above[4 * DEPTH :, :].astype(F32), LANES - rb, 1)
    down = pltpu.roll(below[4 * DEPTH :, :].astype(F32), rb, 1)
    packed = jnp.where(lane % 8 == 0, up, jnp.where(lane % 8 == rb + 1, down, packed))
    blocks = DEPTH // LANES
    for b in range(blocks):
        c = packed if b == 0 else pltpu.roll(packed, LANES - EDGE * b, 1)
        s = pltpu.roll(packed, LANES - EDGE * (b + blocks), 1)
        c2, s2 = pltpu.roll(c, LANES - 8, 1), pltpu.roll(s, LANES - 8, 1)
        for t, v in enumerate(terms(c, s, c2, s2)):
            v = v + pltpu.roll(v, 1, 1) + pltpu.roll(v, LANES - 1, 1)
            edge[t, pl.ds(b * LANES + 8, LANES), :] = v
    for t in range(3):
        for z in (0, DEPTH + 8):
            edge[t, pl.ds(z, 8), :] = jnp.zeros((8, LANES), F32)
            for r in range(rb):
                total[r, t, pl.ds(z, 8), :] = jnp.zeros((8, LANES), F32)

    @pl.loop(0, DEPTH // STEP, unroll=2)
    def _(i):
        z = pl.multiple_of(i * STEP, STEP)
        before = terms(*spectrum(-1, z))
        here = terms(*spectrum(0, z))
        pair = [x + y for x, y in zip(before, here)]
        for r in range(rb):
            after = terms(*spectrum(r + 1, z))
            for t in range(3):
                total[r, t, pl.ds(z + 8, STEP), :] = pair[t] + after[t]
            pair = [x + y for x, y in zip(here, after)]
            here = after

    lane = lax.broadcasted_iota(jnp.int32, (STEP, LANES), 1)
    not_first, not_last = lane > 0, lane < LANES - 1
    at_edge = lane == jnp.where(h == 0, LANES - 1, 0)

    def deep(x):
        return x[0] + x[1] + x[2]

    @pl.loop(0, DEPTH // STEP)
    def _(i):
        z = pl.multiple_of(i * STEP, STEP)
        rim = [deep([edge[t, pl.ds(z + j, STEP), :] for j in (7, 8, 9)]) for t in range(3)]
        for r in range(rb):
            box = []
            for t in range(3):
                v = deep([total[r, t, pl.ds(z + j, STEP), :] for j in (7, 8, 9)])
                left = jnp.where(not_first, pltpu.roll(v, 1, 1), 0.0)
                right = jnp.where(not_last, pltpu.roll(v, LANES - 1, 1), 0.0)
                e = jnp.where(at_edge, pltpu.roll(rim[t], LANES - 2 - r + h, 1), 0.0)
                box.append(v + left + right + e)
            square = box[0] * box[0] + box[1] * box[1]
            d = 1.0 - jnp.sqrt(square) / (box[2] + 1e-05)
            dec[r, pl.ds(z, STEP), :] = (d * jnp.abs(d) * (d * d)).astype(BF16)

    for s in range(n):
        z = pl.multiple_of((me ^ s) * dl, dl)
        for r in range(rb):
            outs[s][pl.ds(r * dl, dl), :] = dec[r, pl.ds(z, dl), :]


def boxed(rows, n, rb):
    return pl.pallas_call(
        functools.partial(box_kernel, n, rb),
        out_shape=[jax.ShapeDtypeStruct((rb * (DEPTH // n), LANES), BF16)] * n,
        scratch_shapes=[
            pltpu.VMEM((3, DEPTH + 16, LANES), F32),
            pltpu.VMEM((rb, 3, DEPTH + 16, LANES), F32),
            pltpu.VMEM((rb, DEPTH, LANES), BF16),
        ],
        compiler_params=params(),
        cost_estimate=pl.CostEstimate(flops=10**7, bytes_accessed=6 * 2**20, transcendentals=0),
        name="boxed",
    )(*rows)


def join_kernel(n, rows, rb, *refs):
    half = n // 2
    pieces, out, held = refs[:n], refs[n], refs[n + 1]
    me = lax.axis_index("ka")
    mirrored = lax.axis_index("row") % 2 == 1
    dl = DEPTH // n
    for s in range(n):
        h, row = place(me ^ s, half, rb, mirrored)
        for r in range(rb):
            coded = pieces[s][pl.ds(r * dl, dl), :].astype(F32)
            d = jnp.sqrt(jnp.sqrt(jnp.abs(coded)))
            d = jnp.where(coded < 0.0, -d, d)
            held[h, pl.ds(row + r, dl, stride=rows), :] = d
    out[:, :LANES] = held[0]
    out[:, LANES:] = held[1]


def join(pieces, n, rows, rb):
    return pl.pallas_call(
        functools.partial(join_kernel, n, rows, rb),
        out_shape=jax.ShapeDtypeStruct((DEPTH // n * rows, 2 * LANES), F32),
        scratch_shapes=[pltpu.VMEM((2, DEPTH // n * rows, LANES), F32)],
        compiler_params=params(),
        cost_estimate=pl.CostEstimate(flops=10**6, bytes_accessed=2 * 2**20, transcendentals=0),
        name="join",
    )(*pieces)


def body(frames):
    n, groups = lax.axis_size("ka"), lax.axis_size("row")
    _, kl, rows, cols = frames.shape
    half = n // 2
    rb = rows // half
    first, rest = (0, rb - 1), tuple(range(1, rb - 1))
    t = jnp.asarray(table().reshape(2 * DEPTH, n, kl).transpose(1, 0, 2))

    order = sorted(range(1, n), key=lambda s: (s & half) == 0)

    def exchange(pieces):
        out = list(pieces)
        for s in order:
            out[s] = lax.ppermute(pieces[s], "ka", [(i, i ^ s) for i in range(n)])
        return out

    a, b = split(frames.reshape(2 * kl * rows, cols), n, rows, kl, rb, first, rest)
    a = exchange(a)
    b = exchange(b) if rest else []
    top, bottom = outer(a, t, n, kl, first)

    def where(h, block):
        g, q = block // half, block % half
        q = q if g % 2 == 0 else half - 1 - q
        return (h * half + q) * groups + g

    steps = [(h, block) for h in range(2) for block in range(groups * half - 1)]
    down = [(where(h, block), where(h, block + 1)) for h, block in steps]
    above = lax.ppermute(bottom, ("ka", "row"), down)
    below = lax.ppermute(top, ("ka", "row"), [(j, i) for i, j in down])
    inside = [inner(b, t, n, kl, rest)] if rest else []
    pieces = boxed([above, top, *inside, bottom, below], n, rb)
    out = join(exchange(pieces), n, rows, rb)
    return out.reshape(DEPTH // n, rows, cols)


def solution(mesh):
    in_specs = (P(None, "ka", "row", None),)
    out_specs = P("ka", "row", None)
    return jax.shard_map(body, mesh=mesh, in_specs=in_specs, out_specs=out_specs, check_vma=False)
```

time: 104 us -> 92.7 us (0.89)
  the two profiles are of different devices: /device:TPU:19 before, /device:TPU:11 now
where the time goes in v2:
time: 92.7 us; the launch traced here: 92.6 us
  waiting for transfers between devices  41.4 us (45%)
  starting transfers between devices  34.5 us (37%)
  Pallas kernels  15 us (16%)
  local copies, waits for them, and re-layouts  1.59 us (2%)
    ppermute x21, waiting for transfers between devices, exchange(): out[s] = lax.ppermute(pieces[s], 'ka', [(i, i ^ s) for i in range(n)])  39.6 us
    ppermute x21, starting transfers between devices, exchange(): out[s] = lax.ppermute(pieces[s], 'ka', [(i, i ^ s) for i in range(n)])  29.2 us
    pallas_call x1, Pallas kernels, boxed(): pl.pallas_call(functools.partial(box_kernel, n, rb), out_shape=[jax.Shape...  7.43 us
    ppermute x1, starting transfers between devices, body(): below = lax.ppermute(top, ('ka', 'row'), [(j, i) for i, j in down])  3.36 us
    pallas_call x1, Pallas kernels, split(): pl.pallas_call(functools.partial(split_kernel, n, rows, kl, rb, first, re...  2.47 us
    pallas_call x1, Pallas kernels, join(): pl.pallas_call(functools.partial(join_kernel, n, rows, rb), out_shape=jax...  1.99 us
    ppermute x1, starting transfers between devices, body(): above = lax.ppermute(bottom, ('ka', 'row'), down)  1.92 us
    pallas_call x1, Pallas kernels, outer(): pl.pallas_call(functools.partial(outer_kernel, n, kl, first), out_shape=[...  1.86 us
  transfers between devices with their start and end apart: 23, of which 12 were waited for; matrix products, arithmetic and copies ran while one was open for 0% of the time, Pallas kernels for 3%

profile of v2, /device:TPU:11, one launch (start us, length us, event | category | flops | bytes accessed | tf_op | source)
XLA Modules:
  0.0 92.6 jit_solution(16504419107496899014)
XLA Ops:
  0.0 0.0 copy-start
  0.0 1.6 %copy-done = bf16[2,128,16,256]{3,2,1,0:T(8,128)(2,1)S(1)} copy-done((bf16[2,128,16,256]{3,2,1,0:T(8,128)(2,1)S(1)}, bf16[2,128,16,256]{3,2,1,0:T(8,128)(2,1)}, u32[]{:S(2)}) %copy-start) | copy-done | bytes 2097176
  1.6 0.0 copy-start.1
  1.6 2.5 %split.1 = (bf16[528,128]{1,0:T(8,128)(2,1)S(1)}, bf16[528,128]{1,0:T(8,128)(2,1)S(1)}, bf16[528,128]{1,0:T(8,128)(2,1)S(1)}, bf16[528,128]{1,0:T(8,128)(2,1)S(1...) custom-call(bf16[4096,256]{1,0:T(8,128)(2,1)S(1)} %bitcast.2), custom_call_target="tpu_custom_call" | custom-call | flops 1000000 | bytes 4194304 | tf_op jit(solution)/shard_map/split/pallas_call | solution.py:69
  4.1 0.7 collective-permute-start
  4.8 0.2 collective-permute-start.1
  5.0 0.3 collective-permute-start.8
  5.3 1.3 %collective-permute-start.9 = (bf16[512,128]{1,0:T(8,128)(2,1)S(1)}, bf16[512,128]{1,0:T(8,128)(2,1)S(1)}, u32[]{:S(2)}, u32[]{:S(2)}) collective-permute-start(bf16[512,128]{1,0:T(8,128)(2,1)S(1)} %get-tuple-element.43), channel_id=1, source_target_pairs={{0,8},{4,12},{8,0},{12,4},{16,24},{20,28},{24,16},{28,20},{1,9},{5... | collective-permute-start | bytes 393224 | tf_op jit(solution)/shard_map/ppermute | solution.py:291
  6.6 0.5 collective-permute-start.2
  7.1 0.0 collective-permute-done.8.refs_1_
  7.1 2.3 %collective-permute-start.3 = (bf16[528,128]{1,0:T(8,128)(2,1)S(1)}, bf16[528,128]{1,0:T(8,128)(2,1)S(1)}, u32[]{:S(2)}, u32[]{:S(2)}) collective-permute-start(bf16[528,128]{1,0:T(8,128)(2,1)S(1)} %get-tuple-element.35), channel_id=1, source_target_pairs={{0,16},{4,20},{8,24},{12,28},{16,0},{20,4},{24,8},{28,12},{1,17},{... | collective-permute-start | bytes 405512 | tf_op jit(solution)/shard_map/ppermute | solution.py:291
  9.4 4.1 %collective-permute-done.9.refs_2_ = bf16[512,128]{1,0:T(8,128)(2,1)S(1)} collective-permute-done((bf16[512,128]{1,0:T(8,128)(2,1)S(1)}, bf16[512,128]{1,0:T(8,128)(2,1)S(1)}, u32[]{:S(2)}, u32[]{:S(2)}) %collective-permute-start.9) | collective-permute-done | bytes 131104 | tf_op jit(solution)/shard_map/ppermute | solution.py:291
  13.5 5.7 %collective-permute-start.4 = (bf16[528,128]{1,0:T(8,128)(2,1)S(1)}, bf16[528,128]{1,0:T(8,128)(2,1)S(1)}, u32[]{:S(2)}, u32[]{:S(2)}) collective-permute-start(bf16[528,128]{1,0:T(8,128)(2,1)S(1)} %get-tuple-element.36), channel_id=1, source_target_pairs={{0,20},{4,16},{8,28},{12,24},{16,4},{20,0},{24,12},{28,8},{1,21},{... | collective-permute-start | bytes 405512 | tf_op jit(solution)/shard_map/ppermute | solution.py:291
  19.2 0.0 collective-permute-done.refs_1_
  19.2 0.0 collective-permute-start.5
  19.2 0.0 collective-permute-done.1.refs_2_
  19.2 0.8 collective-permute-start.6
  20.0 0.0 collective-permute-done.2.refs_3_
  20.0 2.0 %collective-permute-start.10 = (bf16[512,128]{1,0:T(8,128)(2,1)S(1)}, bf16[512,128]{1,0:T(8,128)(2,1)S(1)}, u32[]{:S(2)}, u32[]{:S(2)}) collective-permute-start(bf16[512,128]{1,0:T(8,128)(2,1)S(1)} %get-tuple-element.44), channel_id=1, source_target_pairs={{0,12},{4,8},{8,4},{12,0},{16,28},{20,24},{24,20},{28,16},{1,13},{... | collective-permute-start | bytes 393224 | tf_op jit(solution)/shard_map/ppermute | solution.py:291
  22.0 0.0 collective-permute-done.3.refs_4_
  22.0 0.8 collective-permute-start.11
  22.8 7.0 %collective-permute-done.4.refs_5_ = bf16[528,128]{1,0:T(8,128)(2,1)S(1)} collective-permute-done((bf16[528,128]{1,0:T(8,128)(2,1)S(1)}, bf16[528,128]{1,0:T(8,128)(2,1)S(1)}, u32[]{:S(2)}, u32[]{:S(2)}) %collective-permute-start.4) | collective-permute-done | bytes 135200 | tf_op jit(solution)/shard_map/ppermute | solution.py:291
  29.8 3.5 %collective-permute-start.12 = (bf16[512,128]{1,0:T(8,128)(2,1)S(1)}, bf16[512,128]{1,0:T(8,128)(2,1)S(1)}, u32[]{:S(2)}, u32[]{:S(2)}) collective-permute-start(bf16[512,128]{1,0:T(8,128)(2,1)S(1)} %get-tuple-element.46), channel_id=1, source_target_pairs={{0,20},{4,16},{8,28},{12,24},{16,4},{20,0},{24,12},{28,8},{1,21},{... | collective-permute-start | bytes 393224 | tf_op jit(solution)/shard_map/ppermute | solution.py:291
  33.4 12.4 %collective-permute-done.5.refs_6_ = bf16[528,128]{1,0:T(8,128)(2,1)S(1)} collective-permute-done((bf16[528,128]{1,0:T(8,128)(2,1)S(1)}, bf16[528,128]{1,0:T(8,128)(2,1)S(1)}, u32[]{:S(2)}, u32[]{:S(2)}) %collective-permute-start.5) | collective-permute-done | bytes 135200 | tf_op jit(solution)/shard_map/ppermute | solution.py:291
  45.7 0.2 collective-permute-start.13
  46.0 2.7 %collective-permute-done.6.refs_7_ = bf16[528,128]{1,0:T(8,128)(2,1)S(1)} collective-permute-done((bf16[528,128]{1,0:T(8,128)(2,1)S(1)}, bf16[528,128]{1,0:T(8,128)(2,1)S(1)}, u32[]{:S(2)}, u32[]{:S(2)}) %collective-permute-start.6) | collective-permute-done | bytes 135200 | tf_op jit(solution)/shard_map/ppermute | solution.py:291
  48.6 0.6 collective-permute-start.14
  49.2 0.0 copy-done.1
  49.2 1.9 %outer.1 = (bf16[2176,128]{1,0:T(8,128)(2,1)S(1)}, bf16[2176,128]{1,0:T(8,128)(2,1)S(1)}) custom-call(bf16[528,128]{1,0:T(8,128)(2,1)S(1)} %get-tuple-element.31.refs_0_, bf16[528,128]{1,0:T(8,128)(2,1)S(1)} %collective-permute-done.refs_1_, bf16[528,128]{1,0:T(8,128)(2,1)S(1)} %collective-permute-done.1.refs_2_, ...), custom_call_target="tpu_custom_call" | custom-call | flops 1610612736 | bytes 4194304 | tf_op jit(solution)/shard_map/outer/pallas_call | solution.py:126
  51.1 0.0 collective-permute-done.10.refs_3_
  51.1 1.9 %collective-permute-start.7 = (bf16[2176,128]{1,0:T(8,128)(2,1)S(1)}, bf16[2176,128]{1,0:T(8,128)(2,1)S(1)}, u32[]{:S(2)}, u32[]{:S(2)}) collective-permute-start(bf16[2176,128]{1,0:T(8,128)(2,1)S(1)} %get-tuple-element.39.refs_3_), channel_id=1, source_target_pairs={{0,4},{4,8},{8,12},{12,13},{13,9},{9,5},{5,1},{1,2},{2,6},{6,10},{... | collective-permute-start | bytes 1671176 | tf_op jit(solution)/shard_map/ppermute | solution.py:306
  53.0 0.0 collective-permute-done.11.refs_4_
  53.1 3.4 %collective-permute-start.15 = (bf16[2176,128]{1,0:T(8,128)(2,1)S(1)}, bf16[2176,128]{1,0:T(8,128)(2,1)S(1)}, u32[]{:S(2)}, u32[]{:S(2)}) collective-permute-start(bf16[2176,128]{1,0:T(8,128)(2,1)S(1)} %get-tuple-element.40.refs_1_), channel_id=1, source_target_pairs={{4,0},{8,4},{12,8},{13,12},{9,13},{5,9},{1,5},{2,1},{6,2},{10,6},{... | collective-permute-start | bytes 1671176 | tf_op jit(solution)/shard_map/ppermute | solution.py:307
  56.4 0.0 collective-permute-done.12.refs_5_
  56.4 0.6 collective-permute-done.13.refs_6_
  57.1 2.8 %collective-permute-done.14.refs_7_ = bf16[512,128]{1,0:T(8,128)(2,1)S(1)} collective-permute-done((bf16[512,128]{1,0:T(8,128)(2,1)S(1)}, bf16[512,128]{1,0:T(8,128)(2,1)S(1)}, u32[]{:S(2)}, u32[]{:S(2)}) %collective-permute-start.14) | collective-permute-done | bytes 131104 | tf_op jit(solution)/shard_map/ppermute | solution.py:291
  59.9 1.2 %inner.1.refs_2_ = bf16[2,2048,128]{2,1,0:T(8,128)(2,1)S(1)} custom-call(bf16[512,128]{1,0:T(8,128)(2,1)S(1)} %get-tuple-element.41.refs_0_, bf16[512,128]{1,0:T(8,128)(2,1)S(1)} %collective-permute-done.8.refs_1_, bf16[512,128]{1,0:T(8,128)(2,1)S(1)} %collective-permute-done.9.refs_2_, bf16[512,128]{1,0:T(8,128)(2,1)S(1)} %collective-permute-done.10.refs_3_, ...), custom_call_target="tpu_custom_call" | custom-call | flops 30000001024 | bytes 6291456 | tf_op jit(solution)/shard_map/inner/pallas_call | solution.py:146
  61.1 0.6 collective-permute-done.7.refs_0_
  61.7 1.2 %collective-permute-done.15.refs_4_ = bf16[2176,128]{1,0:T(8,128)(2,1)S(1)} collective-permute-done((bf16[2176,128]{1,0:T(8,128)(2,1)S(1)}, bf16[2176,128]{1,0:T(8,128)(2,1)S(1)}, u32[]{:S(2)}, u32[]{:S(2)}) %collective-permute-start.15) | collective-permute-done | bytes 557088 | tf_op jit(solution)/shard_map/ppermute | solution.py:307
  62.9 7.4 %boxed.1 = (bf16[256,128]{1,0:T(8,128)(2,1)S(1)}, bf16[256,128]{1,0:T(8,128)(2,1)S(1)}, bf16[256,128]{1,0:T(8,128)(2,1)S(1)}, bf16[256,128]{1,0:T(8,128)(2,1)S(1...) custom-call(bf16[2176,128]{1,0:T(8,128)(2,1)S(1)} %collective-permut, ...), custom_call_target="tpu_custom_call" | custom-call | flops 10000000 | bytes 6291456 | tf_op jit(solution)/shard_map/boxed/pallas_call | solution.py:236
  70.3 1.1 %collective-permute-start.16 = (bf16[256,128]{1,0:T(8,128)(2,1)S(1)}, bf16[256,128]{1,0:T(8,128)(2,1)S(1)}, u32[]{:S(2)}, u32[]{:S(2)}) collective-permute-start(bf16[256,128]{1,0:T(8,128)(2,1)S(1)} %get-tuple-element.50), channel_id=1, source_target_pairs={{0,4},{4,0},{8,12},{12,8},{16,20},{20,16},{24,28},{28,24},{1,5},{5... | collective-permute-start | bytes 196616 | tf_op jit(solution)/shard_map/ppermute | solution.py:291
  71.4 1.4 %collective-permute-start.17 = (bf16[256,128]{1,0:T(8,128)(2,1)S(1)}, bf16[256,128]{1,0:T(8,128)(2,1)S(1)}, u32[]{:S(2)}, u32[]{:S(2)}) collective-permute-start(bf16[256,128]{1,0:T(8,128)(2,1)S(1)} %get-tuple-element.51), channel_id=1, source_target_pairs={{0,8},{4,12},{8,0},{12,4},{16,24},{20,28},{24,16},{28,20},{1,9},{5... | collective-permute-start | bytes 196616 | tf_op jit(solution)/shard_map/ppermute | solution.py:291
  72.8 0.3 collective-permute-start.18
  73.1 3.7 %collective-permute-start.19 = (bf16[256,128]{1,0:T(8,128)(2,1)S(1)}, bf16[256,128]{1,0:T(8,128)(2,1)S(1)}, u32[]{:S(2)}, u32[]{:S(2)}) collective-permute-start(bf16[256,128]{1,0:T(8,128)(2,1)S(1)} %get-tuple-element.53), channel_id=1, source_target_pairs={{0,16},{4,20},{8,24},{12,28},{16,0},{20,4},{24,8},{28,12},{1,17},{... | collective-permute-start | bytes 196616 | tf_op jit(solution)/shard_map/ppermute | solution.py:291
  76.9 0.3 collective-permute-start.20
  77.2 0.0 collective-permute-done.16.refs_1_
  77.2 2.9 %collective-permute-start.21 = (bf16[256,128]{1,0:T(8,128)(2,1)S(1)}, bf16[256,128]{1,0:T(8,128)(2,1)S(1)}, u32[]{:S(2)}, u32[]{:S(2)}) collective-permute-start(bf16[256,128]{1,0:T(8,128)(2,1)S(1)} %get-tuple-element.55), channel_id=1, source_target_pairs={{0,24},{4,28},{8,16},{12,20},{16,8},{20,12},{24,0},{28,4},{1,25},{... | collective-permute-start | bytes 196616 | tf_op jit(solution)/shard_map/ppermute | solution.py:291
  80.0 0.0 collective-permute-done.17.refs_2_
  80.0 0.4 collective-permute-start.22
  80.5 0.0 collective-permute-done.18.refs_3_
  80.5 1.3 %collective-permute-done.19.refs_4_ = bf16[256,128]{1,0:T(8,128)(2,1)S(1)} collective-permute-done((bf16[256,128]{1,0:T(8,128)(2,1)S(1)}, bf16[256,128]{1,0:T(8,128)(2,1)S(1)}, u32[]{:S(2)}, u32[]{:S(2)}) %collective-permute-start.19) | collective-permute-done | bytes 65568 | tf_op jit(solution)/shard_map/ppermute | solution.py:291
  81.8 3.1 %collective-permute-done.20.refs_5_ = bf16[256,128]{1,0:T(8,128)(2,1)S(1)} collective-permute-done((bf16[256,128]{1,0:T(8,128)(2,1)S(1)}, bf16[256,128]{1,0:T(8,128)(2,1)S(1)}, u32[]{:S(2)}, u32[]{:S(2)}) %collective-permute-start.20) | collective-permute-done | bytes 65568 | tf_op jit(solution)/shard_map/ppermute | solution.py:291
  84.9 4.3 %collective-permute-done.21.refs_6_ = bf16[256,128]{1,0:T(8,128)(2,1)S(1)} collective-permute-done((bf16[256,128]{1,0:T(8,128)(2,1)S(1)}, bf16[256,128]{1,0:T(8,128)(2,1)S(1)}, u32[]{:S(2)}, u32[]{:S(2)}) %collective-permute-start.21) | collective-permute-done | bytes 65568 | tf_op jit(solution)/shard_map/ppermute | solution.py:291
  89.2 1.4 %collective-permute-done.22.refs_7_ = bf16[256,128]{1,0:T(8,128)(2,1)S(1)} collective-permute-done((bf16[256,128]{1,0:T(8,128)(2,1)S(1)}, bf16[256,128]{1,0:T(8,128)(2,1)S(1)}, u32[]{:S(2)}, u32[]{:S(2)}) %collective-permute-start.22) | collective-permute-done | bytes 65568 | tf_op jit(solution)/shard_map/ppermute | solution.py:291
  90.6 2.0 %join.1 = f32[1024,256]{1,0:T(8,128)} custom-call(bf16[256,128]{1,0:T(8,128)(2,1)S(1)} %get-tuple-element.49.refs_0_, bf16[256,128]{1,0:T(8,128)(2,1)S(1)} %collective-permute-done.16.refs_1_, bf16[256,128]{1,0:T(8,128)(2,1)S(1)} %collective-permute-done.17.refs_2_, bf16[256,128]{1,0:T(8,128)(2,1)S(1)} %collective-permute-done.18.refs_3_, ...), custom_call_target="tpu_custom_call" | custom-call | flops 1000000 | bytes 2097152 | tf_op jit(solution)/shard_map/join/pallas_call | solution.py:268
Async XLA Ops:
  0.0 1.6 %copy-start = (bf16[2,128,16,256]{3,2,1,0:T(8,128)(2,1)S(1)}, bf16[2,128,16,256]{3,2,1,0:T(8,128)(2,1)}, u32[]{:S(2)}) copy-start(bf16[2,128,16,256]{3,2,1,0:T(8,128)(2,1)} %param.2) | copy-start | bytes 6291460
  1.6 47.7 %copy-start.1 = (bf16[8,1024,128]{2,1,0:T(8,128)(2,1)S(1)}, bf16[8,1024,128]{2,1,0:T(8,128)(2,1)}, u32[]{:S(2)}) copy-start(bf16[8,1024,128]{2,1,0:T(8,128)(2,1)} %constant.2.clone.refs_8_) | copy-start | bytes 6291460
  4.1 15.1 %collective-permute-start = (bf16[528,128]{1,0:T(8,128)(2,1)S(1)}, bf16[528,128]{1,0:T(8,128)(2,1)S(1)}, u32[]{:S(2)}, u32[]{:S(2)}) collective-permute-start(bf16[528,128]{1,0:T(8,128)(2,1)S(1)} %get-tuple-element.32), channel_id=1, source_target_pairs={{0,4},{4,0},{8,12},{12,8},{16,20},{20,16},{24,28},{28,24},{1,5},{5... | collective-permute-start | bytes 405512 | tf_op jit(solution)/shard_map/ppermute | solution.py:291
  4.8 14.4 %collective-permute-start.1 = (bf16[528,128]{1,0:T(8,128)(2,1)S(1)}, bf16[528,128]{1,0:T(8,128)(2,1)S(1)}, u32[]{:S(2)}, u32[]{:S(2)}) collective-permute-start(bf16[528,128]{1,0:T(8,128)(2,1)S(1)} %get-tuple-element.33), channel_id=1, source_target_pairs={{0,8},{4,12},{8,0},{12,4},{16,24},{20,28},{24,16},{28,20},{1,9},{5... | collective-permute-start | bytes 405512 | tf_op jit(solution)/shard_map/ppermute | solution.py:291
  5.0 2.1 %collective-permute-start.8 = (bf16[512,128]{1,0:T(8,128)(2,1)S(1)}, bf16[512,128]{1,0:T(8,128)(2,1)S(1)}, u32[]{:S(2)}, u32[]{:S(2)}) collective-permute-start(bf16[512,128]{1,0:T(8,128)(2,1)S(1)} %get-tuple-element.42), channel_id=1, source_target_pairs={{0,4},{4,0},{8,12},{12,8},{16,20},{20,16},{24,28},{28,24},{1,5},{5... | collective-permute-start | bytes 393224 | tf_op jit(solution)/shard_map/ppermute | solution.py:291
  5.3 8.2 %collective-permute-start.9 = (bf16[512,128]{1,0:T(8,128)(2,1)S(1)}, bf16[512,128]{1,0:T(8,128)(2,1)S(1)}, u32[]{:S(2)}, u32[]{:S(2)}) collective-permute-start(bf16[512,128]{1,0:T(8,128)(2,1)S(1)} %get-tuple-element.43), channel_id=1, source_target_pairs={{0,8},{4,12},{8,0},{12,4},{16,24},{20,28},{24,16},{28,20},{1,9},{5... | collective-permute-start | bytes 393224 | tf_op jit(solution)/shard_map/ppermute | solution.py:291
  6.6 13.4 %collective-permute-start.2 = (bf16[528,128]{1,0:T(8,128)(2,1)S(1)}, bf16[528,128]{1,0:T(8,128)(2,1)S(1)}, u32[]{:S(2)}, u32[]{:S(2)}) collective-permute-start(bf16[528,128]{1,0:T(8,128)(2,1)S(1)} %get-tuple-element.34), channel_id=1, source_target_pairs={{0,12},{4,8},{8,4},{12,0},{16,28},{20,24},{24,20},{28,16},{1,13},{... | collective-permute-start | bytes 405512 | tf_op jit(solution)/shard_map/ppermute | solution.py:291
  7.1 14.9 %collective-permute-start.3 = (bf16[528,128]{1,0:T(8,128)(2,1)S(1)}, bf16[528,128]{1,0:T(8,128)(2,1)S(1)}, u32[]{:S(2)}, u32[]{:S(2)}) collective-permute-start(bf16[528,128]{1,0:T(8,128)(2,1)S(1)} %get-tuple-element.35), channel_id=1, source_target_pairs={{0,16},{4,20},{8,24},{12,28},{16,0},{20,4},{24,8},{28,12},{1,17},{... | collective-permute-start | bytes 405512 | tf_op jit(solution)/shard_map/ppermute | solution.py:291
  13.5 16.3 %collective-permute-start.4 = (bf16[528,128]{1,0:T(8,128)(2,1)S(1)}, bf16[528,128]{1,0:T(8,128)(2,1)S(1)}, u32[]{:S(2)}, u32[]{:S(2)}) collective-permute-start(bf16[528,128]{1,0:T(8,128)(2,1)S(1)} %get-tuple-element.36), channel_id=1, source_target_pairs={{0,20},{4,16},{8,28},{12,24},{16,4},{20,0},{24,12},{28,8},{1,21},{... | collective-permute-start | bytes 405512 | tf_op jit(solution)/shard_map/ppermute | solution.py:291
  19.2 26.6 %collective-permute-start.5 = (bf16[528,128]{1,0:T(8,128)(2,1)S(1)}, bf16[528,128]{1,0:T(8,128)(2,1)S(1)}, u32[]{:S(2)}, u32[]{:S(2)}) collective-permute-start(bf16[528,128]{1,0:T(8,128)(2,1)S(1)} %get-tuple-element.37), channel_id=1, source_target_pairs={{0,24},{4,28},{8,16},{12,20},{16,8},{20,12},{24,0},{28,4},{1,25},{... | collective-permute-start | bytes 405512 | tf_op jit(solution)/shard_map/ppermute | solution.py:291
  19.2 29.4 %collective-permute-start.6 = (bf16[528,128]{1,0:T(8,128)(2,1)S(1)}, bf16[528,128]{1,0:T(8,128)(2,1)S(1)}, u32[]{:S(2)}, u32[]{:S(2)}) collective-permute-start(bf16[528,128]{1,0:T(8,128)(2,1)S(1)} %get-tuple-element.38), channel_id=1, source_target_pairs={{0,28},{4,24},{8,20},{12,16},{16,12},{20,8},{24,4},{28,0},{1,29},{... | collective-permute-start | bytes 405512 | tf_op jit(solution)/shard_map/ppermute | solution.py:291
  20.0 31.1 %collective-permute-start.10 = (bf16[512,128]{1,0:T(8,128)(2,1)S(1)}, bf16[512,128]{1,0:T(8,128)(2,1)S(1)}, u32[]{:S(2)}, u32[]{:S(2)}) collective-permute-start(bf16[512,128]{1,0:T(8,128)(2,1)S(1)} %get-tuple-element.44), channel_id=1, source_target_pairs={{0,12},{4,8},{8,4},{12,0},{16,28},{20,24},{24,20},{28,16},{1,13},{... | collective-permute-start | bytes 393224 | tf_op jit(solution)/shard_map/ppermute | solution.py:291
  22.0 31.1 %collective-permute-start.11 = (bf16[512,128]{1,0:T(8,128)(2,1)S(1)}, bf16[512,128]{1,0:T(8,128)(2,1)S(1)}, u32[]{:S(2)}, u32[]{:S(2)}) collective-permute-start(bf16[512,128]{1,0:T(8,128)(2,1)S(1)} %get-tuple-element.45), channel_id=1, source_target_pairs={{0,16},{4,20},{8,24},{12,28},{16,0},{20,4},{24,8},{28,12},{1,17},{... | collective-permute-start | bytes 393224 | tf_op jit(solution)/shard_map/ppermute | solution.py:291
  29.8 26.6 %collective-permute-start.12 = (bf16[512,128]{1,0:T(8,128)(2,1)S(1)}, bf16[512,128]{1,0:T(8,128)(2,1)S(1)}, u32[]{:S(2)}, u32[]{:S(2)}) collective-permute-start(bf16[512,128]{1,0:T(8,128)(2,1)S(1)} %get-tuple-element.46), channel_id=1, source_target_pairs={{0,20},{4,16},{8,28},{12,24},{16,4},{20,0},{24,12},{28,8},{1,21},{... | collective-permute-start | bytes 393224 | tf_op jit(solution)/shard_map/ppermute | solution.py:291
  45.7 11.3 %collective-permute-start.13 = (bf16[512,128]{1,0:T(8,128)(2,1)S(1)}, bf16[512,128]{1,0:T(8,128)(2,1)S(1)}, u32[]{:S(2)}, u32[]{:S(2)}) collective-permute-start(bf16[512,128]{1,0:T(8,128)(2,1)S(1)} %get-tuple-element.47), channel_id=1, source_target_pairs={{0,24},{4,28},{8,16},{12,20},{16,8},{20,12},{24,0},{28,4},{1,25},{... | collective-permute-start | bytes 393224 | tf_op jit(solution)/shard_map/ppermute | solution.py:291
  48.6 11.2 %collective-permute-start.14 = (bf16[512,128]{1,0:T(8,128)(2,1)S(1)}, bf16[512,128]{1,0:T(8,128)(2,1)S(1)}, u32[]{:S(2)}, u32[]{:S(2)}) collective-permute-start(bf16[512,128]{1,0:T(8,128)(2,1)S(1)} %get-tuple-element.48), channel_id=1, source_target_pairs={{0,28},{4,24},{8,20},{12,16},{16,12},{20,8},{24,4},{28,0},{1,29},{... | collective-permute-start | bytes 393224 | tf_op jit(solution)/shard_map/ppermute | solution.py:291
  51.1 10.6 %collective-permute-start.7 = (bf16[2176,128]{1,0:T(8,128)(2,1)S(1)}, bf16[2176,128]{1,0:T(8,128)(2,1)S(1)}, u32[]{:S(2)}, u32[]{:S(2)}) collective-permute-start(bf16[2176,128]{1,0:T(8,128)(2,1)S(1)} %get-tuple-element.39.refs_3_), channel_id=1, source_target_pairs={{0,4},{4,8},{8,12},{12,13},{13,9},{9,5},{5,1},{1,2},{2,6},{6,10},{... | collective-permute-start | bytes 1671176 | tf_op jit(solution)/shard_map/ppermute | solution.py:306
  53.1 9.8 %collective-permute-start.15 = (bf16[2176,128]{1,0:T(8,128)(2,1)S(1)}, bf16[2176,128]{1,0:T(8,128)(2,1)S(1)}, u32[]{:S(2)}, u32[]{:S(2)}) collective-permute-start(bf16[2176,128]{1,0:T(8,128)(2,1)S(1)} %get-tuple-element.40.refs_1_), channel_id=1, source_target_pairs={{4,0},{8,4},{12,8},{13,12},{9,13},{5,9},{1,5},{2,1},{6,2},{10,6},{... | collective-permute-start | bytes 1671176 | tf_op jit(solution)/shard_map/ppermute | solution.py:307
  70.3 6.8 %collective-permute-start.16 = (bf16[256,128]{1,0:T(8,128)(2,1)S(1)}, bf16[256,128]{1,0:T(8,128)(2,1)S(1)}, u32[]{:S(2)}, u32[]{:S(2)}) collective-permute-start(bf16[256,128]{1,0:T(8,128)(2,1)S(1)} %get-tuple-element.50), channel_id=1, source_target_pairs={{0,4},{4,0},{8,12},{12,8},{16,20},{20,16},{24,28},{28,24},{1,5},{5... | collective-permute-start | bytes 196616 | tf_op jit(solution)/shard_map/ppermute | solution.py:291
  71.4 8.6 %collective-permute-start.17 = (bf16[256,128]{1,0:T(8,128)(2,1)S(1)}, bf16[256,128]{1,0:T(8,128)(2,1)S(1)}, u32[]{:S(2)}, u32[]{:S(2)}) collective-permute-start(bf16[256,128]{1,0:T(8,128)(2,1)S(1)} %get-tuple-element.51), channel_id=1, source_target_pairs={{0,8},{4,12},{8,0},{12,4},{16,24},{20,28},{24,16},{28,20},{1,9},{5... | collective-permute-start | bytes 196616 | tf_op jit(solution)/shard_map/ppermute | solution.py:291
  72.8 7.6 %collective-permute-start.18 = (bf16[256,128]{1,0:T(8,128)(2,1)S(1)}, bf16[256,128]{1,0:T(8,128)(2,1)S(1)}, u32[]{:S(2)}, u32[]{:S(2)}) collective-permute-start(bf16[256,128]{1,0:T(8,128)(2,1)S(1)} %get-tuple-element.52), channel_id=1, source_target_pairs={{0,12},{4,8},{8,4},{12,0},{16,28},{20,24},{24,20},{28,16},{1,13},{... | collective-permute-start | bytes 196616 | tf_op jit(solution)/shard_map/ppermute | solution.py:291
  73.1 8.7 %collective-permute-start.19 = (bf16[256,128]{1,0:T(8,128)(2,1)S(1)}, bf16[256,128]{1,0:T(8,128)(2,1)S(1)}, u32[]{:S(2)}, u32[]{:S(2)}) collective-permute-start(bf16[256,128]{1,0:T(8,128)(2,1)S(1)} %get-tuple-element.53), channel_id=1, source_target_pairs={{0,16},{4,20},{8,24},{12,28},{16,0},{20,4},{24,8},{28,12},{1,17},{... | collective-permute-start | bytes 196616 | tf_op jit(solution)/shard_map/ppermute | solution.py:291
  76.9 8.0 %collective-permute-start.20 = (bf16[256,128]{1,0:T(8,128)(2,1)S(1)}, bf16[256,128]{1,0:T(8,128)(2,1)S(1)}, u32[]{:S(2)}, u32[]{:S(2)}) collective-permute-start(bf16[256,128]{1,0:T(8,128)(2,1)S(1)} %get-tuple-element.54), channel_id=1, source_target_pairs={{0,20},{4,16},{8,28},{12,24},{16,4},{20,0},{24,12},{28,8},{1,21},{... | collective-permute-start | bytes 196616 | tf_op jit(solution)/shard_map/ppermute | solution.py:291
  77.2 12.0 %collective-permute-start.21 = (bf16[256,128]{1,0:T(8,128)(2,1)S(1)}, bf16[256,128]{1,0:T(8,128)(2,1)S(1)}, u32[]{:S(2)}, u32[]{:S(2)}) collective-permute-start(bf16[256,128]{1,0:T(8,128)(2,1)S(1)} %get-tuple-element.55), channel_id=1, source_target_pairs={{0,24},{4,28},{8,16},{12,20},{16,8},{20,12},{24,0},{28,4},{1,25},{... | collective-permute-start | bytes 196616 | tf_op jit(solution)/shard_map/ppermute | solution.py:291
  80.0 10.5 %collective-permute-start.22 = (bf16[256,128]{1,0:T(8,128)(2,1)S(1)}, bf16[256,128]{1,0:T(8,128)(2,1)S(1)}, u32[]{:S(2)}, u32[]{:S(2)}) collective-permute-start(bf16[256,128]{1,0:T(8,128)(2,1)S(1)} %get-tuple-element.56), channel_id=1, source_target_pairs={{0,28},{4,24},{8,20},{12,16},{16,12},{20,8},{24,4},{28,0},{1,29},{... | collective-permute-start | bytes 196616 | tf_op jit(solution)/shard_map/ppermute | solution.py:291

commit v3 on v2

--- a/solution.py
+++ b/solution.py
@@ -12,6 +12,7 @@
 K = 1024
 DEPTH = 512
 LANES = 128
+AFTER = 2
 EDGE = 16
 F32 = jnp.float32
 BF16 = jnp.bfloat16
@@ -35,9 +36,9 @@
     return pltpu.CompilerParams(vmem_limit_bytes=mib * 1024 * 1024)
 
 
-def split_kernel(n, rows, kl, rb, first, rest, x_ref, *refs):
+def split_kernel(n, rows, kl, rb, group, edge, x_ref, *refs):
     half = n // 2
-    a_refs, b_refs, x32 = refs[:n], refs[n:-1], refs[-1]
+    outs, x32 = refs[-n - 1 : -1], refs[-1]
     me = lax.axis_index("ka")
     mirrored = lax.axis_index("row") % 2 == 1
     x32[0] = x_ref[:, :LANES].astype(F32)
@@ -46,35 +47,37 @@
     edges = [jnp.zeros((kl, LANES), F32) for _ in range(n * EDGE // LANES)]
     for s in range(n):
         h, row = place(me ^ s, half, rb, mirrored)
-        for refs_of, group in ((a_refs, first), (b_refs, rest)):
-            for slot, j in enumerate(group):
-                for p in range(2):
-                    y = x32[h, pl.ds(p * kl * rows + row + j, kl, stride=rows), :]
-                    refs_of[s][pl.ds((slot * 2 + p) * kl, kl), :] = y.astype(BF16)
-                    at, m = divmod(s * EDGE + p * 8 + 1 + j, LANES)[::-1]
+        for j in range(rb) if edge else group:
+            for p in range(2):
+                y = x32[h, pl.ds(p * kl * rows + row + j, kl, stride=rows), :]
+                if j in group:
+                    slot = group.index(j)
+                    outs[s][pl.ds((slot * 2 + p) * kl, kl), :] = y.astype(BF16)
+                if edge:
+                    m, at = divmod(s * EDGE + p * 8 + 1 + j, LANES)
                     y = pltpu.roll(y, (at + 1 - h) % LANES, 1)
                     edges[m] = jnp.where(lane == at, y, edges[m])
-    for m, e in enumerate(edges):
+    for m, e in enumerate(edges if edge else []):
         if kl < LANES:
             e = jnp.concatenate([e, jnp.zeros((LANES - kl, LANES), F32)], axis=0)
         e = e.T.astype(BF16)
         for i in range(LANES // EDGE):
             s = (m * LANES // EDGE + i) ^ half
-            a_refs[s][pl.ds(len(first) * 2 * kl, EDGE), :] = e[i * EDGE : (i + 1) * EDGE]
-
-
-def split(x, n, rows, kl, rb, first, rest):
-    a_shape = jax.ShapeDtypeStruct((len(first) * 2 * kl + EDGE, LANES), BF16)
-    b_shape = jax.ShapeDtypeStruct((len(rest) * 2 * kl, LANES), BF16)
-    out = pl.pallas_call(
-        functools.partial(split_kernel, n, rows, kl, rb, first, rest),
-        out_shape=[a_shape] * n + ([b_shape] * n if rest else []),
+            outs[s][pl.ds(len(group) * 2 * kl, EDGE), :] = e[i * EDGE : (i + 1) * EDGE]
+
+
+def split(x, n, rows, kl, rb, group, edge, after=()):
+    size = len(group) * 2 * kl + (EDGE if edge else 0)
+    return pl.pallas_call(
+        functools.partial(split_kernel, n, rows, kl, rb, group, edge),
+        out_shape=[jax.ShapeDtypeStruct((size, LANES), BF16)] * n,
+        in_specs=[pl.BlockSpec(memory_space=pltpu.VMEM)]
+        + [pl.BlockSpec(memory_space=pl.ANY)] * len(after),
         scratch_shapes=[pltpu.VMEM((2, 2 * kl * rows, LANES), F32)],
         compiler_params=params(),
         cost_estimate=pl.CostEstimate(flops=10**6, bytes_accessed=4 * 2**20, transcendentals=0),
         name="split",
-    )(x)
-    return out[:n], out[n:]
+    )(x, *after)
 
 
 def transform(t_ref, pieces, kl, slot):
@@ -147,7 +150,7 @@
         functools.partial(inner_kernel, n, kl, rest),
         out_shape=jax.ShapeDtypeStruct((len(rest), 4 * DEPTH, LANES), BF16),
         compiler_params=params(),
-        cost_estimate=pl.CostEstimate(flops=3 * 10**10, bytes_accessed=6 * 2**20, transcendentals=0),
+        cost_estimate=pl.CostEstimate(flops=4 * 10**9, bytes_accessed=6 * 2**20, transcendentals=0),
         name="inner",
     )(*pieces, t)
 
@@ -210,7 +213,7 @@
     def deep(x):
         return x[0] + x[1] + x[2]
 
-    @pl.loop(0, DEPTH // STEP)
+    @pl.loop(0, DEPTH // STEP, unroll=4)
     def _(i):
         z = pl.multiple_of(i * STEP, STEP)
         rim = [deep([edge[t, pl.ds(z + j, STEP), :] for j in (7, 8, 9)]) for t in range(3)]
@@ -283,17 +286,19 @@
     first, rest = (0, rb - 1), tuple(range(1, rb - 1))
     t = jnp.asarray(table().reshape(2 * DEPTH, n, kl).transpose(1, 0, 2))
 
-    order = sorted(range(1, n), key=lambda s: (s & half) == 0)
-
-    def exchange(pieces):
+    far, near, core = range(half, n), range(2, half), range(1, 2)
+
+    def exchange(pieces, order):
         out = list(pieces)
         for s in order:
             out[s] = lax.ppermute(pieces[s], "ka", [(i, i ^ s) for i in range(n)])
         return out
 
-    a, b = split(frames.reshape(2 * kl * rows, cols), n, rows, kl, rb, first, rest)
-    a = exchange(a)
-    b = exchange(b) if rest else []
+    x = frames.reshape(2 * kl * rows, cols)
+    a = exchange(split(x, n, rows, kl, rb, first, True), [*far, *near, *core])
+    b = []
+    if rest:
+        b = exchange(split(x, n, rows, kl, rb, rest, False, [a[[*far, *near, *core][AFTER]]]), [*far, *near, *core])
     top, bottom = outer(a, t, n, kl, first)
 
     def where(h, block):
@@ -307,7 +312,7 @@
     below = lax.ppermute(top, ("ka", "row"), [(j, i) for i, j in down])
     inside = [inner(b, t, n, kl, rest)] if rest else []
     pieces = boxed([above, top, *inside, bottom, below], n, rb)
-    out = join(exchange(pieces), n, rows, rb)
+    out = join(exchange(pieces, [*near, *far, *core]), n, rows, rb)
     return out.reshape(DEPTH // n, rows, cols)
 
 

time: 92.7 us -> 84 us (0.906)
  the two profiles are of different devices: /device:TPU:11 before, /device:TPU:1 now
where the time goes in v3:
time: 84 us; the launch traced here: 82.9 us
  starting transfers between devices  42.3 us (50%)
  waiting for transfers between devices  24.8 us (30%)
  Pallas kernels  14.1 us (17%)
  local copies, waits for them, and re-layouts  1.59 us (2%)
    ppermute x21, starting transfers between devices, exchange(): out[s] = lax.ppermute(pieces[s], 'ka', [(i, i ^ s) for i in range(n)])  28 us
    ppermute x21, waiting for transfers between devices, exchange(): out[s] = lax.ppermute(pieces[s], 'ka', [(i, i ^ s) for i in range(n)])  24.8 us
    ppermute x1, starting transfers between devices, body(): above = lax.ppermute(bottom, ('ka', 'row'), down)  9.15 us
    pallas_call x1, Pallas kernels, boxed(): pl.pallas_call(functools.partial(box_kernel, n, rb), out_shape=[jax.Shape...  5.36 us
    ppermute x1, starting transfers between devices, body(): below = lax.ppermute(top, ('ka', 'row'), [(j, i) for i, j in down])  5.13 us
    pallas_call x2, Pallas kernels, split(): pl.pallas_call(functools.partial(split_kernel, n, rows, kl, rb, group, ed...  3.61 us
    pallas_call x1, Pallas kernels, join(): pl.pallas_call(functools.partial(join_kernel, n, rows, rb), out_shape=jax...  1.99 us
    pallas_call x1, Pallas kernels, outer(): pl.pallas_call(functools.partial(outer_kernel, n, kl, first), out_shape=[...  1.87 us
  transfers between devices with their start and end apart: 23, of which 7 were waited for; matrix products, arithmetic and copies ran while one was open for 0% of the time, Pallas kernels for 5%

profile of v3, /device:TPU:1, one launch (start us, length us, event | category | flops | bytes accessed | tf_op | source)
XLA Modules:
  0.0 82.9 jit_solution(5481392346996290788)
XLA Ops:
  0.0 0.0 copy-start
  0.0 1.6 %copy-done = bf16[2,128,16,256]{3,2,1,0:T(8,128)(2,1)S(1)} copy-done((bf16[2,128,16,256]{3,2,1,0:T(8,128)(2,1)S(1)}, bf16[2,128,16,256]{3,2,1,0:T(8,128)(2,1)}, u32[]{:S(2)}) %copy-start) | copy-done | bytes 2097176
  1.6 0.0 copy-start.1
  1.6 2.5 %split.2 = (bf16[528,128]{1,0:T(8,128)(2,1)S(1)}, bf16[528,128]{1,0:T(8,128)(2,1)S(1)}, bf16[528,128]{1,0:T(8,128)(2,1)S(1)}, bf16[528,128]{1,0:T(8,128)(2,1)S(1...) custom-call(bf16[4096,256]{1,0:T(8,128)(2,1)S(1)} %bitcast.2), custom_call_target="tpu_custom_call" | custom-call | flops 1000000 | bytes 4194304 | tf_op jit(solution)/shard_map/split/pallas_call | solution.py:71
  4.0 4.2 %collective-permute-start.5 = (bf16[528,128]{1,0:T(8,128)(2,1)S(1)}, bf16[528,128]{1,0:T(8,128)(2,1)S(1)}, u32[]{:S(2)}, u32[]{:S(2)}) collective-permute-start(bf16[528,128]{1,0:T(8,128)(2,1)S(1)} %get-tuple-element.37), channel_id=1, source_target_pairs={{0,24},{4,28},{8,16},{12,20},{16,8},{20,12},{24,0},{28,4},{1,25},{... | collective-permute-start | bytes 405512 | tf_op jit(solution)/shard_map/ppermute | solution.py:294
  8.2 1.0 %collective-permute-start = (bf16[528,128]{1,0:T(8,128)(2,1)S(1)}, bf16[528,128]{1,0:T(8,128)(2,1)S(1)}, u32[]{:S(2)}, u32[]{:S(2)}) collective-permute-start(bf16[528,128]{1,0:T(8,128)(2,1)S(1)} %get-tuple-element.32), channel_id=1, source_target_pairs={{0,4},{4,0},{8,12},{12,8},{16,20},{20,16},{24,28},{28,24},{1,5},{5... | collective-permute-start | bytes 405512 | tf_op jit(solution)/shard_map/ppermute | solution.py:294
  9.2 0.0 collective-permute-start.1
  9.2 1.6 %collective-permute-start.2 = (bf16[528,128]{1,0:T(8,128)(2,1)S(1)}, bf16[528,128]{1,0:T(8,128)(2,1)S(1)}, u32[]{:S(2)}, u32[]{:S(2)}) collective-permute-start(bf16[528,128]{1,0:T(8,128)(2,1)S(1)} %get-tuple-element.34), channel_id=1, source_target_pairs={{0,12},{4,8},{8,4},{12,0},{16,28},{20,24},{24,20},{28,16},{1,13},{... | collective-permute-start | bytes 405512 | tf_op jit(solution)/shard_map/ppermute | solution.py:294
  10.8 0.0 collective-permute-start.3
  10.8 0.8 collective-permute-done.5.refs_6_.refs_0_
  11.6 5.3 %collective-permute-start.4 = (bf16[528,128]{1,0:T(8,128)(2,1)S(1)}, bf16[528,128]{1,0:T(8,128)(2,1)S(1)}, u32[]{:S(2)}, u32[]{:S(2)}) collective-permute-start(bf16[528,128]{1,0:T(8,128)(2,1)S(1)} %get-tuple-element.36), channel_id=1, source_target_pairs={{0,20},{4,16},{8,28},{12,24},{16,4},{20,0},{24,12},{28,8},{1,21},{... | collective-permute-start | bytes 405512 | tf_op jit(solution)/shard_map/ppermute | solution.py:294
  16.9 0.0 collective-permute-done.refs_1_
  16.9 0.3 collective-permute-start.6
  17.1 1.2 %split.3 = (bf16[512,128]{1,0:T(8,128)(2,1)S(1)}, bf16[512,128]{1,0:T(8,128)(2,1)S(1)}, bf16[512,128]{1,0:T(8,128)(2,1)S(1)}, bf16[512,128]{1,0:T(8,128)(2,1)S(1...) custom-call(bf16[4096,256]{1,0:T(8,128)(2,1)S(1)} %bitcast.3, ...), custom_call_target="tpu_custom_call" | custom-call | flops 1000000 | bytes 4194304 | tf_op jit(solution)/shard_map/split/pallas_call | solution.py:71
  18.3 0.6 collective-permute-done.1.refs_2_
  18.9 0.0 collective-permute-start.10
  19.0 3.3 %collective-permute-done.2.refs_3_ = bf16[528,128]{1,0:T(8,128)(2,1)S(1)} collective-permute-done((bf16[528,128]{1,0:T(8,128)(2,1)S(1)}, bf16[528,128]{1,0:T(8,128)(2,1)S(1)}, u32[]{:S(2)}, u32[]{:S(2)}) %collective-permute-start.2) | collective-permute-done | bytes 135200 | tf_op jit(solution)/shard_map/ppermute | solution.py:294
  22.2 1.2 %collective-permute-start.11 = (bf16[512,128]{1,0:T(8,128)(2,1)S(1)}, bf16[512,128]{1,0:T(8,128)(2,1)S(1)}, u32[]{:S(2)}, u32[]{:S(2)}) collective-permute-start(bf16[512,128]{1,0:T(8,128)(2,1)S(1)} %get-tuple-element.45), channel_id=1, source_target_pairs={{0,16},{4,20},{8,24},{12,28},{16,0},{20,4},{24,8},{28,12},{1,17},{... | collective-permute-start | bytes 393224 | tf_op jit(solution)/shard_map/ppermute | solution.py:294
  23.4 0.0 collective-permute-done.3.refs_4_
  23.4 1.6 %collective-permute-start.12 = (bf16[512,128]{1,0:T(8,128)(2,1)S(1)}, bf16[512,128]{1,0:T(8,128)(2,1)S(1)}, u32[]{:S(2)}, u32[]{:S(2)}) collective-permute-start(bf16[512,128]{1,0:T(8,128)(2,1)S(1)} %get-tuple-element.46), channel_id=1, source_target_pairs={{0,20},{4,16},{8,28},{12,24},{16,4},{20,0},{24,12},{28,8},{1,21},{... | collective-permute-start | bytes 393224 | tf_op jit(solution)/shard_map/ppermute | solution.py:294
  25.0 4.9 %collective-permute-done.4.refs_5_ = bf16[528,128]{1,0:T(8,128)(2,1)S(1)} collective-permute-done((bf16[528,128]{1,0:T(8,128)(2,1)S(1)}, bf16[528,128]{1,0:T(8,128)(2,1)S(1)}, u32[]{:S(2)}, u32[]{:S(2)}) %collective-permute-start.4) | collective-permute-done | bytes 135200 | tf_op jit(solution)/shard_map/ppermute | solution.py:294
  29.9 0.0 collective-permute-start.13
  29.9 0.0 collective-permute-done.6.refs_7_
  29.9 0.0 copy-done.1
  29.9 1.9 %outer.1 = (bf16[2176,128]{1,0:T(8,128)(2,1)S(1)}, bf16[2176,128]{1,0:T(8,128)(2,1)S(1)}) custom-call(bf16[528,128]{1,0:T(8,128)(2,1)S(1)} %get-tuple-element.31.refs_0_, bf16[528,128]{1,0:T(8,128)(2,1)S(1)} %collective-permute-done.refs_1_, bf16[528,128]{1,0:T(8,128)(2,1)S(1)} %collective-permute-done.1.refs_2_, ...), custom_call_target="tpu_custom_call" | custom-call | flops 1610612736 | bytes 4194304 | tf_op jit(solution)/shard_map/outer/pallas_call | solution.py:129
  31.8 5.1 %collective-permute-start.15 = (bf16[2176,128]{1,0:T(8,128)(2,1)S(1)}, bf16[2176,128]{1,0:T(8,128)(2,1)S(1)}, u32[]{:S(2)}, u32[]{:S(2)}) collective-permute-start(bf16[2176,128]{1,0:T(8,128)(2,1)S(1)} %get-tuple-element.40.refs_1_), channel_id=1, source_target_pairs={{4,0},{8,4},{12,8},{13,12},{9,13},{5,9},{1,5},{2,1},{6,2},{10,6},{... | collective-permute-start | bytes 1671176 | tf_op jit(solution)/shard_map/ppermute | solution.py:312
  36.9 0.0 collective-permute-done.10.refs_3_
  36.9 9.2 %collective-permute-start.7 = (bf16[2176,128]{1,0:T(8,128)(2,1)S(1)}, bf16[2176,128]{1,0:T(8,128)(2,1)S(1)}, u32[]{:S(2)}, u32[]{:S(2)}) collective-permute-start(bf16[2176,128]{1,0:T(8,128)(2,1)S(1)} %get-tuple-element.39.refs_3_), channel_id=1, source_target_pairs={{0,4},{4,8},{8,12},{12,13},{13,9},{9,5},{5,1},{1,2},{2,6},{6,10},{... | collective-permute-start | bytes 1671176 | tf_op jit(solution)/shard_map/ppermute | solution.py:311
  46.1 0.0 collective-permute-done.11.refs_4_
  46.1 0.2 collective-permute-start.14
  46.3 0.0 collective-permute-done.12.refs_5_
  46.3 0.1 collective-permute-start.8
  46.4 0.0 collective-permute-done.13.refs_6_
  46.4 3.2 %collective-permute-start.9 = (bf16[512,128]{1,0:T(8,128)(2,1)S(1)}, bf16[512,128]{1,0:T(8,128)(2,1)S(1)}, u32[]{:S(2)}, u32[]{:S(2)}) collective-permute-start(bf16[512,128]{1,0:T(8,128)(2,1)S(1)} %get-tuple-element.43), channel_id=1, source_target_pairs={{0,8},{4,12},{8,0},{12,4},{16,24},{20,28},{24,16},{28,20},{1,9},{5... | collective-permute-start | bytes 393224 | tf_op jit(solution)/shard_map/ppermute | solution.py:294
  49.6 7.2 %collective-permute-done.14.refs_7_ = bf16[512,128]{1,0:T(8,128)(2,1)S(1)} collective-permute-done((bf16[512,128]{1,0:T(8,128)(2,1)S(1)}, bf16[512,128]{1,0:T(8,128)(2,1)S(1)}, u32[]{:S(2)}, u32[]{:S(2)}) %collective-permute-start.14) | collective-permute-done | bytes 131104 | tf_op jit(solution)/shard_map/ppermute | solution.py:294
  56.8 0.0 collective-permute-done.8.refs_1_
  56.8 1.4 %collective-permute-done.9.refs_2_ = bf16[512,128]{1,0:T(8,128)(2,1)S(1)} collective-permute-done((bf16[512,128]{1,0:T(8,128)(2,1)S(1)}, bf16[512,128]{1,0:T(8,128)(2,1)S(1)}, u32[]{:S(2)}, u32[]{:S(2)}) %collective-permute-start.9) | collective-permute-done | bytes 131104 | tf_op jit(solution)/shard_map/ppermute | solution.py:294
  58.2 1.2 %inner.1.refs_2_ = bf16[2,2048,128]{2,1,0:T(8,128)(2,1)S(1)} custom-call(bf16[512,128]{1,0:T(8,128)(2,1)S(1)} %get-tuple-element.41.refs_0_, bf16[512,128]{1,0:T(8,128)(2,1)S(1)} %collective-permute-done.8.refs_1_, bf16[512,128]{1,0:T(8,128)(2,1)S(1)} %collective-permute-done.9.refs_2_, bf16[512,128]{1,0:T(8,128)(2,1)S(1)} %collective-permute-done.10.refs_3_, ...), custom_call_target="tpu_custom_call" | custom-call | flops 4000000000 | bytes 6291456 | tf_op jit(solution)/shard_map/inner/pallas_call | solution.py:149
  59.4 0.0 collective-permute-done.15.refs_4_
  59.4 0.0 collective-permute-done.7.refs_0_
  59.4 5.4 %boxed.1 = (bf16[256,128]{1,0:T(8,128)(2,1)S(1)}, bf16[256,128]{1,0:T(8,128)(2,1)S(1)}, bf16[256,128]{1,0:T(8,128)(2,1)S(1)}, bf16[256,128]{1,0:T(8,128)(2,1)S(1...) custom-call(bf16[2176,128]{1,0:T(8,128)(2,1)S(1)} %collective-permut, ...), custom_call_target="tpu_custom_call" | custom-call | flops 10000000 | bytes 6291456 | tf_op jit(solution)/shard_map/boxed/pallas_call | solution.py:239
  64.8 0.1 collective-permute-start.16
  64.9 2.0 %collective-permute-start.17 = (bf16[256,128]{1,0:T(8,128)(2,1)S(1)}, bf16[256,128]{1,0:T(8,128)(2,1)S(1)}, u32[]{:S(2)}, u32[]{:S(2)}) collective-permute-start(bf16[256,128]{1,0:T(8,128)(2,1)S(1)} %get-tuple-element.51), channel_id=1, source_target_pairs={{0,8},{4,12},{8,0},{12,4},{16,24},{20,28},{24,16},{28,20},{1,9},{5... | collective-permute-start | bytes 196616 | tf_op jit(solution)/shard_map/ppermute | solution.py:294
  66.8 0.3 collective-permute-start.18
  67.2 2.6 %collective-permute-start.19 = (bf16[256,128]{1,0:T(8,128)(2,1)S(1)}, bf16[256,128]{1,0:T(8,128)(2,1)S(1)}, u32[]{:S(2)}, u32[]{:S(2)}) collective-permute-start(bf16[256,128]{1,0:T(8,128)(2,1)S(1)} %get-tuple-element.53), channel_id=1, source_target_pairs={{0,16},{4,20},{8,24},{12,28},{16,0},{20,4},{24,8},{28,12},{1,17},{... | collective-permute-start | bytes 196616 | tf_op jit(solution)/shard_map/ppermute | solution.py:294
  69.8 0.3 collective-permute-start.20
  70.1 0.0 collective-permute-done.16.refs_1_
  70.1 3.5 %collective-permute-start.21 = (bf16[256,128]{1,0:T(8,128)(2,1)S(1)}, bf16[256,128]{1,0:T(8,128)(2,1)S(1)}, u32[]{:S(2)}, u32[]{:S(2)}) collective-permute-start(bf16[256,128]{1,0:T(8,128)(2,1)S(1)} %get-tuple-element.55), channel_id=1, source_target_pairs={{0,24},{4,28},{8,16},{12,20},{16,8},{20,12},{24,0},{28,4},{1,25},{... | collective-permute-start | bytes 196616 | tf_op jit(solution)/shard_map/ppermute | solution.py:294
  73.6 0.0 collective-permute-done.17.refs_2_
  73.6 0.7 collective-permute-start.22
  74.3 0.0 collective-permute-done.18.refs_3_
  74.3 0.0 collective-permute-done.19.refs_4_
  74.3 6.6 %collective-permute-done.20.refs_5_ = bf16[256,128]{1,0:T(8,128)(2,1)S(1)} collective-permute-done((bf16[256,128]{1,0:T(8,128)(2,1)S(1)}, bf16[256,128]{1,0:T(8,128)(2,1)S(1)}, u32[]{:S(2)}, u32[]{:S(2)}) %collective-permute-start.20) | collective-permute-done | bytes 65568 | tf_op jit(solution)/shard_map/ppermute | solution.py:294
  80.9 0.0 collective-permute-done.21.refs_6_
  80.9 0.0 collective-permute-done.22.refs_7_
  80.9 2.0 %join.1 = f32[1024,256]{1,0:T(8,128)} custom-call(bf16[256,128]{1,0:T(8,128)(2,1)S(1)} %get-tuple-element.49.refs_0_, bf16[256,128]{1,0:T(8,128)(2,1)S(1)} %collective-permute-done.16.refs_1_, bf16[256,128]{1,0:T(8,128)(2,1)S(1)} %collective-permute-done.17.refs_2_, bf16[256,128]{1,0:T(8,128)(2,1)S(1)} %collective-permute-done.18.refs_3_, ...), custom_call_target="tpu_custom_call" | custom-call | flops 1000000 | bytes 2097152 | tf_op jit(solution)/shard_map/join/pallas_call | solution.py:271
Async XLA Ops:
  0.0 1.6 %copy-start = (bf16[2,128,16,256]{3,2,1,0:T(8,128)(2,1)S(1)}, bf16[2,128,16,256]{3,2,1,0:T(8,128)(2,1)}, u32[]{:S(2)}) copy-start(bf16[2,128,16,256]{3,2,1,0:T(8,128)(2,1)} %param.2) | copy-start | bytes 6291460
  1.6 28.3 %copy-start.1 = (bf16[8,1024,128]{2,1,0:T(8,128)(2,1)S(1)}, bf16[8,1024,128]{2,1,0:T(8,128)(2,1)}, u32[]{:S(2)}) copy-start(bf16[8,1024,128]{2,1,0:T(8,128)(2,1)} %constant.2.clone.refs_8_) | copy-start | bytes 6291460
  4.0 7.6 %collective-permute-start.5 = (bf16[528,128]{1,0:T(8,128)(2,1)S(1)}, bf16[528,128]{1,0:T(8,128)(2,1)S(1)}, u32[]{:S(2)}, u32[]{:S(2)}) collective-permute-start(bf16[528,128]{1,0:T(8,128)(2,1)S(1)} %get-tuple-element.37), channel_id=1, source_target_pairs={{0,24},{4,28},{8,16},{12,20},{16,8},{20,12},{24,0},{28,4},{1,25},{... | collective-permute-start | bytes 405512 | tf_op jit(solution)/shard_map/ppermute | solution.py:294
  8.2 8.6 %collective-permute-start = (bf16[528,128]{1,0:T(8,128)(2,1)S(1)}, bf16[528,128]{1,0:T(8,128)(2,1)S(1)}, u32[]{:S(2)}, u32[]{:S(2)}) collective-permute-start(bf16[528,128]{1,0:T(8,128)(2,1)S(1)} %get-tuple-element.32), channel_id=1, source_target_pairs={{0,4},{4,0},{8,12},{12,8},{16,20},{20,16},{24,28},{28,24},{1,5},{5... | collective-permute-start | bytes 405512 | tf_op jit(solution)/shard_map/ppermute | solution.py:294
  9.2 9.7 %collective-permute-start.1 = (bf16[528,128]{1,0:T(8,128)(2,1)S(1)}, bf16[528,128]{1,0:T(8,128)(2,1)S(1)}, u32[]{:S(2)}, u32[]{:S(2)}) collective-permute-start(bf16[528,128]{1,0:T(8,128)(2,1)S(1)} %get-tuple-element.33), channel_id=1, source_target_pairs={{0,8},{4,12},{8,0},{12,4},{16,24},{20,28},{24,16},{28,20},{1,9},{5... | collective-permute-start | bytes 405512 | tf_op jit(solution)/shard_map/ppermute | solution.py:294
  9.2 13.0 %collective-permute-start.2 = (bf16[528,128]{1,0:T(8,128)(2,1)S(1)}, bf16[528,128]{1,0:T(8,128)(2,1)S(1)}, u32[]{:S(2)}, u32[]{:S(2)}) collective-permute-start(bf16[528,128]{1,0:T(8,128)(2,1)S(1)} %get-tuple-element.34), channel_id=1, source_target_pairs={{0,12},{4,8},{8,4},{12,0},{16,28},{20,24},{24,20},{28,16},{1,13},{... | collective-permute-start | bytes 405512 | tf_op jit(solution)/shard_map/ppermute | solution.py:294
  10.8 12.5 %collective-permute-start.3 = (bf16[528,128]{1,0:T(8,128)(2,1)S(1)}, bf16[528,128]{1,0:T(8,128)(2,1)S(1)}, u32[]{:S(2)}, u32[]{:S(2)}) collective-permute-start(bf16[528,128]{1,0:T(8,128)(2,1)S(1)} %get-tuple-element.35), channel_id=1, source_target_pairs={{0,16},{4,20},{8,24},{12,28},{16,0},{20,4},{24,8},{28,12},{1,17},{... | collective-permute-start | bytes 405512 | tf_op jit(solution)/shard_map/ppermute | solution.py:294
  11.6 18.3 %collective-permute-start.4 = (bf16[528,128]{1,0:T(8,128)(2,1)S(1)}, bf16[528,128]{1,0:T(8,128)(2,1)S(1)}, u32[]{:S(2)}, u32[]{:S(2)}) collective-permute-start(bf16[528,128]{1,0:T(8,128)(2,1)S(1)} %get-tuple-element.36), channel_id=1, source_target_pairs={{0,20},{4,16},{8,28},{12,24},{16,4},{20,0},{24,12},{28,8},{1,21},{... | collective-permute-start | bytes 405512 | tf_op jit(solution)/shard_map/ppermute | solution.py:294
  16.9 13.0 %collective-permute-start.6 = (bf16[528,128]{1,0:T(8,128)(2,1)S(1)}, bf16[528,128]{1,0:T(8,128)(2,1)S(1)}, u32[]{:S(2)}, u32[]{:S(2)}) collective-permute-start(bf16[528,128]{1,0:T(8,128)(2,1)S(1)} %get-tuple-element.38), channel_id=1, source_target_pairs={{0,28},{4,24},{8,20},{12,16},{16,12},{20,8},{24,4},{28,0},{1,29},{... | collective-permute-start | bytes 405512 | tf_op jit(solution)/shard_map/ppermute | solution.py:294
  18.9 18.0 %collective-permute-start.10 = (bf16[512,128]{1,0:T(8,128)(2,1)S(1)}, bf16[512,128]{1,0:T(8,128)(2,1)S(1)}, u32[]{:S(2)}, u32[]{:S(2)}) collective-permute-start(bf16[512,128]{1,0:T(8,128)(2,1)S(1)} %get-tuple-element.44), channel_id=1, source_target_pairs={{0,12},{4,8},{8,4},{12,0},{16,28},{20,24},{24,20},{28,16},{1,13},{... | collective-permute-start | bytes 393224 | tf_op jit(solution)/shard_map/ppermute | solution.py:294
  22.2 23.9 %collective-permute-start.11 = (bf16[512,128]{1,0:T(8,128)(2,1)S(1)}, bf16[512,128]{1,0:T(8,128)(2,1)S(1)}, u32[]{:S(2)}, u32[]{:S(2)}) collective-permute-start(bf16[512,128]{1,0:T(8,128)(2,1)S(1)} %get-tuple-element.45), channel_id=1, source_target_pairs={{0,16},{4,20},{8,24},{12,28},{16,0},{20,4},{24,8},{28,12},{1,17},{... | collective-permute-start | bytes 393224 | tf_op jit(solution)/shard_map/ppermute | solution.py:294
  23.4 22.9 %collective-permute-start.12 = (bf16[512,128]{1,0:T(8,128)(2,1)S(1)}, bf16[512,128]{1,0:T(8,128)(2,1)S(1)}, u32[]{:S(2)}, u32[]{:S(2)}) collective-permute-start(bf16[512,128]{1,0:T(8,128)(2,1)S(1)} %get-tuple-element.46), channel_id=1, source_target_pairs={{0,20},{4,16},{8,28},{12,24},{16,4},{20,0},{24,12},{28,8},{1,21},{... | collective-permute-start | bytes 393224 | tf_op jit(solution)/shard_map/ppermute | solution.py:294
  29.9 16.5 %collective-permute-start.13 = (bf16[512,128]{1,0:T(8,128)(2,1)S(1)}, bf16[512,128]{1,0:T(8,128)(2,1)S(1)}, u32[]{:S(2)}, u32[]{:S(2)}) collective-permute-start(bf16[512,128]{1,0:T(8,128)(2,1)S(1)} %get-tuple-element.47), channel_id=1, source_target_pairs={{0,24},{4,28},{8,16},{12,20},{16,8},{20,12},{24,0},{28,4},{1,25},{... | collective-permute-start | bytes 393224 | tf_op jit(solution)/shard_map/ppermute | solution.py:294
  31.8 27.6 %collective-permute-start.15 = (bf16[2176,128]{1,0:T(8,128)(2,1)S(1)}, bf16[2176,128]{1,0:T(8,128)(2,1)S(1)}, u32[]{:S(2)}, u32[]{:S(2)}) collective-permute-start(bf16[2176,128]{1,0:T(8,128)(2,1)S(1)} %get-tuple-element.40.refs_1_), channel_id=1, source_target_pairs={{4,0},{8,4},{12,8},{13,12},{9,13},{5,9},{1,5},{2,1},{6,2},{10,6},{... | collective-permute-start | bytes 1671176 | tf_op jit(solution)/shard_map/ppermute | solution.py:312
  36.9 22.5 %collective-permute-start.7 = (bf16[2176,128]{1,0:T(8,128)(2,1)S(1)}, bf16[2176,128]{1,0:T(8,128)(2,1)S(1)}, u32[]{:S(2)}, u32[]{:S(2)}) collective-permute-start(bf16[2176,128]{1,0:T(8,128)(2,1)S(1)} %get-tuple-element.39.refs_3_), channel_id=1, source_target_pairs={{0,4},{4,8},{8,12},{12,13},{13,9},{9,5},{5,1},{1,2},{2,6},{6,10},{... | collective-permute-start | bytes 1671176 | tf_op jit(solution)/shard_map/ppermute | solution.py:311
  46.1 10.7 %collective-permute-start.14 = (bf16[512,128]{1,0:T(8,128)(2,1)S(1)}, bf16[512,128]{1,0:T(8,128)(2,1)S(1)}, u32[]{:S(2)}, u32[]{:S(2)}) collective-permute-start(bf16[512,128]{1,0:T(8,128)(2,1)S(1)} %get-tuple-element.48), channel_id=1, source_target_pairs={{0,28},{4,24},{8,20},{12,16},{16,12},{20,8},{24,4},{28,0},{1,29},{... | collective-permute-start | bytes 393224 | tf_op jit(solution)/shard_map/ppermute | solution.py:294
  46.3 10.4 %collective-permute-start.8 = (bf16[512,128]{1,0:T(8,128)(2,1)S(1)}, bf16[512,128]{1,0:T(8,128)(2,1)S(1)}, u32[]{:S(2)}, u32[]{:S(2)}) collective-permute-start(bf16[512,128]{1,0:T(8,128)(2,1)S(1)} %get-tuple-element.42), channel_id=1, source_target_pairs={{0,4},{4,0},{8,12},{12,8},{16,20},{20,16},{24,28},{28,24},{1,5},{5... | collective-permute-start | bytes 393224 | tf_op jit(solution)/shard_map/ppermute | solution.py:294
  46.4 11.7 %collective-permute-start.9 = (bf16[512,128]{1,0:T(8,128)(2,1)S(1)}, bf16[512,128]{1,0:T(8,128)(2,1)S(1)}, u32[]{:S(2)}, u32[]{:S(2)}) collective-permute-start(bf16[512,128]{1,0:T(8,128)(2,1)S(1)} %get-tuple-element.43), channel_id=1, source_target_pairs={{0,8},{4,12},{8,0},{12,4},{16,24},{20,28},{24,16},{28,20},{1,9},{5... | collective-permute-start | bytes 393224 | tf_op jit(solution)/shard_map/ppermute | solution.py:294
  64.8 5.3 %collective-permute-start.16 = (bf16[256,128]{1,0:T(8,128)(2,1)S(1)}, bf16[256,128]{1,0:T(8,128)(2,1)S(1)}, u32[]{:S(2)}, u32[]{:S(2)}) collective-permute-start(bf16[256,128]{1,0:T(8,128)(2,1)S(1)} %get-tuple-element.50), channel_id=1, source_target_pairs={{0,4},{4,0},{8,12},{12,8},{16,20},{20,16},{24,28},{28,24},{1,5},{5... | collective-permute-start | bytes 196616 | tf_op jit(solution)/shard_map/ppermute | solution.py:294
  64.9 8.7 %collective-permute-start.17 = (bf16[256,128]{1,0:T(8,128)(2,1)S(1)}, bf16[256,128]{1,0:T(8,128)(2,1)S(1)}, u32[]{:S(2)}, u32[]{:S(2)}) collective-permute-start(bf16[256,128]{1,0:T(8,128)(2,1)S(1)} %get-tuple-element.51), channel_id=1, source_target_pairs={{0,8},{4,12},{8,0},{12,4},{16,24},{20,28},{24,16},{28,20},{1,9},{5... | collective-permute-start | bytes 196616 | tf_op jit(solution)/shard_map/ppermute | solution.py:294
  66.8 7.4 %collective-permute-start.18 = (bf16[256,128]{1,0:T(8,128)(2,1)S(1)}, bf16[256,128]{1,0:T(8,128)(2,1)S(1)}, u32[]{:S(2)}, u32[]{:S(2)}) collective-permute-start(bf16[256,128]{1,0:T(8,128)(2,1)S(1)} %get-tuple-element.52), channel_id=1, source_target_pairs={{0,12},{4,8},{8,4},{12,0},{16,28},{20,24},{24,20},{28,16},{1,13},{... | collective-permute-start | bytes 196616 | tf_op jit(solution)/shard_map/ppermute | solution.py:294
  67.2 7.1 %collective-permute-start.19 = (bf16[256,128]{1,0:T(8,128)(2,1)S(1)}, bf16[256,128]{1,0:T(8,128)(2,1)S(1)}, u32[]{:S(2)}, u32[]{:S(2)}) collective-permute-start(bf16[256,128]{1,0:T(8,128)(2,1)S(1)} %get-tuple-element.53), channel_id=1, source_target_pairs={{0,16},{4,20},{8,24},{12,28},{16,0},{20,4},{24,8},{28,12},{1,17},{... | collective-permute-start | bytes 196616 | tf_op jit(solution)/shard_map/ppermute | solution.py:294
  69.8 11.1 %collective-permute-start.20 = (bf16[256,128]{1,0:T(8,128)(2,1)S(1)}, bf16[256,128]{1,0:T(8,128)(2,1)S(1)}, u32[]{:S(2)}, u32[]{:S(2)}) collective-permute-start(bf16[256,128]{1,0:T(8,128)(2,1)S(1)} %get-tuple-element.54), channel_id=1, source_target_pairs={{0,20},{4,16},{8,28},{12,24},{16,4},{20,0},{24,12},{28,8},{1,21},{... | collective-permute-start | bytes 196616 | tf_op jit(solution)/shard_map/ppermute | solution.py:294
  70.1 10.8 %collective-permute-start.21 = (bf16[256,128]{1,0:T(8,128)(2,1)S(1)}, bf16[256,128]{1,0:T(8,128)(2,1)S(1)}, u32[]{:S(2)}, u32[]{:S(2)}) collective-permute-start(bf16[256,128]{1,0:T(8,128)(2,1)S(1)} %get-tuple-element.55), channel_id=1, source_target_pairs={{0,24},{4,28},{8,16},{12,20},{16,8},{20,12},{24,0},{28,4},{1,25},{... | collective-permute-start | bytes 196616 | tf_op jit(solution)/shard_map/ppermute | solution.py:294
  73.6 7.3 %collective-permute-start.22 = (bf16[256,128]{1,0:T(8,128)(2,1)S(1)}, bf16[256,128]{1,0:T(8,128)(2,1)S(1)}, u32[]{:S(2)}, u32[]{:S(2)}) collective-permute-start(bf16[256,128]{1,0:T(8,128)(2,1)S(1)} %get-tuple-element.56), channel_id=1, source_target_pairs={{0,28},{4,24},{8,20},{12,16},{16,12},{20,8},{24,4},{28,0},{1,29},{... | collective-permute-start | bytes 196616 | tf_op jit(solution)/shard_map/ppermute | solution.py:294

commit v4 on v3

--- a/solution.py
+++ b/solution.py
@@ -38,18 +38,26 @@
 
 def split_kernel(n, rows, kl, rb, group, edge, x_ref, *refs):
     half = n // 2
-    outs, x32 = refs[-n - 1 : -1], refs[-1]
+    outs, held, x32, sem = refs[-n - 3 : -3], refs[-3], refs[-2], refs[-1]
     me = lax.axis_index("ka")
     mirrored = lax.axis_index("row") % 2 == 1
-    x32[0] = x_ref[:, :LANES].astype(F32)
-    x32[1] = x_ref[:, LANES:].astype(F32)
+    size = kl * rows
+    copies = [
+        pltpu.make_async_copy(x_ref.at[pl.ds(p * size, size)], held.at[p], sem.at[p])
+        for p in range(2)
+    ]
+    for c in copies:
+        c.start()
     lane = lax.broadcasted_iota(jnp.int32, (kl, LANES), 1)
     edges = [jnp.zeros((kl, LANES), F32) for _ in range(n * EDGE // LANES)]
-    for s in range(n):
-        h, row = place(me ^ s, half, rb, mirrored)
-        for j in range(rb) if edge else group:
-            for p in range(2):
-                y = x32[h, pl.ds(p * kl * rows + row + j, kl, stride=rows), :]
+    for p in range(2):
+        copies[p].wait()
+        for h in range(2):
+            x32[p, h] = held[p, :, h * LANES : (h + 1) * LANES].astype(F32)
+        for s in range(n):
+            h, row = place(me ^ s, half, rb, mirrored)
+            for j in range(rb) if edge else group:
+                y = x32[p, h, pl.ds(row + j, kl, stride=rows), :]
                 if j in group:
                     slot = group.index(j)
                     outs[s][pl.ds((slot * 2 + p) * kl, kl), :] = y.astype(BF16)
@@ -71,9 +79,13 @@
     return pl.pallas_call(
         functools.partial(split_kernel, n, rows, kl, rb, group, edge),
         out_shape=[jax.ShapeDtypeStruct((size, LANES), BF16)] * n,
-        in_specs=[pl.BlockSpec(memory_space=pltpu.VMEM)]
+        in_specs=[pl.BlockSpec(memory_space=pltpu.HBM)]
         + [pl.BlockSpec(memory_space=pl.ANY)] * len(after),
-        scratch_shapes=[pltpu.VMEM((2, 2 * kl * rows, LANES), F32)],
+        scratch_shapes=[
+            pltpu.VMEM((2, kl * rows, 2 * LANES), BF16),
+            pltpu.VMEM((2, 2, kl * rows, LANES), F32),
+            pltpu.SemaphoreType.DMA((2,)),
+        ],
         compiler_params=params(),
         cost_estimate=pl.CostEstimate(flops=10**6, bytes_accessed=4 * 2**20, transcendentals=0),
         name="split",
@@ -158,15 +170,17 @@
 STEP = 16
 
 
-def box_kernel(n, rb, *refs):
-    above, top = refs[0], refs[1]
-    inside = refs[2] if rb > 2 else None
-    bottom, below = refs[2 + (rb > 2)], refs[3 + (rb > 2)]
-    outs = refs[4 + (rb > 2) :][:n]
-    edge, total, dec = refs[-3:]
-    me = lax.axis_index("ka")
-    h = me // (n // 2)
+def box_kernel(n, rb, far, *refs):
+    half, span, count = n // 2, DEPTH // 2, 4 + (rb > 2)
+    above, top, bottom, below = refs[0], refs[1], refs[count - 2], refs[count - 1]
+    inside = refs[2]
+    outs = refs[count : count + half] if far else refs[count + 1 : count + 1 + half]
+    edge = refs[count + half] if far else refs[count]
+    total, dec = refs[-2:]
+    me = lax.axis_index("ka")
+    h = me // half
     dl = DEPTH // n
+    base = pl.multiple_of((1 - h if far else h) * span, span)
 
     def spectrum(r, z):
         ref = {-1: above, 0: top, rb - 1: bottom, rb: below}.get(r)
@@ -174,37 +188,49 @@
         rows = [ref[w, :] for w in where] if ref is not None else [inside[r - 1, w, :] for w in where]
         return [x.astype(F32) for x in rows]
 
-    lane = lax.broadcasted_iota(jnp.int32, (LANES, LANES), 1)
-    packed = top[4 * DEPTH :, :].astype(F32)
-    up = pltpu.roll(above[4 * DEPTH :, :].astype(F32), LANES - rb, 1)
-    down = pltpu.roll(below[4 * DEPTH :, :].astype(F32), rb, 1)
-    packed = jnp.where(lane % 8 == 0, up, jnp.where(lane % 8 == rb + 1, down, packed))
-    blocks = DEPTH // LANES
-    for b in range(blocks):
-        c = packed if b == 0 else pltpu.roll(packed, LANES - EDGE * b, 1)
-        s = pltpu.roll(packed, LANES - EDGE * (b + blocks), 1)
-        c2, s2 = pltpu.roll(c, LANES - 8, 1), pltpu.roll(s, LANES - 8, 1)
-        for t, v in enumerate(terms(c, s, c2, s2)):
-            v = v + pltpu.roll(v, 1, 1) + pltpu.roll(v, LANES - 1, 1)
-            edge[t, pl.ds(b * LANES + 8, LANES), :] = v
-    for t in range(3):
-        for z in (0, DEPTH + 8):
-            edge[t, pl.ds(z, 8), :] = jnp.zeros((8, LANES), F32)
-            for r in range(rb):
-                total[r, t, pl.ds(z, 8), :] = jnp.zeros((8, LANES), F32)
-
-    @pl.loop(0, DEPTH // STEP, unroll=2)
-    def _(i):
-        z = pl.multiple_of(i * STEP, STEP)
+    def make_edge():
+        lane = lax.broadcasted_iota(jnp.int32, (LANES, LANES), 1)
+        packed = top[4 * DEPTH :, :].astype(F32)
+        up = pltpu.roll(above[4 * DEPTH :, :].astype(F32), LANES - rb, 1)
+        down = pltpu.roll(below[4 * DEPTH :, :].astype(F32), rb, 1)
+        packed = jnp.where(lane % 8 == 0, up, jnp.where(lane % 8 == rb + 1, down, packed))
+        blocks = DEPTH // LANES
+        for b in range(blocks):
+            c = packed if b == 0 else pltpu.roll(packed, LANES - EDGE * b, 1)
+            s = pltpu.roll(packed, LANES - EDGE * (b + blocks), 1)
+            c2, s2 = pltpu.roll(c, LANES - 8, 1), pltpu.roll(s, LANES - 8, 1)
+            for t, v in enumerate(terms(c, s, c2, s2)):
+                v = v + pltpu.roll(v, 1, 1) + pltpu.roll(v, LANES - 1, 1)
+                edge[t, pl.ds(b * LANES + 8, LANES), :] = v
+        for t in range(3):
+            for z in (0, DEPTH + 8):
+                edge[t, pl.ds(z, 8), :] = jnp.zeros((8, LANES), F32)
+
+    if far:
+        make_edge()
+
+    def over_rows(z, at, keep=None):
         before = terms(*spectrum(-1, z))
         here = terms(*spectrum(0, z))
         pair = [x + y for x, y in zip(before, here)]
         for r in range(rb):
             after = terms(*spectrum(r + 1, z))
             for t in range(3):
-                total[r, t, pl.ds(z + 8, STEP), :] = pair[t] + after[t]
+                v = pair[t] + after[t]
+                v = v if keep is None else jnp.where(keep, v, 0.0)
+                total[r, t, pl.ds(at, STEP), :] = v
             pair = [x + y for x, y in zip(here, after)]
             here = after
+
+    @pl.loop(0, span // STEP, unroll=4)
+    def _(i):
+        z = pl.multiple_of(i * STEP, STEP)
+        over_rows(pl.multiple_of(base + z, STEP), pl.multiple_of(z + STEP, STEP))
+
+    z = pl.multiple_of(jnp.maximum(base - STEP, 0), STEP)
+    over_rows(z, 0, base > 0)
+    z = pl.multiple_of(jnp.minimum(base + span, DEPTH - STEP), STEP)
+    over_rows(z, span + STEP, base + span < DEPTH)
 
     lane = lax.broadcasted_iota(jnp.int32, (STEP, LANES), 1)
     not_first, not_last = lane > 0, lane < LANES - 1
@@ -213,69 +239,80 @@
     def deep(x):
         return x[0] + x[1] + x[2]
 
-    @pl.loop(0, DEPTH // STEP, unroll=4)
+    @pl.loop(0, span // STEP, unroll=8)
     def _(i):
         z = pl.multiple_of(i * STEP, STEP)
-        rim = [deep([edge[t, pl.ds(z + j, STEP), :] for j in (7, 8, 9)]) for t in range(3)]
+        rim = [deep([edge[t, pl.ds(base + z + j, STEP), :] for j in (7, 8, 9)]) for t in range(3)]
         for r in range(rb):
             box = []
             for t in range(3):
-                v = deep([total[r, t, pl.ds(z + j, STEP), :] for j in (7, 8, 9)])
+                v = deep([total[r, t, pl.ds(z + STEP + j, STEP), :] for j in (-1, 0, 1)])
                 left = jnp.where(not_first, pltpu.roll(v, 1, 1), 0.0)
                 right = jnp.where(not_last, pltpu.roll(v, LANES - 1, 1), 0.0)
                 e = jnp.where(at_edge, pltpu.roll(rim[t], LANES - 2 - r + h, 1), 0.0)
                 box.append(v + left + right + e)
             square = box[0] * box[0] + box[1] * box[1]
-            d = 1.0 - jnp.sqrt(square) / (box[2] + 1e-05)
+            floor = box[2] + 1e-05
+            scaled = jnp.maximum(square, 1e-27) * (floor * floor)
+            d = 1.0 - square * lax.rsqrt(scaled)
             dec[r, pl.ds(z, STEP), :] = (d * jnp.abs(d) * (d * d)).astype(BF16)
 
-    for s in range(n):
-        z = pl.multiple_of((me ^ s) * dl, dl)
+    for i in range(half):
+        z = pl.multiple_of(((me ^ i) % half) * dl, dl)
         for r in range(rb):
-            outs[s][pl.ds(r * dl, dl), :] = dec[r, pl.ds(z, dl), :]
-
-
-def boxed(rows, n, rb):
-    return pl.pallas_call(
-        functools.partial(box_kernel, n, rb),
-        out_shape=[jax.ShapeDtypeStruct((rb * (DEPTH // n), LANES), BF16)] * n,
+            outs[i][pl.ds(r * dl, dl), :] = dec[r, pl.ds(z, dl), :]
+
+
+def boxed(rows, n, rb, edge=None):
+    far = edge is None
+    return pl.pallas_call(
+        functools.partial(box_kernel, n, rb, far),
+        out_shape=[jax.ShapeDtypeStruct((rb * (DEPTH // n), LANES), BF16)] * (n // 2)
+        + ([jax.ShapeDtypeStruct((3, DEPTH + 16, LANES), F32)] if far else []),
         scratch_shapes=[
-            pltpu.VMEM((3, DEPTH + 16, LANES), F32),
-            pltpu.VMEM((rb, 3, DEPTH + 16, LANES), F32),
-            pltpu.VMEM((rb, DEPTH, LANES), BF16),
+            pltpu.VMEM((rb, 3, DEPTH // 2 + 2 * STEP, LANES), F32),
+            pltpu.VMEM((rb, DEPTH // 2, LANES), BF16),
         ],
         compiler_params=params(),
         cost_estimate=pl.CostEstimate(flops=10**7, bytes_accessed=6 * 2**20, transcendentals=0),
         name="boxed",
-    )(*rows)
-
-
-def join_kernel(n, rows, rb, *refs):
+    )(*rows, *([] if far else [edge]))
+
+
+def join_kernel(n, rows, rb, far, *refs):
     half = n // 2
-    pieces, out, held = refs[:n], refs[n], refs[n + 1]
+    pieces = refs[:half]
     me = lax.axis_index("ka")
     mirrored = lax.axis_index("row") % 2 == 1
     dl = DEPTH // n
-    for s in range(n):
-        h, row = place(me ^ s, half, rb, mirrored)
+    held = refs[-1]
+    for i in range(half):
+        _, row = place(me ^ i, half, rb, mirrored)
         for r in range(rb):
-            coded = pieces[s][pl.ds(r * dl, dl), :].astype(F32)
+            coded = pieces[i][pl.ds(r * dl, dl), :].astype(F32)
             d = jnp.sqrt(jnp.sqrt(jnp.abs(coded)))
             d = jnp.where(coded < 0.0, -d, d)
-            held[h, pl.ds(row + r, dl, stride=rows), :] = d
-    out[:, :LANES] = held[0]
-    out[:, LANES:] = held[1]
-
-
-def join(pieces, n, rows, rb):
-    return pl.pallas_call(
-        functools.partial(join_kernel, n, rows, rb),
-        out_shape=jax.ShapeDtypeStruct((DEPTH // n * rows, 2 * LANES), F32),
-        scratch_shapes=[pltpu.VMEM((2, DEPTH // n * rows, LANES), F32)],
-        compiler_params=params(),
-        cost_estimate=pl.CostEstimate(flops=10**6, bytes_accessed=2 * 2**20, transcendentals=0),
+            held[pl.ds(row + r, dl, stride=rows), :] = d
+    if not far:
+        other, out = refs[half], refs[half + 1]
+        left = me < half
+        out[:, :LANES] = jnp.where(left, held[...], other[...])
+        out[:, LANES:] = jnp.where(left, other[...], held[...])
+
+
+def join(pieces, n, rows, rb, other=None):
+    far = other is None
+    size = DEPTH // n * rows
+    return pl.pallas_call(
+        functools.partial(join_kernel, n, rows, rb, far),
+        out_shape=jax.ShapeDtypeStruct((size, LANES if far else 2 * LANES), F32),
+        scratch_shapes=[] if far else [pltpu.VMEM((size, LANES), F32)],
+        compiler_params=params(),
+        cost_estimate=pl.CostEstimate(
+            flops=1 * 10**9 if far else 10**6, bytes_accessed=2 * 2**20, transcendentals=0
+        ),
         name="join",
-    )(*pieces)
+    )(*pieces, *([] if far else [other]))
 
 
 def body(frames):
@@ -294,7 +331,7 @@
             out[s] = lax.ppermute(pieces[s], "ka", [(i, i ^ s) for i in range(n)])
         return out
 
-    x = frames.reshape(2 * kl * rows, cols)
+    x = pltpu.with_memory_space_constraint(frames.reshape(2 * kl * rows, cols), pltpu.HBM)
     a = exchange(split(x, n, rows, kl, rb, first, True), [*far, *near, *core])
     b = []
     if rest:
@@ -311,8 +348,11 @@
     above = lax.ppermute(bottom, ("ka", "row"), down)
     below = lax.ppermute(top, ("ka", "row"), [(j, i) for i, j in down])
     inside = [inner(b, t, n, kl, rest)] if rest else []
-    pieces = boxed([above, top, *inside, bottom, below], n, rb)
-    out = join(exchange(pieces, [*near, *far, *core]), n, rows, rb)
+    spectra = [above, top, *inside, bottom, below]
+    *away, edge = boxed(spectra, n, rb)
+    pieces = [*boxed(spectra, n, rb, edge), *away]
+    pieces = exchange(pieces, [*far, *near, *core])
+    out = join(pieces[:half], n, rows, rb, join(pieces[half:], n, rows, rb))
     return out.reshape(DEPTH // n, rows, cols)
 
 

time: 84 us -> 79.2 us (0.943); the launches traced: 82.9 us -> 79 us
  starting transfers between devices: 42.3 us -> 36.1 us
  Pallas kernels: 14.1 us -> 16.1 us
  waiting for transfers between devices: 24.8 us -> 26.7 us
  local copies, waits for them, and re-layouts: 1.59 us -> 0.01 us
    ppermute x1, starting transfers between devices: 9.15 us -> 4.74 us  [body(): above = lax.ppermute(bottom, ('ka', 'row'), down)]
    ppermute x1, starting transfers between devices: 5.13 us -> 1.92 us  [body(): below = lax.ppermute(top, ('ka', 'row'), [(j, i) for i, j in down])]
    pallas_call x2, Pallas kernels: 3.61 us -> 5.96 us  [split(): pl.pallas_call(functools.partial(split_kernel, n, rows, kl, rb, group, ed...]
    ppermute x21, waiting for transfers between devices: 24.8 us -> 26.7 us  [exchange(): out[s] = lax.ppermute(pieces[s], 'ka', [(i, i ^ s) for i in range(n)])]
    unnamed x4 -> x2, local copies, waits for them, and re-layouts: 1.59 us -> 0.01 us
    ppermute x21, starting transfers between devices: 28 us -> 29.4 us  [exchange(): out[s] = lax.ppermute(pieces[s], 'ka', [(i, i ^ s) for i in range(n)])]
    pallas_call x2 -> x4, Pallas kernels: 7.35 us -> 6.98 us  [the longest x2 5.04 us: boxed(): pl.pallas_call(functools.partial(box_kernel, n, rb, far), out_shape=[jax....]
  transfers between devices with their start and end apart: 23 -> 23, of which waited for: 7 -> 8; matrix products, arithmetic and copies ran while one was open for 0% -> 0% of each run, Pallas kernels for 5% -> 10%
where the time goes in v4:
time: 79.2 us; the launch traced here: 79 us
  starting transfers between devices  36.1 us (46%)
  waiting for transfers between devices  26.7 us (34%)
  Pallas kernels  16.1 us (20%)
    ppermute x21, starting transfers between devices, exchange(): out[s] = lax.ppermute(pieces[s], 'ka', [(i, i ^ s) for i in range(n)])  29.4 us
    ppermute x21, waiting for transfers between devices, exchange(): out[s] = lax.ppermute(pieces[s], 'ka', [(i, i ^ s) for i in range(n)])  26.7 us
    pallas_call x2, Pallas kernels, split(): pl.pallas_call(functools.partial(split_kernel, n, rows, kl, rb, group, ed...  5.96 us
    pallas_call x2, Pallas kernels, boxed(): pl.pallas_call(functools.partial(box_kernel, n, rb, far), out_shape=[jax....  5.04 us
    ppermute x1, starting transfers between devices, body(): above = lax.ppermute(bottom, ('ka', 'row'), down)  4.74 us
    pallas_call x2, Pallas kernels, join(): pl.pallas_call(functools.partial(join_kernel, n, rows, rb, far), out_shap...  1.94 us
    ppermute x1, starting transfers between devices, body(): below = lax.ppermute(top, ('ka', 'row'), [(j, i) for i, j in down])  1.92 us
    pallas_call x1, Pallas kernels, outer(): pl.pallas_call(functools.partial(outer_kernel, n, kl, first), out_shape=[...  1.87 us
  transfers between devices with their start and end apart: 23, of which 8 were waited for; matrix products, arithmetic and copies ran while one was open for 0% of the time, Pallas kernels for 10%

profile of v4, /device:TPU:1, one launch (start us, length us, event | category | flops | bytes accessed | tf_op | source)
XLA Modules:
  0.0 79.0 jit_solution(13774616269836481641)
XLA Ops:
  0.0 0.0 copy-start
  0.0 3.8 %split.2 = (bf16[528,128]{1,0:T(8,128)(2,1)S(1)}, bf16[528,128]{1,0:T(8,128)(2,1)S(1)}, bf16[528,128]{1,0:T(8,128)(2,1)S(1)}, bf16[528,128]{1,0:T(8,128)(2,1)S(1...) custom-call(bf16[4096,256]{1,0:T(8,128)(2,1)} %bitcast.2), custom_call_target="tpu_custom_call" | custom-call | flops 1000000 | bytes 4194304 | tf_op jit(solution)/shard_map/split/pallas_call | solution.py:79
  3.8 0.1 collective-permute-start
  3.9 4.7 %collective-permute-start.5 = (bf16[528,128]{1,0:T(8,128)(2,1)S(1)}, bf16[528,128]{1,0:T(8,128)(2,1)S(1)}, u32[]{:S(2)}, u32[]{:S(2)}) collective-permute-start(bf16[528,128]{1,0:T(8,128)(2,1)S(1)} %get-tuple-element.38), channel_id=1, source_target_pairs={{0,24},{4,28},{8,16},{12,20},{16,8},{20,12},{24,0},{28,4},{1,25},{... | collective-permute-start | bytes 405512 | tf_op jit(solution)/shard_map/ppermute | solution.py:331
  8.7 0.0 collective-permute-start.1
  8.7 2.0 %collective-permute-start.2 = (bf16[528,128]{1,0:T(8,128)(2,1)S(1)}, bf16[528,128]{1,0:T(8,128)(2,1)S(1)}, u32[]{:S(2)}, u32[]{:S(2)}) collective-permute-start(bf16[528,128]{1,0:T(8,128)(2,1)S(1)} %get-tuple-element.35), channel_id=1, source_target_pairs={{0,12},{4,8},{8,4},{12,0},{16,28},{20,24},{24,20},{28,16},{1,13},{... | collective-permute-start | bytes 405512 | tf_op jit(solution)/shard_map/ppermute | solution.py:331
  10.6 0.0 collective-permute-start.3
  10.6 0.0 collective-permute-done.refs_1_
  10.6 2.4 %collective-permute-start.4 = (bf16[528,128]{1,0:T(8,128)(2,1)S(1)}, bf16[528,128]{1,0:T(8,128)(2,1)S(1)}, u32[]{:S(2)}, u32[]{:S(2)}) collective-permute-start(bf16[528,128]{1,0:T(8,128)(2,1)S(1)} %get-tuple-element.37), channel_id=1, source_target_pairs={{0,20},{4,16},{8,28},{12,24},{16,4},{20,0},{24,12},{28,8},{1,21},{... | collective-permute-start | bytes 405512 | tf_op jit(solution)/shard_map/ppermute | solution.py:331
  13.1 0.0 collective-permute-done.5.refs_6_.refs_0_
  13.1 3.8 %collective-permute-start.6 = (bf16[528,128]{1,0:T(8,128)(2,1)S(1)}, bf16[528,128]{1,0:T(8,128)(2,1)S(1)}, u32[]{:S(2)}, u32[]{:S(2)}) collective-permute-start(bf16[528,128]{1,0:T(8,128)(2,1)S(1)} %get-tuple-element.39), channel_id=1, source_target_pairs={{0,28},{4,24},{8,20},{12,16},{16,12},{20,8},{24,4},{28,0},{1,29},{... | collective-permute-start | bytes 405512 | tf_op jit(solution)/shard_map/ppermute | solution.py:331
  16.8 2.2 %split.3 = (bf16[512,128]{1,0:T(8,128)(2,1)S(1)}, bf16[512,128]{1,0:T(8,128)(2,1)S(1)}, bf16[512,128]{1,0:T(8,128)(2,1)S(1)}, bf16[512,128]{1,0:T(8,128)(2,1)S(1...) custom-call(bf16[4096,256]{1,0:T(8,128)(2,1)} %bitcast.3, ...), custom_call_target="tpu_custom_call" | custom-call | flops 1000000 | bytes 4194304 | tf_op jit(solution)/shard_map/split/pallas_call | solution.py:79
  19.0 0.5 collective-permute-done.1.refs_2_
  19.5 0.5 collective-permute-start.8
  20.1 2.4 %collective-permute-done.2.refs_3_ = bf16[528,128]{1,0:T(8,128)(2,1)S(1)} collective-permute-done((bf16[528,128]{1,0:T(8,128)(2,1)S(1)}, bf16[528,128]{1,0:T(8,128)(2,1)S(1)}, u32[]{:S(2)}, u32[]{:S(2)}) %collective-permute-start.2) | collective-permute-done | bytes 135200 | tf_op jit(solution)/shard_map/ppermute | solution.py:331
  22.5 0.0 collective-permute-start.9
  22.5 0.0 collective-permute-done.3.refs_4_
  22.5 1.9 %collective-permute-start.10 = (bf16[512,128]{1,0:T(8,128)(2,1)S(1)}, bf16[512,128]{1,0:T(8,128)(2,1)S(1)}, u32[]{:S(2)}, u32[]{:S(2)}) collective-permute-start(bf16[512,128]{1,0:T(8,128)(2,1)S(1)} %get-tuple-element.45), channel_id=1, source_target_pairs={{0,12},{4,8},{8,4},{12,0},{16,28},{20,24},{24,20},{28,16},{1,13},{... | collective-permute-start | bytes 393224 | tf_op jit(solution)/shard_map/ppermute | solution.py:331
  24.5 5.1 %collective-permute-done.4.refs_5_ = bf16[528,128]{1,0:T(8,128)(2,1)S(1)} collective-permute-done((bf16[528,128]{1,0:T(8,128)(2,1)S(1)}, bf16[528,128]{1,0:T(8,128)(2,1)S(1)}, u32[]{:S(2)}, u32[]{:S(2)}) %collective-permute-start.4) | collective-permute-done | bytes 135200 | tf_op jit(solution)/shard_map/ppermute | solution.py:331
  29.6 0.0 collective-permute-start.11
  29.6 0.0 collective-permute-done.6.refs_7_
  29.6 0.0 copy-done
  29.6 1.9 %outer.1 = (bf16[2176,128]{1,0:T(8,128)(2,1)S(1)}, bf16[2176,128]{1,0:T(8,128)(2,1)S(1)}) custom-call(bf16[528,128]{1,0:T(8,128)(2,1)S(1)} %get-tuple-element.32.refs_0_, bf16[528,128]{1,0:T(8,128)(2,1)S(1)} %collective-permute-done.refs_1_, bf16[528,128]{1,0:T(8,128)(2,1)S(1)} %collective-permute-done.1.refs_2_, ...), custom_call_target="tpu_custom_call" | custom-call | flops 1610612736 | bytes 4194304 | tf_op jit(solution)/shard_map/outer/pallas_call | solution.py:141
  31.5 4.7 %collective-permute-start.7 = (bf16[2176,128]{1,0:T(8,128)(2,1)S(1)}, bf16[2176,128]{1,0:T(8,128)(2,1)S(1)}, u32[]{:S(2)}, u32[]{:S(2)}) collective-permute-start(bf16[2176,128]{1,0:T(8,128)(2,1)S(1)} %get-tuple-element.40.refs_3_), channel_id=1, source_target_pairs={{0,4},{4,8},{8,12},{12,13},{13,9},{9,5},{5,1},{1,2},{2,6},{6,10},{... | collective-permute-start | bytes 1671176 | tf_op jit(solution)/shard_map/ppermute | solution.py:348
  36.2 0.0 collective-permute-done.8.refs_1_
  36.2 1.9 %collective-permute-start.15 = (bf16[2176,128]{1,0:T(8,128)(2,1)S(1)}, bf16[2176,128]{1,0:T(8,128)(2,1)S(1)}, u32[]{:S(2)}, u32[]{:S(2)}) collective-permute-start(bf16[2176,128]{1,0:T(8,128)(2,1)S(1)} %get-tuple-element.41.refs_1_), channel_id=1, source_target_pairs={{4,0},{8,4},{12,8},{13,12},{9,13},{5,9},{1,5},{2,1},{6,2},{10,6},{... | collective-permute-start | bytes 1671176 | tf_op jit(solution)/shard_map/ppermute | solution.py:349
  38.1 0.0 collective-permute-done.9.refs_2_
  38.2 0.8 collective-permute-start.12
  38.9 0.0 collective-permute-done.10.refs_3_
  38.9 3.1 %collective-permute-start.13 = (bf16[512,128]{1,0:T(8,128)(2,1)S(1)}, bf16[512,128]{1,0:T(8,128)(2,1)S(1)}, u32[]{:S(2)}, u32[]{:S(2)}) collective-permute-start(bf16[512,128]{1,0:T(8,128)(2,1)S(1)} %get-tuple-element.48), channel_id=1, source_target_pairs={{0,24},{4,28},{8,16},{12,20},{16,8},{20,12},{24,0},{28,4},{1,25},{... | collective-permute-start | bytes 393224 | tf_op jit(solution)/shard_map/ppermute | solution.py:331
  42.1 0.0 collective-permute-done.11.refs_4_
  42.1 1.4 %collective-permute-start.14 = (bf16[512,128]{1,0:T(8,128)(2,1)S(1)}, bf16[512,128]{1,0:T(8,128)(2,1)S(1)}, u32[]{:S(2)}, u32[]{:S(2)}) collective-permute-start(bf16[512,128]{1,0:T(8,128)(2,1)S(1)} %get-tuple-element.49), channel_id=1, source_target_pairs={{0,28},{4,24},{8,20},{12,16},{16,12},{20,8},{24,4},{28,0},{1,29},{... | collective-permute-start | bytes 393224 | tf_op jit(solution)/shard_map/ppermute | solution.py:331
  43.5 3.9 %collective-permute-done.12.refs_5_ = bf16[512,128]{1,0:T(8,128)(2,1)S(1)} collective-permute-done((bf16[512,128]{1,0:T(8,128)(2,1)S(1)}, bf16[512,128]{1,0:T(8,128)(2,1)S(1)}, u32[]{:S(2)}, u32[]{:S(2)}) %collective-permute-start.12) | collective-permute-done | bytes 131104 | tf_op jit(solution)/shard_map/ppermute | solution.py:331
  47.4 2.3 %collective-permute-done.13.refs_6_ = bf16[512,128]{1,0:T(8,128)(2,1)S(1)} collective-permute-done((bf16[512,128]{1,0:T(8,128)(2,1)S(1)}, bf16[512,128]{1,0:T(8,128)(2,1)S(1)}, u32[]{:S(2)}, u32[]{:S(2)}) %collective-permute-start.13) | collective-permute-done | bytes 131104 | tf_op jit(solution)/shard_map/ppermute | solution.py:331
  49.7 6.5 %collective-permute-done.14.refs_7_ = bf16[512,128]{1,0:T(8,128)(2,1)S(1)} collective-permute-done((bf16[512,128]{1,0:T(8,128)(2,1)S(1)}, bf16[512,128]{1,0:T(8,128)(2,1)S(1)}, u32[]{:S(2)}, u32[]{:S(2)}) %collective-permute-start.14) | collective-permute-done | bytes 131104 | tf_op jit(solution)/shard_map/ppermute | solution.py:331
  56.2 1.2 %inner.1.refs_2_ = bf16[2,2048,128]{2,1,0:T(8,128)(2,1)S(1)} custom-call(bf16[512,128]{1,0:T(8,128)(2,1)S(1)} %get-tuple-element.42.refs_0_, bf16[512,128]{1,0:T(8,128)(2,1)S(1)} %collective-permute-done.8.refs_1_, bf16[512,128]{1,0:T(8,128)(2,1)S(1)} %collective-permute-done.9.refs_2_, bf16[512,128]{1,0:T(8,128)(2,1)S(1)} %collective-permute-done.10.refs_3_, ...), custom_call_target="tpu_custom_call" | custom-call | flops 4000000000 | bytes 6291456 | tf_op jit(solution)/shard_map/inner/pallas_call | solution.py:161
  57.5 0.0 collective-permute-done.7.refs_0_
  57.5 0.0 collective-permute-done.15.refs_4_
  57.5 3.0 %boxed.2 = (bf16[256,128]{1,0:T(8,128)(2,1)S(1)}, bf16[256,128]{1,0:T(8,128)(2,1)S(1)}, bf16[256,128]{1,0:T(8,128)(2,1)S(1)}, bf16[256,128]{1,0:T(8,128)(2,1)S(1)}, f32[3,528,128]{2,1,0:T(8,128)S(1)}) custom-call(bf16[2176,128]{1,0:T(8,128)(2,1)S(1)} %collective-permute-done.7.refs_0_, bf16[2176,128]{1,0:T(8,128)(2,1)S(1)} %get-tuple-element.41.refs_1_, ...), custom_call_target="tpu_custom_call" | custom-call | flops 10000000 | bytes 6291456 | tf_op jit(solution)/shard_map/boxed/pallas_call | solution.py:268
  60.5 2.9 %collective-permute-start.19 = (bf16[256,128]{1,0:T(8,128)(2,1)S(1)}, bf16[256,128]{1,0:T(8,128)(2,1)S(1)}, u32[]{:S(2)}, u32[]{:S(2)}) collective-permute-start(bf16[256,128]{1,0:T(8,128)(2,1)S(1)} %get-tuple-element.55), channel_id=1, source_target_pairs={{0,16},{4,20},{8,24},{12,28},{16,0},{20,4},{24,8},{28,12},{1,17},{... | collective-permute-start | bytes 196616 | tf_op jit(solution)/shard_map/ppermute | solution.py:331
  63.4 0.9 %collective-permute-start.20 = (bf16[256,128]{1,0:T(8,128)(2,1)S(1)}, bf16[256,128]{1,0:T(8,128)(2,1)S(1)}, u32[]{:S(2)}, u32[]{:S(2)}) collective-permute-start(bf16[256,128]{1,0:T(8,128)(2,1)S(1)} %get-tuple-element.56), channel_id=1, source_target_pairs={{0,20},{4,16},{8,28},{12,24},{16,4},{20,0},{24,12},{28,8},{1,21},{... | collective-permute-start | bytes 196616 | tf_op jit(solution)/shard_map/ppermute | solution.py:331
  64.3 0.1 collective-permute-start.21
  64.4 3.6 %collective-permute-start.22 = (bf16[256,128]{1,0:T(8,128)(2,1)S(1)}, bf16[256,128]{1,0:T(8,128)(2,1)S(1)}, u32[]{:S(2)}, u32[]{:S(2)}) collective-permute-start(bf16[256,128]{1,0:T(8,128)(2,1)S(1)} %get-tuple-element.58), channel_id=1, source_target_pairs={{0,28},{4,24},{8,20},{12,16},{16,12},{20,8},{24,4},{28,0},{1,29},{... | collective-permute-start | bytes 196616 | tf_op jit(solution)/shard_map/ppermute | solution.py:331
  68.1 2.0 %boxed.3 = (bf16[256,128]{1,0:T(8,128)(2,1)S(1)}, bf16[256,128]{1,0:T(8,128)(2,1)S(1)}, bf16[256,128]{1,0:T(8,128)(2,1)S(1)}, bf16[256,128]{1,0:T(8,128)(2,1)S(1)}) custom-call(bf16[2176,128]{1,0:T(8,128)(2,1)S(1)} %collective-permute-done.7.refs_0_, bf16[2176,128]{1,0:T(8,128)(2,1)S(1)} %get-tuple-element.41.refs_1_, ...), custom_call_target="tpu_custom_call" | custom-call | flops 10000000 | bytes 6291456 | tf_op jit(solution)/shard_map/boxed/pallas_call | solution.py:268
  70.1 0.1 collective-permute-start.16
  70.2 0.0 collective-permute-done.19.refs_0_
  70.2 0.1 collective-permute-start.17
  70.3 3.3 %collective-permute-done.20.refs_1_ = bf16[256,128]{1,0:T(8,128)(2,1)S(1)} collective-permute-done((bf16[256,128]{1,0:T(8,128)(2,1)S(1)}, bf16[256,128]{1,0:T(8,128)(2,1)S(1)}, u32[]{:S(2)}, u32[]{:S(2)}) %collective-permute-start.20) | collective-permute-done | bytes 65568 | tf_op jit(solution)/shard_map/ppermute | solution.py:331
  73.6 0.9 %collective-permute-start.18 = (bf16[256,128]{1,0:T(8,128)(2,1)S(1)}, bf16[256,128]{1,0:T(8,128)(2,1)S(1)}, u32[]{:S(2)}, u32[]{:S(2)}) collective-permute-start(bf16[256,128]{1,0:T(8,128)(2,1)S(1)} %get-tuple-element.54), channel_id=1, source_target_pairs={{0,12},{4,8},{8,4},{12,0},{16,28},{20,24},{24,20},{28,16},{1,13},{... | collective-permute-start | bytes 196616 | tf_op jit(solution)/shard_map/ppermute | solution.py:331
  74.5 0.0 collective-permute-done.21.refs_2_
  74.5 0.0 collective-permute-done.22.refs_3_
  74.5 0.4 join.2.refs_4_
  74.9 0.0 collective-permute-done.16.refs_1_
  74.9 0.0 collective-permute-done.17.refs_2_
  74.9 2.5 %collective-permute-done.18.refs_3_ = bf16[256,128]{1,0:T(8,128)(2,1)S(1)} collective-permute-done((bf16[256,128]{1,0:T(8,128)(2,1)S(1)}, bf16[256,128]{1,0:T(8,128)(2,1)S(1)}, u32[]{:S(2)}, u32[]{:S(2)}) %collective-permute-start.18) | collective-permute-done | bytes 65568 | tf_op jit(solution)/shard_map/ppermute | solution.py:331
  77.5 1.5 %join.3 = f32[1024,256]{1,0:T(8,128)} custom-call(bf16[256,128]{1,0:T(8,128)(2,1)S(1)} %get-tuple-element.51.refs_0_, bf16[256,128]{1,0:T(8,128)(2,1)S(1)} %collective-permute-done.16.refs_1_, bf16[256,128]{1,0:T(8,128)(2,1)S(1)} %collective-permute-done.17.refs_2_, bf16[256,128]{1,0:T(8,128)(2,1)S(1)} %collective-permute-done.18.refs_3_, ...), custom_call_target="tpu_custom_call" | custom-call | flops 1000000 | bytes 2097152 | tf_op jit(solution)/shard_map/join/pallas_call | solution.py:306
Async XLA Ops:
  0.0 29.6 %copy-start = (bf16[8,1024,128]{2,1,0:T(8,128)(2,1)S(1)}, bf16[8,1024,128]{2,1,0:T(8,128)(2,1)}, u32[]{:S(2)}) copy-start(bf16[8,1024,128]{2,1,0:T(8,128)(2,1)} %constant.2.clone.refs_8_) | copy-start | bytes 6291460
  3.8 6.8 %collective-permute-start = (bf16[528,128]{1,0:T(8,128)(2,1)S(1)}, bf16[528,128]{1,0:T(8,128)(2,1)S(1)}, u32[]{:S(2)}, u32[]{:S(2)}) collective-permute-start(bf16[528,128]{1,0:T(8,128)(2,1)S(1)} %get-tuple-element.33), channel_id=1, source_target_pairs={{0,4},{4,0},{8,12},{12,8},{16,20},{20,16},{24,28},{28,24},{1,5},{5... | collective-permute-start | bytes 405512 | tf_op jit(solution)/shard_map/ppermute | solution.py:331
  3.9 9.1 %collective-permute-start.5 = (bf16[528,128]{1,0:T(8,128)(2,1)S(1)}, bf16[528,128]{1,0:T(8,128)(2,1)S(1)}, u32[]{:S(2)}, u32[]{:S(2)}) collective-permute-start(bf16[528,128]{1,0:T(8,128)(2,1)S(1)} %get-tuple-element.38), channel_id=1, source_target_pairs={{0,24},{4,28},{8,16},{12,20},{16,8},{20,12},{24,0},{28,4},{1,25},{... | collective-permute-start | bytes 405512 | tf_op jit(solution)/shard_map/ppermute | solution.py:331
  8.7 10.9 %collective-permute-start.1 = (bf16[528,128]{1,0:T(8,128)(2,1)S(1)}, bf16[528,128]{1,0:T(8,128)(2,1)S(1)}, u32[]{:S(2)}, u32[]{:S(2)}) collective-permute-start(bf16[528,128]{1,0:T(8,128)(2,1)S(1)} %get-tuple-element.34), channel_id=1, source_target_pairs={{0,8},{4,12},{8,0},{12,4},{16,24},{20,28},{24,16},{28,20},{1,9},{5... | collective-permute-start | bytes 405512 | tf_op jit(solution)/shard_map/ppermute | solution.py:331
  8.7 13.8 %collective-permute-start.2 = (bf16[528,128]{1,0:T(8,128)(2,1)S(1)}, bf16[528,128]{1,0:T(8,128)(2,1)S(1)}, u32[]{:S(2)}, u32[]{:S(2)}) collective-permute-start(bf16[528,128]{1,0:T(8,128)(2,1)S(1)} %get-tuple-element.35), channel_id=1, source_target_pairs={{0,12},{4,8},{8,4},{12,0},{16,28},{20,24},{24,20},{28,16},{1,13},{... | collective-permute-start | bytes 405512 | tf_op jit(solution)/shard_map/ppermute | solution.py:331
  10.6 11.9 %collective-permute-start.3 = (bf16[528,128]{1,0:T(8,128)(2,1)S(1)}, bf16[528,128]{1,0:T(8,128)(2,1)S(1)}, u32[]{:S(2)}, u32[]{:S(2)}) collective-permute-start(bf16[528,128]{1,0:T(8,128)(2,1)S(1)} %get-tuple-element.36), channel_id=1, source_target_pairs={{0,16},{4,20},{8,24},{12,28},{16,0},{20,4},{24,8},{28,12},{1,17},{... | collective-permute-start | bytes 405512 | tf_op jit(solution)/shard_map/ppermute | solution.py:331
  10.6 18.9 %collective-permute-start.4 = (bf16[528,128]{1,0:T(8,128)(2,1)S(1)}, bf16[528,128]{1,0:T(8,128)(2,1)S(1)}, u32[]{:S(2)}, u32[]{:S(2)}) collective-permute-start(bf16[528,128]{1,0:T(8,128)(2,1)S(1)} %get-tuple-element.37), channel_id=1, source_target_pairs={{0,20},{4,16},{8,28},{12,24},{16,4},{20,0},{24,12},{28,8},{1,21},{... | collective-permute-start | bytes 405512 | tf_op jit(solution)/shard_map/ppermute | solution.py:331
  13.1 16.5 %collective-permute-start.6 = (bf16[528,128]{1,0:T(8,128)(2,1)S(1)}, bf16[528,128]{1,0:T(8,128)(2,1)S(1)}, u32[]{:S(2)}, u32[]{:S(2)}) collective-permute-start(bf16[528,128]{1,0:T(8,128)(2,1)S(1)} %get-tuple-element.39), channel_id=1, source_target_pairs={{0,28},{4,24},{8,20},{12,16},{16,12},{20,8},{24,4},{28,0},{1,29},{... | collective-permute-start | bytes 405512 | tf_op jit(solution)/shard_map/ppermute | solution.py:331
  19.5 16.7 %collective-permute-start.8 = (bf16[512,128]{1,0:T(8,128)(2,1)S(1)}, bf16[512,128]{1,0:T(8,128)(2,1)S(1)}, u32[]{:S(2)}, u32[]{:S(2)}) collective-permute-start(bf16[512,128]{1,0:T(8,128)(2,1)S(1)} %get-tuple-element.43), channel_id=1, source_target_pairs={{0,4},{4,0},{8,12},{12,8},{16,20},{20,16},{24,28},{28,24},{1,5},{5... | collective-permute-start | bytes 393224 | tf_op jit(solution)/shard_map/ppermute | solution.py:331
  22.5 15.6 %collective-permute-start.9 = (bf16[512,128]{1,0:T(8,128)(2,1)S(1)}, bf16[512,128]{1,0:T(8,128)(2,1)S(1)}, u32[]{:S(2)}, u32[]{:S(2)}) collective-permute-start(bf16[512,128]{1,0:T(8,128)(2,1)S(1)} %get-tuple-element.44), channel_id=1, source_target_pairs={{0,8},{4,12},{8,0},{12,4},{16,24},{20,28},{24,16},{28,20},{1,9},{5... | collective-permute-start | bytes 393224 | tf_op jit(solution)/shard_map/ppermute | solution.py:331
  22.5 16.4 %collective-permute-start.10 = (bf16[512,128]{1,0:T(8,128)(2,1)S(1)}, bf16[512,128]{1,0:T(8,128)(2,1)S(1)}, u32[]{:S(2)}, u32[]{:S(2)}) collective-permute-start(bf16[512,128]{1,0:T(8,128)(2,1)S(1)} %get-tuple-element.45), channel_id=1, source_target_pairs={{0,12},{4,8},{8,4},{12,0},{16,28},{20,24},{24,20},{28,16},{1,13},{... | collective-permute-start | bytes 393224 | tf_op jit(solution)/shard_map/ppermute | solution.py:331
  29.6 12.5 %collective-permute-start.11 = (bf16[512,128]{1,0:T(8,128)(2,1)S(1)}, bf16[512,128]{1,0:T(8,128)(2,1)S(1)}, u32[]{:S(2)}, u32[]{:S(2)}) collective-permute-start(bf16[512,128]{1,0:T(8,128)(2,1)S(1)} %get-tuple-element.46), channel_id=1, source_target_pairs={{0,16},{4,20},{8,24},{12,28},{16,0},{20,4},{24,8},{28,12},{1,17},{... | collective-permute-start | bytes 393224 | tf_op jit(solution)/shard_map/ppermute | solution.py:331
  31.5 26.0 %collective-permute-start.7 = (bf16[2176,128]{1,0:T(8,128)(2,1)S(1)}, bf16[2176,128]{1,0:T(8,128)(2,1)S(1)}, u32[]{:S(2)}, u32[]{:S(2)}) collective-permute-start(bf16[2176,128]{1,0:T(8,128)(2,1)S(1)} %get-tuple-element.40.refs_3_), channel_id=1, source_target_pairs={{0,4},{4,8},{8,12},{12,13},{13,9},{9,5},{5,1},{1,2},{2,6},{6,10},{... | collective-permute-start | bytes 1671176 | tf_op jit(solution)/shard_map/ppermute | solution.py:348
  36.2 21.3 %collective-permute-start.15 = (bf16[2176,128]{1,0:T(8,128)(2,1)S(1)}, bf16[2176,128]{1,0:T(8,128)(2,1)S(1)}, u32[]{:S(2)}, u32[]{:S(2)}) collective-permute-start(bf16[2176,128]{1,0:T(8,128)(2,1)S(1)} %get-tuple-element.41.refs_1_), channel_id=1, source_target_pairs={{4,0},{8,4},{12,8},{13,12},{9,13},{5,9},{1,5},{2,1},{6,2},{10,6},{... | collective-permute-start | bytes 1671176 | tf_op jit(solution)/shard_map/ppermute | solution.py:349
  38.2 9.2 %collective-permute-start.12 = (bf16[512,128]{1,0:T(8,128)(2,1)S(1)}, bf16[512,128]{1,0:T(8,128)(2,1)S(1)}, u32[]{:S(2)}, u32[]{:S(2)}) collective-permute-start(bf16[512,128]{1,0:T(8,128)(2,1)S(1)} %get-tuple-element.47), channel_id=1, source_target_pairs={{0,20},{4,16},{8,28},{12,24},{16,4},{20,0},{24,12},{28,8},{1,21},{... | collective-permute-start | bytes 393224 | tf_op jit(solution)/shard_map/ppermute | solution.py:331
  38.9 10.8 %collective-permute-start.13 = (bf16[512,128]{1,0:T(8,128)(2,1)S(1)}, bf16[512,128]{1,0:T(8,128)(2,1)S(1)}, u32[]{:S(2)}, u32[]{:S(2)}) collective-permute-start(bf16[512,128]{1,0:T(8,128)(2,1)S(1)} %get-tuple-element.48), channel_id=1, source_target_pairs={{0,24},{4,28},{8,16},{12,20},{16,8},{20,12},{24,0},{28,4},{1,25},{... | collective-permute-start | bytes 393224 | tf_op jit(solution)/shard_map/ppermute | solution.py:331
  42.1 14.2 %collective-permute-start.14 = (bf16[512,128]{1,0:T(8,128)(2,1)S(1)}, bf16[512,128]{1,0:T(8,128)(2,1)S(1)}, u32[]{:S(2)}, u32[]{:S(2)}) collective-permute-start(bf16[512,128]{1,0:T(8,128)(2,1)S(1)} %get-tuple-element.49), channel_id=1, source_target_pairs={{0,28},{4,24},{8,20},{12,16},{16,12},{20,8},{24,4},{28,0},{1,29},{... | collective-permute-start | bytes 393224 | tf_op jit(solution)/shard_map/ppermute | solution.py:331
  60.5 9.6 %collective-permute-start.19 = (bf16[256,128]{1,0:T(8,128)(2,1)S(1)}, bf16[256,128]{1,0:T(8,128)(2,1)S(1)}, u32[]{:S(2)}, u32[]{:S(2)}) collective-permute-start(bf16[256,128]{1,0:T(8,128)(2,1)S(1)} %get-tuple-element.55), channel_id=1, source_target_pairs={{0,16},{4,20},{8,24},{12,28},{16,0},{20,4},{24,8},{28,12},{1,17},{... | collective-permute-start | bytes 196616 | tf_op jit(solution)/shard_map/ppermute | solution.py:331
  63.4 10.2 %collective-permute-start.20 = (bf16[256,128]{1,0:T(8,128)(2,1)S(1)}, bf16[256,128]{1,0:T(8,128)(2,1)S(1)}, u32[]{:S(2)}, u32[]{:S(2)}) collective-permute-start(bf16[256,128]{1,0:T(8,128)(2,1)S(1)} %get-tuple-element.56), channel_id=1, source_target_pairs={{0,20},{4,16},{8,28},{12,24},{16,4},{20,0},{24,12},{28,8},{1,21},{... | collective-permute-start | bytes 196616 | tf_op jit(solution)/shard_map/ppermute | solution.py:331
  64.3 10.2 %collective-permute-start.21 = (bf16[256,128]{1,0:T(8,128)(2,1)S(1)}, bf16[256,128]{1,0:T(8,128)(2,1)S(1)}, u32[]{:S(2)}, u32[]{:S(2)}) collective-permute-start(bf16[256,128]{1,0:T(8,128)(2,1)S(1)} %get-tuple-element.57), channel_id=1, source_target_pairs={{0,24},{4,28},{8,16},{12,20},{16,8},{20,12},{24,0},{28,4},{1,25},{... | collective-permute-start | bytes 196616 | tf_op jit(solution)/shard_map/ppermute | solution.py:331
  64.4 10.1 %collective-permute-start.22 = (bf16[256,128]{1,0:T(8,128)(2,1)S(1)}, bf16[256,128]{1,0:T(8,128)(2,1)S(1)}, u32[]{:S(2)}, u32[]{:S(2)}) collective-permute-start(bf16[256,128]{1,0:T(8,128)(2,1)S(1)} %get-tuple-element.58), channel_id=1, source_target_pairs={{0,28},{4,24},{8,20},{12,16},{16,12},{20,8},{24,4},{28,0},{1,29},{... | collective-permute-start | bytes 196616 | tf_op jit(solution)/shard_map/ppermute | solution.py:331
  70.1 4.8 %collective-permute-start.16 = (bf16[256,128]{1,0:T(8,128)(2,1)S(1)}, bf16[256,128]{1,0:T(8,128)(2,1)S(1)}, u32[]{:S(2)}, u32[]{:S(2)}) collective-permute-start(bf16[256,128]{1,0:T(8,128)(2,1)S(1)} %get-tuple-element.52), channel_id=1, source_target_pairs={{0,4},{4,0},{8,12},{12,8},{16,20},{20,16},{24,28},{28,24},{1,5},{5... | collective-permute-start | bytes 196616 | tf_op jit(solution)/shard_map/ppermute | solution.py:331
  70.2 4.7 %collective-permute-start.17 = (bf16[256,128]{1,0:T(8,128)(2,1)S(1)}, bf16[256,128]{1,0:T(8,128)(2,1)S(1)}, u32[]{:S(2)}, u32[]{:S(2)}) collective-permute-start(bf16[256,128]{1,0:T(8,128)(2,1)S(1)} %get-tuple-element.53), channel_id=1, source_target_pairs={{0,8},{4,12},{8,0},{12,4},{16,24},{20,28},{24,16},{28,20},{1,9},{5... | collective-permute-start | bytes 196616 | tf_op jit(solution)/shard_map/ppermute | solution.py:331
  73.6 3.9 %collective-permute-start.18 = (bf16[256,128]{1,0:T(8,128)(2,1)S(1)}, bf16[256,128]{1,0:T(8,128)(2,1)S(1)}, u32[]{:S(2)}, u32[]{:S(2)}) collective-permute-start(bf16[256,128]{1,0:T(8,128)(2,1)S(1)} %get-tuple-element.54), channel_id=1, source_target_pairs={{0,12},{4,8},{8,4},{12,0},{16,28},{20,24},{24,20},{28,16},{1,13},{... | collective-permute-start | bytes 196616 | tf_op jit(solution)/shard_map/ppermute | solution.py:331

commit v5 on v4

--- a/solution.py
+++ b/solution.py
@@ -195,13 +195,13 @@
         down = pltpu.roll(below[4 * DEPTH :, :].astype(F32), rb, 1)
         packed = jnp.where(lane % 8 == 0, up, jnp.where(lane % 8 == rb + 1, down, packed))
         blocks = DEPTH // LANES
-        for b in range(blocks):
-            c = packed if b == 0 else pltpu.roll(packed, LANES - EDGE * b, 1)
-            s = pltpu.roll(packed, LANES - EDGE * (b + blocks), 1)
-            c2, s2 = pltpu.roll(c, LANES - 8, 1), pltpu.roll(s, LANES - 8, 1)
-            for t, v in enumerate(terms(c, s, c2, s2)):
-                v = v + pltpu.roll(v, 1, 1) + pltpu.roll(v, LANES - 1, 1)
-                edge[t, pl.ds(b * LANES + 8, LANES), :] = v
+        sines = pltpu.roll(packed, LANES - EDGE * blocks, 1)
+        second = [pltpu.roll(x, LANES - 8, 1) for x in (packed, sines)]
+        for t, v in enumerate(terms(packed, sines, *second)):
+            v = v + pltpu.roll(v, 1, 1) + pltpu.roll(v, LANES - 1, 1)
+            for b in range(blocks):
+                turned = pltpu.roll(v, LANES - EDGE * b, 1) if b else v
+                edge[t, pl.ds(b * LANES + 8, LANES), :] = turned
         for t in range(3):
             for z in (0, DEPTH + 8):
                 edge[t, pl.ds(z, 8), :] = jnp.zeros((8, LANES), F32)
@@ -282,10 +282,10 @@
 def join_kernel(n, rows, rb, far, *refs):
     half = n // 2
     pieces = refs[:half]
+    out, held, sem = refs[-3:]
     me = lax.axis_index("ka")
     mirrored = lax.axis_index("row") % 2 == 1
     dl = DEPTH // n
-    held = refs[-1]
     for i in range(half):
         _, row = place(me ^ i, half, rb, mirrored)
         for r in range(rb):
@@ -293,23 +293,27 @@
             d = jnp.sqrt(jnp.sqrt(jnp.abs(coded)))
             d = jnp.where(coded < 0.0, -d, d)
             held[pl.ds(row + r, dl, stride=rows), :] = d
-    if not far:
-        other, out = refs[half], refs[half + 1]
-        left = me < half
-        out[:, :LANES] = jnp.where(left, held[...], other[...])
-        out[:, LANES:] = jnp.where(left, other[...], held[...])
+    h = me // half
+    column = pl.multiple_of((1 - h if far else h) * LANES, LANES)
+    copy = pltpu.make_async_copy(held, out.at[:, pl.ds(column, LANES)], sem)
+    copy.start()
+    copy.wait()
 
 
 def join(pieces, n, rows, rb, other=None):
     far = other is None
-    size = DEPTH // n * rows
+    half, size = n // 2, DEPTH // n * rows
     return pl.pallas_call(
         functools.partial(join_kernel, n, rows, rb, far),
-        out_shape=jax.ShapeDtypeStruct((size, LANES if far else 2 * LANES), F32),
-        scratch_shapes=[] if far else [pltpu.VMEM((size, LANES), F32)],
+        out_shape=jax.ShapeDtypeStruct((size, 2 * LANES), F32),
+        in_specs=[pl.BlockSpec(memory_space=pltpu.VMEM)] * half
+        + ([] if far else [pl.BlockSpec(memory_space=pltpu.HBM)]),
+        out_specs=pl.BlockSpec(memory_space=pltpu.HBM),
+        input_output_aliases={} if far else {half: 0},
+        scratch_shapes=[pltpu.VMEM((size, LANES), F32), pltpu.SemaphoreType.DMA],
         compiler_params=params(),
         cost_estimate=pl.CostEstimate(
-            flops=1 * 10**9 if far else 10**6, bytes_accessed=2 * 2**20, transcendentals=0
+            flops=10**9 if far else 10**6, bytes_accessed=2 * 2**20, transcendentals=0
         ),
         name="join",
     )(*pieces, *([] if far else [other]))

time: 79.2 us -> 78.4 us (0.990)
  waiting for transfers between devices: 26.7 us -> 25.9 us
    ppermute x21, waiting for transfers between devices: 26.7 us -> 25.9 us  [exchange(): out[s] = lax.ppermute(pieces[s], 'ka', [(i, i ^ s) for i in range(n)])]
  transfers between devices with their start and end apart: 23 -> 23, of which waited for: 8 -> 8; matrix products, arithmetic and copies ran while one was open for 0% -> 0% of each run, Pallas kernels for 10% -> 11%
where the time goes in v5:
time: 78.4 us; the launch traced here: 78.2 us
  starting transfers between devices  36.1 us (46%)
  waiting for transfers between devices  25.9 us (33%)
  Pallas kernels  16.1 us (21%)
    ppermute x21, starting transfers between devices, exchange(): out[s] = lax.ppermute(pieces[s], 'ka', [(i, i ^ s) for i in range(n)])  29.4 us
    ppermute x21, waiting for transfers between devices, exchange(): out[s] = lax.ppermute(pieces[s], 'ka', [(i, i ^ s) for i in range(n)])  25.9 us
    pallas_call x2, Pallas kernels, split(): pl.pallas_call(functools.partial(split_kernel, n, rows, kl, rb, group, ed...  5.96 us
    ppermute x1, starting transfers between devices, body(): above = lax.ppermute(bottom, ('ka', 'row'), down)  4.74 us
    pallas_call x2, Pallas kernels, boxed(): pl.pallas_call(functools.partial(box_kernel, n, rb, far), out_shape=[jax....  4.58 us
    pallas_call x2, Pallas kernels, join(): pl.pallas_call(functools.partial(join_kernel, n, rows, rb, far), out_shap...  2.39 us
    ppermute x1, starting transfers between devices, body(): below = lax.ppermute(top, ('ka', 'row'), [(j, i) for i, j in down])  1.92 us
    pallas_call x1, Pallas kernels, outer(): pl.pallas_call(functools.partial(outer_kernel, n, kl, first), out_shape=[...  1.87 us
  transfers between devices with their start and end apart: 23, of which 8 were waited for; matrix products, arithmetic and copies ran while one was open for 0% of the time, Pallas kernels for 11%

profile of v5, /device:TPU:1, one launch (start us, length us, event | category | flops | bytes accessed | tf_op | source)
XLA Modules:
  0.0 78.2 jit_solution(12955030129583463310)
XLA Ops:
  0.0 0.0 copy-start
  0.0 3.8 %split.2 = (bf16[528,128]{1,0:T(8,128)(2,1)S(1)}, bf16[528,128]{1,0:T(8,128)(2,1)S(1)}, bf16[528,128]{1,0:T(8,128)(2,1)S(1)}, bf16[528,128]{1,0:T(8,128)(2,1)S(1...) custom-call(bf16[4096,256]{1,0:T(8,128)(2,1)} %bitcast.2), custom_call_target="tpu_custom_call" | custom-call | flops 1000000 | bytes 4194304 | tf_op jit(solution)/shard_map/split/pallas_call | solution.py:79
  3.8 0.1 collective-permute-start
  3.9 4.7 %collective-permute-start.5 = (bf16[528,128]{1,0:T(8,128)(2,1)S(1)}, bf16[528,128]{1,0:T(8,128)(2,1)S(1)}, u32[]{:S(2)}, u32[]{:S(2)}) collective-permute-start(bf16[528,128]{1,0:T(8,128)(2,1)S(1)} %get-tuple-element.38), channel_id=1, source_target_pairs={{0,24},{4,28},{8,16},{12,20},{16,8},{20,12},{24,0},{28,4},{1,25},{... | collective-permute-start | bytes 405512 | tf_op jit(solution)/shard_map/ppermute | solution.py:335
  8.7 0.0 collective-permute-start.1
  8.7 2.0 %collective-permute-start.2 = (bf16[528,128]{1,0:T(8,128)(2,1)S(1)}, bf16[528,128]{1,0:T(8,128)(2,1)S(1)}, u32[]{:S(2)}, u32[]{:S(2)}) collective-permute-start(bf16[528,128]{1,0:T(8,128)(2,1)S(1)} %get-tuple-element.35), channel_id=1, source_target_pairs={{0,12},{4,8},{8,4},{12,0},{16,28},{20,24},{24,20},{28,16},{1,13},{... | collective-permute-start | bytes 405512 | tf_op jit(solution)/shard_map/ppermute | solution.py:335
  10.6 0.0 collective-permute-start.3
  10.6 0.0 collective-permute-done.refs_1_
  10.6 2.4 %collective-permute-start.4 = (bf16[528,128]{1,0:T(8,128)(2,1)S(1)}, bf16[528,128]{1,0:T(8,128)(2,1)S(1)}, u32[]{:S(2)}, u32[]{:S(2)}) collective-permute-start(bf16[528,128]{1,0:T(8,128)(2,1)S(1)} %get-tuple-element.37), channel_id=1, source_target_pairs={{0,20},{4,16},{8,28},{12,24},{16,4},{20,0},{24,12},{28,8},{1,21},{... | collective-permute-start | bytes 405512 | tf_op jit(solution)/shard_map/ppermute | solution.py:335
  13.1 0.0 collective-permute-done.5.refs_6_.refs_0_
  13.1 3.8 %collective-permute-start.6 = (bf16[528,128]{1,0:T(8,128)(2,1)S(1)}, bf16[528,128]{1,0:T(8,128)(2,1)S(1)}, u32[]{:S(2)}, u32[]{:S(2)}) collective-permute-start(bf16[528,128]{1,0:T(8,128)(2,1)S(1)} %get-tuple-element.39), channel_id=1, source_target_pairs={{0,28},{4,24},{8,20},{12,16},{16,12},{20,8},{24,4},{28,0},{1,29},{... | collective-permute-start | bytes 405512 | tf_op jit(solution)/shard_map/ppermute | solution.py:335
  16.8 2.2 %split.3 = (bf16[512,128]{1,0:T(8,128)(2,1)S(1)}, bf16[512,128]{1,0:T(8,128)(2,1)S(1)}, bf16[512,128]{1,0:T(8,128)(2,1)S(1)}, bf16[512,128]{1,0:T(8,128)(2,1)S(1...) custom-call(bf16[4096,256]{1,0:T(8,128)(2,1)} %bitcast.3, ...), custom_call_target="tpu_custom_call" | custom-call | flops 1000000 | bytes 4194304 | tf_op jit(solution)/shard_map/split/pallas_call | solution.py:79
  19.0 0.5 collective-permute-done.1.refs_2_
  19.5 0.5 collective-permute-start.8
  20.1 2.4 %collective-permute-done.2.refs_3_ = bf16[528,128]{1,0:T(8,128)(2,1)S(1)} collective-permute-done((bf16[528,128]{1,0:T(8,128)(2,1)S(1)}, bf16[528,128]{1,0:T(8,128)(2,1)S(1)}, u32[]{:S(2)}, u32[]{:S(2)}) %collective-permute-start.2) | collective-permute-done | bytes 135200 | tf_op jit(solution)/shard_map/ppermute | solution.py:335
  22.5 0.0 collective-permute-start.9
  22.5 0.0 collective-permute-done.3.refs_4_
  22.5 1.9 %collective-permute-start.10 = (bf16[512,128]{1,0:T(8,128)(2,1)S(1)}, bf16[512,128]{1,0:T(8,128)(2,1)S(1)}, u32[]{:S(2)}, u32[]{:S(2)}) collective-permute-start(bf16[512,128]{1,0:T(8,128)(2,1)S(1)} %get-tuple-element.45), channel_id=1, source_target_pairs={{0,12},{4,8},{8,4},{12,0},{16,28},{20,24},{24,20},{28,16},{1,13},{... | collective-permute-start | bytes 393224 | tf_op jit(solution)/shard_map/ppermute | solution.py:335
  24.5 5.1 %collective-permute-done.4.refs_5_ = bf16[528,128]{1,0:T(8,128)(2,1)S(1)} collective-permute-done((bf16[528,128]{1,0:T(8,128)(2,1)S(1)}, bf16[528,128]{1,0:T(8,128)(2,1)S(1)}, u32[]{:S(2)}, u32[]{:S(2)}) %collective-permute-start.4) | collective-permute-done | bytes 135200 | tf_op jit(solution)/shard_map/ppermute | solution.py:335
  29.6 0.0 collective-permute-start.11
  29.6 0.0 collective-permute-done.6.refs_7_
  29.6 0.0 copy-done
  29.6 1.9 %outer.1 = (bf16[2176,128]{1,0:T(8,128)(2,1)S(1)}, bf16[2176,128]{1,0:T(8,128)(2,1)S(1)}) custom-call(bf16[528,128]{1,0:T(8,128)(2,1)S(1)} %get-tuple-element.32.refs_0_, bf16[528,128]{1,0:T(8,128)(2,1)S(1)} %collective-permute-done.refs_1_, bf16[528,128]{1,0:T(8,128)(2,1)S(1)} %collective-permute-done.1.refs_2_, ...), custom_call_target="tpu_custom_call" | custom-call | flops 1610612736 | bytes 4194304 | tf_op jit(solution)/shard_map/outer/pallas_call | solution.py:141
  31.5 4.7 %collective-permute-start.7 = (bf16[2176,128]{1,0:T(8,128)(2,1)S(1)}, bf16[2176,128]{1,0:T(8,128)(2,1)S(1)}, u32[]{:S(2)}, u32[]{:S(2)}) collective-permute-start(bf16[2176,128]{1,0:T(8,128)(2,1)S(1)} %get-tuple-element.40.refs_3_), channel_id=1, source_target_pairs={{0,4},{4,8},{8,12},{12,13},{13,9},{9,5},{5,1},{1,2},{2,6},{6,10},{... | collective-permute-start | bytes 1671176 | tf_op jit(solution)/shard_map/ppermute | solution.py:352
  36.2 0.0 collective-permute-done.8.refs_1_
  36.2 1.9 %collective-permute-start.15 = (bf16[2176,128]{1,0:T(8,128)(2,1)S(1)}, bf16[2176,128]{1,0:T(8,128)(2,1)S(1)}, u32[]{:S(2)}, u32[]{:S(2)}) collective-permute-start(bf16[2176,128]{1,0:T(8,128)(2,1)S(1)} %get-tuple-element.41.refs_1_), channel_id=1, source_target_pairs={{4,0},{8,4},{12,8},{13,12},{9,13},{5,9},{1,5},{2,1},{6,2},{10,6},{... | collective-permute-start | bytes 1671176 | tf_op jit(solution)/shard_map/ppermute | solution.py:353
  38.1 0.0 collective-permute-done.9.refs_2_
  38.2 0.8 collective-permute-start.12
  38.9 0.0 collective-permute-done.10.refs_3_
  38.9 3.1 %collective-permute-start.13 = (bf16[512,128]{1,0:T(8,128)(2,1)S(1)}, bf16[512,128]{1,0:T(8,128)(2,1)S(1)}, u32[]{:S(2)}, u32[]{:S(2)}) collective-permute-start(bf16[512,128]{1,0:T(8,128)(2,1)S(1)} %get-tuple-element.48), channel_id=1, source_target_pairs={{0,24},{4,28},{8,16},{12,20},{16,8},{20,12},{24,0},{28,4},{1,25},{... | collective-permute-start | bytes 393224 | tf_op jit(solution)/shard_map/ppermute | solution.py:335
  42.1 0.0 collective-permute-done.11.refs_4_
  42.1 1.4 %collective-permute-start.14 = (bf16[512,128]{1,0:T(8,128)(2,1)S(1)}, bf16[512,128]{1,0:T(8,128)(2,1)S(1)}, u32[]{:S(2)}, u32[]{:S(2)}) collective-permute-start(bf16[512,128]{1,0:T(8,128)(2,1)S(1)} %get-tuple-element.49), channel_id=1, source_target_pairs={{0,28},{4,24},{8,20},{12,16},{16,12},{20,8},{24,4},{28,0},{1,29},{... | collective-permute-start | bytes 393224 | tf_op jit(solution)/shard_map/ppermute | solution.py:335
  43.5 3.9 %collective-permute-done.12.refs_5_ = bf16[512,128]{1,0:T(8,128)(2,1)S(1)} collective-permute-done((bf16[512,128]{1,0:T(8,128)(2,1)S(1)}, bf16[512,128]{1,0:T(8,128)(2,1)S(1)}, u32[]{:S(2)}, u32[]{:S(2)}) %collective-permute-start.12) | collective-permute-done | bytes 131104 | tf_op jit(solution)/shard_map/ppermute | solution.py:335
  47.4 2.3 %collective-permute-done.13.refs_6_ = bf16[512,128]{1,0:T(8,128)(2,1)S(1)} collective-permute-done((bf16[512,128]{1,0:T(8,128)(2,1)S(1)}, bf16[512,128]{1,0:T(8,128)(2,1)S(1)}, u32[]{:S(2)}, u32[]{:S(2)}) %collective-permute-start.13) | collective-permute-done | bytes 131104 | tf_op jit(solution)/shard_map/ppermute | solution.py:335
  49.7 6.5 %collective-permute-done.14.refs_7_ = bf16[512,128]{1,0:T(8,128)(2,1)S(1)} collective-permute-done((bf16[512,128]{1,0:T(8,128)(2,1)S(1)}, bf16[512,128]{1,0:T(8,128)(2,1)S(1)}, u32[]{:S(2)}, u32[]{:S(2)}) %collective-permute-start.14) | collective-permute-done | bytes 131104 | tf_op jit(solution)/shard_map/ppermute | solution.py:335
  56.2 1.2 %inner.1.refs_2_ = bf16[2,2048,128]{2,1,0:T(8,128)(2,1)S(1)} custom-call(bf16[512,128]{1,0:T(8,128)(2,1)S(1)} %get-tuple-element.42.refs_0_, bf16[512,128]{1,0:T(8,128)(2,1)S(1)} %collective-permute-done.8.refs_1_, bf16[512,128]{1,0:T(8,128)(2,1)S(1)} %collective-permute-done.9.refs_2_, bf16[512,128]{1,0:T(8,128)(2,1)S(1)} %collective-permute-done.10.refs_3_, ...), custom_call_target="tpu_custom_call" | custom-call | flops 4000000000 | bytes 6291456 | tf_op jit(solution)/shard_map/inner/pallas_call | solution.py:161
  57.5 0.0 collective-permute-done.7.refs_0_
  57.5 0.0 collective-permute-done.15.refs_4_
  57.5 2.6 %boxed.2 = (bf16[256,128]{1,0:T(8,128)(2,1)S(1)}, bf16[256,128]{1,0:T(8,128)(2,1)S(1)}, bf16[256,128]{1,0:T(8,128)(2,1)S(1)}, bf16[256,128]{1,0:T(8,128)(2,1)S(1)}, f32[3,528,128]{2,1,0:T(8,128)S(1)}) custom-call(bf16[2176,128]{1,0:T(8,128)(2,1)S(1)} %collective-permute-done.7.refs_0_, bf16[2176,128]{1,0:T(8,128)(2,1)S(1)} %get-tuple-element.41.refs_1_, ...), custom_call_target="tpu_custom_call" | custom-call | flops 10000000 | bytes 6291456 | tf_op jit(solution)/shard_map/boxed/pallas_call | solution.py:268
  60.1 2.9 %collective-permute-start.19 = (bf16[256,128]{1,0:T(8,128)(2,1)S(1)}, bf16[256,128]{1,0:T(8,128)(2,1)S(1)}, u32[]{:S(2)}, u32[]{:S(2)}) collective-permute-start(bf16[256,128]{1,0:T(8,128)(2,1)S(1)} %get-tuple-element.55), channel_id=1, source_target_pairs={{0,16},{4,20},{8,24},{12,28},{16,0},{20,4},{24,8},{28,12},{1,17},{... | collective-permute-start | bytes 196616 | tf_op jit(solution)/shard_map/ppermute | solution.py:335
  62.9 0.9 %collective-permute-start.20 = (bf16[256,128]{1,0:T(8,128)(2,1)S(1)}, bf16[256,128]{1,0:T(8,128)(2,1)S(1)}, u32[]{:S(2)}, u32[]{:S(2)}) collective-permute-start(bf16[256,128]{1,0:T(8,128)(2,1)S(1)} %get-tuple-element.56), channel_id=1, source_target_pairs={{0,20},{4,16},{8,28},{12,24},{16,4},{20,0},{24,12},{28,8},{1,21},{... | collective-permute-start | bytes 196616 | tf_op jit(solution)/shard_map/ppermute | solution.py:335
  63.9 0.1 collective-permute-start.21
  64.0 3.6 %collective-permute-start.22 = (bf16[256,128]{1,0:T(8,128)(2,1)S(1)}, bf16[256,128]{1,0:T(8,128)(2,1)S(1)}, u32[]{:S(2)}, u32[]{:S(2)}) collective-permute-start(bf16[256,128]{1,0:T(8,128)(2,1)S(1)} %get-tuple-element.58), channel_id=1, source_target_pairs={{0,28},{4,24},{8,20},{12,16},{16,12},{20,8},{24,4},{28,0},{1,29},{... | collective-permute-start | bytes 196616 | tf_op jit(solution)/shard_map/ppermute | solution.py:335
  67.6 2.0 %boxed.3 = (bf16[256,128]{1,0:T(8,128)(2,1)S(1)}, bf16[256,128]{1,0:T(8,128)(2,1)S(1)}, bf16[256,128]{1,0:T(8,128)(2,1)S(1)}, bf16[256,128]{1,0:T(8,128)(2,1)S(1)}) custom-call(bf16[2176,128]{1,0:T(8,128)(2,1)S(1)} %collective-permute-done.7.refs_0_, bf16[2176,128]{1,0:T(8,128)(2,1)S(1)} %get-tuple-element.41.refs_1_, ...), custom_call_target="tpu_custom_call" | custom-call | flops 10000000 | bytes 6291456 | tf_op jit(solution)/shard_map/boxed/pallas_call | solution.py:268
  69.6 0.1 collective-permute-start.16
  69.7 0.0 collective-permute-done.19.refs_0_
  69.7 0.1 collective-permute-start.17
  69.8 3.3 %collective-permute-done.20.refs_1_ = bf16[256,128]{1,0:T(8,128)(2,1)S(1)} collective-permute-done((bf16[256,128]{1,0:T(8,128)(2,1)S(1)}, bf16[256,128]{1,0:T(8,128)(2,1)S(1)}, u32[]{:S(2)}, u32[]{:S(2)}) %collective-permute-start.20) | collective-permute-done | bytes 65568 | tf_op jit(solution)/shard_map/ppermute | solution.py:335
  73.1 0.9 %collective-permute-start.18 = (bf16[256,128]{1,0:T(8,128)(2,1)S(1)}, bf16[256,128]{1,0:T(8,128)(2,1)S(1)}, u32[]{:S(2)}, u32[]{:S(2)}) collective-permute-start(bf16[256,128]{1,0:T(8,128)(2,1)S(1)} %get-tuple-element.54), channel_id=1, source_target_pairs={{0,12},{4,8},{8,4},{12,0},{16,28},{20,24},{24,20},{28,16},{1,13},{... | collective-permute-start | bytes 196616 | tf_op jit(solution)/shard_map/ppermute | solution.py:335
  74.0 0.0 collective-permute-done.21.refs_2_
  74.0 0.0 collective-permute-done.22.refs_3_
  74.0 1.2 %join.2.refs_4_ = f32[1024,256]{1,0:T(8,128)} custom-call(bf16[256,128]{1,0:T(8,128)(2,1)S(1)} %collective-permute-done.19.refs_0_, bf16[256,128]{1,0:T(8,128)(2,1)S(1)} %collective-permute-done.20.refs_1_, bf16[256,128]{1,0:T(8,128)(2,1)S(1)} %collective-permute-done.21.refs_2_, bf16[256,128]{1,0:T(8,128)(2,1)S(1)} %collective-permute-done.22.refs_3_), custom_call_target="tpu_custom_call" | custom-call | flops 1000000000 | bytes 2097152 | tf_op jit(solution)/shard_map/join/pallas_call | solution.py:306
  75.2 0.0 collective-permute-done.16.refs_1_
  75.3 0.0 collective-permute-done.17.refs_2_
  75.3 1.7 %collective-permute-done.18.refs_3_ = bf16[256,128]{1,0:T(8,128)(2,1)S(1)} collective-permute-done((bf16[256,128]{1,0:T(8,128)(2,1)S(1)}, bf16[256,128]{1,0:T(8,128)(2,1)S(1)}, u32[]{:S(2)}, u32[]{:S(2)}) %collective-permute-start.18) | collective-permute-done | bytes 65568 | tf_op jit(solution)/shard_map/ppermute | solution.py:335
  77.0 1.2 %join.3 = f32[1024,256]{1,0:T(8,128)} custom-call(bf16[256,128]{1,0:T(8,128)(2,1)S(1)} %get-tuple-element.51.refs_0_, bf16[256,128]{1,0:T(8,128)(2,1)S(1)} %collective-permute-done.16.refs_1_, bf16[256,128]{1,0:T(8,128)(2,1)S(1)} %collective-permute-done.17.refs_2_, ...), custom_call_target="tpu_custom_call", output_to_operand_aliasing={{}: (4, {})} | custom-call | flops 1000000 | bytes 2097152 | tf_op jit(solution)/shard_map/join/pallas_call | solution.py:306
Async XLA Ops:
  0.0 29.6 %copy-start = (bf16[8,1024,128]{2,1,0:T(8,128)(2,1)S(1)}, bf16[8,1024,128]{2,1,0:T(8,128)(2,1)}, u32[]{:S(2)}) copy-start(bf16[8,1024,128]{2,1,0:T(8,128)(2,1)} %constant.2.clone.refs_8_) | copy-start | bytes 6291460
  3.8 6.8 %collective-permute-start = (bf16[528,128]{1,0:T(8,128)(2,1)S(1)}, bf16[528,128]{1,0:T(8,128)(2,1)S(1)}, u32[]{:S(2)}, u32[]{:S(2)}) collective-permute-start(bf16[528,128]{1,0:T(8,128)(2,1)S(1)} %get-tuple-element.33), channel_id=1, source_target_pairs={{0,4},{4,0},{8,12},{12,8},{16,20},{20,16},{24,28},{28,24},{1,5},{5... | collective-permute-start | bytes 405512 | tf_op jit(solution)/shard_map/ppermute | solution.py:335
  3.9 9.1 %collective-permute-start.5 = (bf16[528,128]{1,0:T(8,128)(2,1)S(1)}, bf16[528,128]{1,0:T(8,128)(2,1)S(1)}, u32[]{:S(2)}, u32[]{:S(2)}) collective-permute-start(bf16[528,128]{1,0:T(8,128)(2,1)S(1)} %get-tuple-element.38), channel_id=1, source_target_pairs={{0,24},{4,28},{8,16},{12,20},{16,8},{20,12},{24,0},{28,4},{1,25},{... | collective-permute-start | bytes 405512 | tf_op jit(solution)/shard_map/ppermute | solution.py:335
  8.7 10.9 %collective-permute-start.1 = (bf16[528,128]{1,0:T(8,128)(2,1)S(1)}, bf16[528,128]{1,0:T(8,128)(2,1)S(1)}, u32[]{:S(2)}, u32[]{:S(2)}) collective-permute-start(bf16[528,128]{1,0:T(8,128)(2,1)S(1)} %get-tuple-element.34), channel_id=1, source_target_pairs={{0,8},{4,12},{8,0},{12,4},{16,24},{20,28},{24,16},{28,20},{1,9},{5... | collective-permute-start | bytes 405512 | tf_op jit(solution)/shard_map/ppermute | solution.py:335
  8.7 13.8 %collective-permute-start.2 = (bf16[528,128]{1,0:T(8,128)(2,1)S(1)}, bf16[528,128]{1,0:T(8,128)(2,1)S(1)}, u32[]{:S(2)}, u32[]{:S(2)}) collective-permute-start(bf16[528,128]{1,0:T(8,128)(2,1)S(1)} %get-tuple-element.35), channel_id=1, source_target_pairs={{0,12},{4,8},{8,4},{12,0},{16,28},{20,24},{24,20},{28,16},{1,13},{... | collective-permute-start | bytes 405512 | tf_op jit(solution)/shard_map/ppermute | solution.py:335
  10.6 11.9 %collective-permute-start.3 = (bf16[528,128]{1,0:T(8,128)(2,1)S(1)}, bf16[528,128]{1,0:T(8,128)(2,1)S(1)}, u32[]{:S(2)}, u32[]{:S(2)}) collective-permute-start(bf16[528,128]{1,0:T(8,128)(2,1)S(1)} %get-tuple-element.36), channel_id=1, source_target_pairs={{0,16},{4,20},{8,24},{12,28},{16,0},{20,4},{24,8},{28,12},{1,17},{... | collective-permute-start | bytes 405512 | tf_op jit(solution)/shard_map/ppermute | solution.py:335
  10.6 18.9 %collective-permute-start.4 = (bf16[528,128]{1,0:T(8,128)(2,1)S(1)}, bf16[528,128]{1,0:T(8,128)(2,1)S(1)}, u32[]{:S(2)}, u32[]{:S(2)}) collective-permute-start(bf16[528,128]{1,0:T(8,128)(2,1)S(1)} %get-tuple-element.37), channel_id=1, source_target_pairs={{0,20},{4,16},{8,28},{12,24},{16,4},{20,0},{24,12},{28,8},{1,21},{... | collective-permute-start | bytes 405512 | tf_op jit(solution)/shard_map/ppermute | solution.py:335
  13.1 16.5 %collective-permute-start.6 = (bf16[528,128]{1,0:T(8,128)(2,1)S(1)}, bf16[528,128]{1,0:T(8,128)(2,1)S(1)}, u32[]{:S(2)}, u32[]{:S(2)}) collective-permute-start(bf16[528,128]{1,0:T(8,128)(2,1)S(1)} %get-tuple-element.39), channel_id=1, source_target_pairs={{0,28},{4,24},{8,20},{12,16},{16,12},{20,8},{24,4},{28,0},{1,29},{... | collective-permute-start | bytes 405512 | tf_op jit(solution)/shard_map/ppermute | solution.py:335
  19.5 16.7 %collective-permute-start.8 = (bf16[512,128]{1,0:T(8,128)(2,1)S(1)}, bf16[512,128]{1,0:T(8,128)(2,1)S(1)}, u32[]{:S(2)}, u32[]{:S(2)}) collective-permute-start(bf16[512,128]{1,0:T(8,128)(2,1)S(1)} %get-tuple-element.43), channel_id=1, source_target_pairs={{0,4},{4,0},{8,12},{12,8},{16,20},{20,16},{24,28},{28,24},{1,5},{5... | collective-permute-start | bytes 393224 | tf_op jit(solution)/shard_map/ppermute | solution.py:335
  22.5 15.6 %collective-permute-start.9 = (bf16[512,128]{1,0:T(8,128)(2,1)S(1)}, bf16[512,128]{1,0:T(8,128)(2,1)S(1)}, u32[]{:S(2)}, u32[]{:S(2)}) collective-permute-start(bf16[512,128]{1,0:T(8,128)(2,1)S(1)} %get-tuple-element.44), channel_id=1, source_target_pairs={{0,8},{4,12},{8,0},{12,4},{16,24},{20,28},{24,16},{28,20},{1,9},{5... | collective-permute-start | bytes 393224 | tf_op jit(solution)/shard_map/ppermute | solution.py:335
  22.5 16.4 %collective-permute-start.10 = (bf16[512,128]{1,0:T(8,128)(2,1)S(1)}, bf16[512,128]{1,0:T(8,128)(2,1)S(1)}, u32[]{:S(2)}, u32[]{:S(2)}) collective-permute-start(bf16[512,128]{1,0:T(8,128)(2,1)S(1)} %get-tuple-element.45), channel_id=1, source_target_pairs={{0,12},{4,8},{8,4},{12,0},{16,28},{20,24},{24,20},{28,16},{1,13},{... | collective-permute-start | bytes 393224 | tf_op jit(solution)/shard_map/ppermute | solution.py:335
  29.6 12.5 %collective-permute-start.11 = (bf16[512,128]{1,0:T(8,128)(2,1)S(1)}, bf16[512,128]{1,0:T(8,128)(2,1)S(1)}, u32[]{:S(2)}, u32[]{:S(2)}) collective-permute-start(bf16[512,128]{1,0:T(8,128)(2,1)S(1)} %get-tuple-element.46), channel_id=1, source_target_pairs={{0,16},{4,20},{8,24},{12,28},{16,0},{20,4},{24,8},{28,12},{1,17},{... | collective-permute-start | bytes 393224 | tf_op jit(solution)/shard_map/ppermute | solution.py:335
  31.5 26.0 %collective-permute-start.7 = (bf16[2176,128]{1,0:T(8,128)(2,1)S(1)}, bf16[2176,128]{1,0:T(8,128)(2,1)S(1)}, u32[]{:S(2)}, u32[]{:S(2)}) collective-permute-start(bf16[2176,128]{1,0:T(8,128)(2,1)S(1)} %get-tuple-element.40.refs_3_), channel_id=1, source_target_pairs={{0,4},{4,8},{8,12},{12,13},{13,9},{9,5},{5,1},{1,2},{2,6},{6,10},{... | collective-permute-start | bytes 1671176 | tf_op jit(solution)/shard_map/ppermute | solution.py:352
  36.2 21.3 %collective-permute-start.15 = (bf16[2176,128]{1,0:T(8,128)(2,1)S(1)}, bf16[2176,128]{1,0:T(8,128)(2,1)S(1)}, u32[]{:S(2)}, u32[]{:S(2)}) collective-permute-start(bf16[2176,128]{1,0:T(8,128)(2,1)S(1)} %get-tuple-element.41.refs_1_), channel_id=1, source_target_pairs={{4,0},{8,4},{12,8},{13,12},{9,13},{5,9},{1,5},{2,1},{6,2},{10,6},{... | collective-permute-start | bytes 1671176 | tf_op jit(solution)/shard_map/ppermute | solution.py:353
  38.2 9.2 %collective-permute-start.12 = (bf16[512,128]{1,0:T(8,128)(2,1)S(1)}, bf16[512,128]{1,0:T(8,128)(2,1)S(1)}, u32[]{:S(2)}, u32[]{:S(2)}) collective-permute-start(bf16[512,128]{1,0:T(8,128)(2,1)S(1)} %get-tuple-element.47), channel_id=1, source_target_pairs={{0,20},{4,16},{8,28},{12,24},{16,4},{20,0},{24,12},{28,8},{1,21},{... | collective-permute-start | bytes 393224 | tf_op jit(solution)/shard_map/ppermute | solution.py:335
  38.9 10.8 %collective-permute-start.13 = (bf16[512,128]{1,0:T(8,128)(2,1)S(1)}, bf16[512,128]{1,0:T(8,128)(2,1)S(1)}, u32[]{:S(2)}, u32[]{:S(2)}) collective-permute-start(bf16[512,128]{1,0:T(8,128)(2,1)S(1)} %get-tuple-element.48), channel_id=1, source_target_pairs={{0,24},{4,28},{8,16},{12,20},{16,8},{20,12},{24,0},{28,4},{1,25},{... | collective-permute-start | bytes 393224 | tf_op jit(solution)/shard_map/ppermute | solution.py:335
  42.1 14.2 %collective-permute-start.14 = (bf16[512,128]{1,0:T(8,128)(2,1)S(1)}, bf16[512,128]{1,0:T(8,128)(2,1)S(1)}, u32[]{:S(2)}, u32[]{:S(2)}) collective-permute-start(bf16[512,128]{1,0:T(8,128)(2,1)S(1)} %get-tuple-element.49), channel_id=1, source_target_pairs={{0,28},{4,24},{8,20},{12,16},{16,12},{20,8},{24,4},{28,0},{1,29},{... | collective-permute-start | bytes 393224 | tf_op jit(solution)/shard_map/ppermute | solution.py:335
  60.1 9.6 %collective-permute-start.19 = (bf16[256,128]{1,0:T(8,128)(2,1)S(1)}, bf16[256,128]{1,0:T(8,128)(2,1)S(1)}, u32[]{:S(2)}, u32[]{:S(2)}) collective-permute-start(bf16[256,128]{1,0:T(8,128)(2,1)S(1)} %get-tuple-element.55), channel_id=1, source_target_pairs={{0,16},{4,20},{8,24},{12,28},{16,0},{20,4},{24,8},{28,12},{1,17},{... | collective-permute-start | bytes 196616 | tf_op jit(solution)/shard_map/ppermute | solution.py:335
  62.9 10.2 %collective-permute-start.20 = (bf16[256,128]{1,0:T(8,128)(2,1)S(1)}, bf16[256,128]{1,0:T(8,128)(2,1)S(1)}, u32[]{:S(2)}, u32[]{:S(2)}) collective-permute-start(bf16[256,128]{1,0:T(8,128)(2,1)S(1)} %get-tuple-element.56), channel_id=1, source_target_pairs={{0,20},{4,16},{8,28},{12,24},{16,4},{20,0},{24,12},{28,8},{1,21},{... | collective-permute-start | bytes 196616 | tf_op jit(solution)/shard_map/ppermute | solution.py:335
  63.9 10.2 %collective-permute-start.21 = (bf16[256,128]{1,0:T(8,128)(2,1)S(1)}, bf16[256,128]{1,0:T(8,128)(2,1)S(1)}, u32[]{:S(2)}, u32[]{:S(2)}) collective-permute-start(bf16[256,128]{1,0:T(8,128)(2,1)S(1)} %get-tuple-element.57), channel_id=1, source_target_pairs={{0,24},{4,28},{8,16},{12,20},{16,8},{20,12},{24,0},{28,4},{1,25},{... | collective-permute-start | bytes 196616 | tf_op jit(solution)/shard_map/ppermute | solution.py:335
  64.0 10.1 %collective-permute-start.22 = (bf16[256,128]{1,0:T(8,128)(2,1)S(1)}, bf16[256,128]{1,0:T(8,128)(2,1)S(1)}, u32[]{:S(2)}, u32[]{:S(2)}) collective-permute-start(bf16[256,128]{1,0:T(8,128)(2,1)S(1)} %get-tuple-element.58), channel_id=1, source_target_pairs={{0,28},{4,24},{8,20},{12,16},{16,12},{20,8},{24,4},{28,0},{1,29},{... | collective-permute-start | bytes 196616 | tf_op jit(solution)/shard_map/ppermute | solution.py:335
  69.6 5.6 %collective-permute-start.16 = (bf16[256,128]{1,0:T(8,128)(2,1)S(1)}, bf16[256,128]{1,0:T(8,128)(2,1)S(1)}, u32[]{:S(2)}, u32[]{:S(2)}) collective-permute-start(bf16[256,128]{1,0:T(8,128)(2,1)S(1)} %get-tuple-element.52), channel_id=1, source_target_pairs={{0,4},{4,0},{8,12},{12,8},{16,20},{20,16},{24,28},{28,24},{1,5},{5... | collective-permute-start | bytes 196616 | tf_op jit(solution)/shard_map/ppermute | solution.py:335
  69.7 5.5 %collective-permute-start.17 = (bf16[256,128]{1,0:T(8,128)(2,1)S(1)}, bf16[256,128]{1,0:T(8,128)(2,1)S(1)}, u32[]{:S(2)}, u32[]{:S(2)}) collective-permute-start(bf16[256,128]{1,0:T(8,128)(2,1)S(1)} %get-tuple-element.53), channel_id=1, source_target_pairs={{0,8},{4,12},{8,0},{12,4},{16,24},{20,28},{24,16},{28,20},{1,9},{5... | collective-permute-start | bytes 196616 | tf_op jit(solution)/shard_map/ppermute | solution.py:335
  73.1 3.9 %collective-permute-start.18 = (bf16[256,128]{1,0:T(8,128)(2,1)S(1)}, bf16[256,128]{1,0:T(8,128)(2,1)S(1)}, u32[]{:S(2)}, u32[]{:S(2)}) collective-permute-start(bf16[256,128]{1,0:T(8,128)(2,1)S(1)} %get-tuple-element.54), channel_id=1, source_target_pairs={{0,12},{4,8},{8,4},{12,0},{16,28},{20,24},{24,20},{28,16},{1,13},{... | collective-permute-start | bytes 196616 | tf_op jit(solution)/shard_map/ppermute | solution.py:335

commit v6 on v5

--- a/solution.py
+++ b/solution.py
@@ -13,6 +13,7 @@
 DEPTH = 512
 LANES = 128
 AFTER = 2
+STEP = 16
 EDGE = 16
 F32 = jnp.float32
 BF16 = jnp.bfloat16
@@ -92,10 +93,20 @@
     )(x, *after)
 
 
-def transform(t_ref, pieces, kl, slot):
+def transform(t_ref, pieces, kl, slot, base=None):
     n = len(pieces)
     me = lax.axis_index("ka")
-    t = jnp.concatenate([t_ref[me ^ s] for s in range(n)], axis=1)
+    if base is None:
+        blocks = [t_ref[me ^ s] for s in range(n)]
+    else:
+        span = DEPTH // 2
+        other = pl.multiple_of(jnp.where(base == 0, span, span - STEP), STEP)
+        parts = [(z + at, size) for z in (0, DEPTH) for at, size in ((base, span), (other, STEP))]
+        blocks = [
+            jnp.concatenate([t_ref[me ^ s, pl.ds(z, size), :] for z, size in parts], axis=0)
+            for s in range(n)
+        ]
+    t = jnp.concatenate(blocks, axis=1)
     x = jnp.concatenate(
         [
             jnp.concatenate([p[pl.ds((slot * 2 + q) * kl, kl), :] for p in pieces], axis=0)
@@ -149,43 +160,57 @@
     )(*pieces, t)
 
 
-def inner_kernel(n, kl, rest, *refs):
-    pieces, t_ref, out = refs[:n], refs[n], refs[n + 1]
+def half_rows(t_ref, pieces, kl, rest, base, out):
     for slot in range(len(rest)):
-        s = transform(t_ref, pieces, kl, slot)
-        out[slot, : 2 * DEPTH, :] = s[:, :LANES]
-        out[slot, 2 * DEPTH :, :] = s[:, LANES:]
-
-
-def inner(pieces, t, n, kl, rest):
-    return pl.pallas_call(
-        functools.partial(inner_kernel, n, kl, rest),
-        out_shape=jax.ShapeDtypeStruct((len(rest), 4 * DEPTH, LANES), BF16),
-        compiler_params=params(),
-        cost_estimate=pl.CostEstimate(flops=4 * 10**9, bytes_accessed=6 * 2**20, transcendentals=0),
+        s = transform(t_ref, pieces, kl, slot, base)
+        out[slot, : DEPTH + 2 * STEP, :] = s[:, :LANES]
+        out[slot, DEPTH + 2 * STEP :, :] = s[:, LANES:]
+
+
+def inner_kernel(n, kl, rest, far, *refs):
+    pieces, t_ref, out = refs[:n], refs[n], refs[-1]
+    h = lax.axis_index("ka") // (n // 2)
+    base = pl.multiple_of((1 - h if far else h) * (DEPTH // 2), DEPTH // 2)
+    half_rows(t_ref, pieces, kl, rest, base, out)
+
+
+def inner(pieces, t, n, kl, rest, after=()):
+    return pl.pallas_call(
+        functools.partial(inner_kernel, n, kl, rest, not after),
+        out_shape=jax.ShapeDtypeStruct((len(rest), 2 * (DEPTH + 2 * STEP), LANES), BF16),
+        in_specs=[pl.BlockSpec(memory_space=pltpu.VMEM)] * (n + 1)
+        + [pl.BlockSpec(memory_space=pl.ANY)] * len(after),
+        compiler_params=params(),
+        cost_estimate=pl.CostEstimate(flops=10**7 if after else 4 * 10**9, bytes_accessed=6 * 2**20, transcendentals=0),
         name="inner",
-    )(*pieces, t)
-
-
-STEP = 16
-
-
-def box_kernel(n, rb, far, *refs):
-    half, span, count = n // 2, DEPTH // 2, 4 + (rb > 2)
-    above, top, bottom, below = refs[0], refs[1], refs[count - 2], refs[count - 1]
-    inside = refs[2]
-    outs = refs[count : count + half] if far else refs[count + 1 : count + 1 + half]
-    edge = refs[count + half] if far else refs[count]
-    total, dec = refs[-2:]
+    )(*pieces, t, *after)
+
+
+def box_kernel(n, kl, rb, far, *refs):
+    half, span = n // 2, DEPTH // 2
+    above, top, bottom, below = refs[:4]
+    own = 0 if far or rb == 2 else 1
+    total, dec, inside = refs[-3:]
+    if far:
+        inside = refs[4] if rb > 2 else None
+        outs, edge = refs[-half - 4 : -4], refs[-4]
+    else:
+        edge, sources = refs[4], refs[5 : 5 + own]
+        outs = refs[5 + own : 5 + own + half]
     me = lax.axis_index("ka")
     h = me // half
     dl = DEPTH // n
     base = pl.multiple_of((1 - h if far else h) * span, span)
 
-    def spectrum(r, z):
+    if own:
+        inside = sources[0]
+
+    def spectrum(r, z, near):
         ref = {-1: above, 0: top, rb - 1: bottom, rb: below}.get(r)
-        where = [pl.ds(z + j * DEPTH, STEP) for j in range(4)]
-        rows = [ref[w, :] for w in where] if ref is not None else [inside[r - 1, w, :] for w in where]
+        if ref is not None:
+            rows = [ref[pl.ds(z + j * DEPTH, STEP), :] for j in range(4)]
+        else:
+            rows = [inside[r - 1, pl.ds(near + j * (span + STEP), STEP), :] for j in range(4)]
         return [x.astype(F32) for x in rows]
 
     def make_edge():
@@ -209,12 +234,12 @@
     if far:
         make_edge()
 
-    def over_rows(z, at, keep=None):
-        before = terms(*spectrum(-1, z))
-        here = terms(*spectrum(0, z))
+    def over_rows(z, at, near, keep=None):
+        before = terms(*spectrum(-1, z, near))
+        here = terms(*spectrum(0, z, near))
         pair = [x + y for x, y in zip(before, here)]
         for r in range(rb):
-            after = terms(*spectrum(r + 1, z))
+            after = terms(*spectrum(r + 1, z, near))
             for t in range(3):
                 v = pair[t] + after[t]
                 v = v if keep is None else jnp.where(keep, v, 0.0)
@@ -225,12 +250,12 @@
     @pl.loop(0, span // STEP, unroll=4)
     def _(i):
         z = pl.multiple_of(i * STEP, STEP)
-        over_rows(pl.multiple_of(base + z, STEP), pl.multiple_of(z + STEP, STEP))
+        over_rows(pl.multiple_of(base + z, STEP), pl.multiple_of(z + STEP, STEP), z)
 
     z = pl.multiple_of(jnp.maximum(base - STEP, 0), STEP)
-    over_rows(z, 0, base > 0)
+    over_rows(z, 0, span, base > 0)
     z = pl.multiple_of(jnp.minimum(base + span, DEPTH - STEP), STEP)
-    over_rows(z, span + STEP, base + span < DEPTH)
+    over_rows(z, span + STEP, span, base + span < DEPTH)
 
     lane = lax.broadcasted_iota(jnp.int32, (STEP, LANES), 1)
     not_first, not_last = lane > 0, lane < LANES - 1
@@ -263,20 +288,20 @@
             outs[i][pl.ds(r * dl, dl), :] = dec[r, pl.ds(z, dl), :]
 
 
-def boxed(rows, n, rb, edge=None):
-    far = edge is None
-    return pl.pallas_call(
-        functools.partial(box_kernel, n, rb, far),
+def boxed(rows, n, kl, rb, far):
+    return pl.pallas_call(
+        functools.partial(box_kernel, n, kl, rb, far),
         out_shape=[jax.ShapeDtypeStruct((rb * (DEPTH // n), LANES), BF16)] * (n // 2)
         + ([jax.ShapeDtypeStruct((3, DEPTH + 16, LANES), F32)] if far else []),
         scratch_shapes=[
             pltpu.VMEM((rb, 3, DEPTH // 2 + 2 * STEP, LANES), F32),
             pltpu.VMEM((rb, DEPTH // 2, LANES), BF16),
+            pltpu.VMEM((max(rb - 2, 1), 16 if far else 2 * (DEPTH + 2 * STEP), LANES), BF16),
         ],
         compiler_params=params(),
         cost_estimate=pl.CostEstimate(flops=10**7, bytes_accessed=6 * 2**20, transcendentals=0),
         name="boxed",
-    )(*rows, *([] if far else [edge]))
+    )(*rows)
 
 
 def join_kernel(n, rows, rb, far, *refs):
@@ -352,9 +377,10 @@
     above = lax.ppermute(bottom, ("ka", "row"), down)
     below = lax.ppermute(top, ("ka", "row"), [(j, i) for i, j in down])
     inside = [inner(b, t, n, kl, rest)] if rest else []
-    spectra = [above, top, *inside, bottom, below]
-    *away, edge = boxed(spectra, n, rb)
-    pieces = [*boxed(spectra, n, rb, edge), *away]
+    outside = [above, top, bottom, below]
+    *away, edge = boxed([*outside, *inside], n, kl, rb, True)
+    here = boxed([*outside, edge, *([inner(b, t, n, kl, rest, [edge])] if rest else [])], n, kl, rb, False)
+    pieces = [*here, *away]
     pieces = exchange(pieces, [*far, *near, *core])
     out = join(pieces[:half], n, rows, rb, join(pieces[half:], n, rows, rb))
     return out.reshape(DEPTH // n, rows, cols)

time: 78.4 us -> 77.9 us (level)
  waiting for transfers between devices: 25.9 us -> 25.1 us
    pallas_call x3 -> x4, Pallas kernels: 5.83 us -> 6.13 us  [the longest x2 4.63 us: boxed(): pl.pallas_call(functools.partial(box_kernel, n, kl, rb, far), out_shape=[...]
where the time goes in v6:
time: 77.9 us; the launch traced here: 77.7 us
  starting transfers between devices  36.1 us (46%)
  waiting for transfers between devices  25.1 us (32%)
  Pallas kernels  16.3 us (21%)
    ppermute x21, starting transfers between devices, exchange(): out[s] = lax.ppermute(pieces[s], 'ka', [(i, i ^ s) for i in range(n)])  29.4 us
    ppermute x21, waiting for transfers between devices, exchange(): out[s] = lax.ppermute(pieces[s], 'ka', [(i, i ^ s) for i in range(n)])  25.1 us
    pallas_call x2, Pallas kernels, split(): pl.pallas_call(functools.partial(split_kernel, n, rows, kl, rb, group, ed...  5.96 us
    ppermute x1, starting transfers between devices, body(): above = lax.ppermute(bottom, ('ka', 'row'), down)  4.74 us
    pallas_call x2, Pallas kernels, boxed(): pl.pallas_call(functools.partial(box_kernel, n, kl, rb, far), out_shape=[...  4.63 us
    pallas_call x2, Pallas kernels, join(): pl.pallas_call(functools.partial(join_kernel, n, rows, rb, far), out_shap...  2.39 us
    ppermute x1, starting transfers between devices, body(): below = lax.ppermute(top, ('ka', 'row'), [(j, i) for i, j in down])  1.92 us
    pallas_call x1, Pallas kernels, outer(): pl.pallas_call(functools.partial(outer_kernel, n, kl, first), out_shape=[...  1.87 us
  transfers between devices with their start and end apart: 23, of which 8 were waited for; matrix products, arithmetic and copies ran while one was open for 0% of the time, Pallas kernels for 11%

profile of v6, /device:TPU:1, one launch (start us, length us, event | category | flops | bytes accessed | tf_op | source)
XLA Modules:
  0.0 77.7 jit_solution(12379697240922212897)
XLA Ops:
  0.0 0.0 copy-start
  0.0 3.8 %split.2 = (bf16[528,128]{1,0:T(8,128)(2,1)S(1)}, bf16[528,128]{1,0:T(8,128)(2,1)S(1)}, bf16[528,128]{1,0:T(8,128)(2,1)S(1)}, bf16[528,128]{1,0:T(8,128)(2,1)S(1...) custom-call(bf16[4096,256]{1,0:T(8,128)(2,1)} %bitcast.2), custom_call_target="tpu_custom_call" | custom-call | flops 1000000 | bytes 4194304 | tf_op jit(solution)/shard_map/split/pallas_call | solution.py:80
  3.8 0.1 collective-permute-start
  3.9 4.7 %collective-permute-start.5 = (bf16[528,128]{1,0:T(8,128)(2,1)S(1)}, bf16[528,128]{1,0:T(8,128)(2,1)S(1)}, u32[]{:S(2)}, u32[]{:S(2)}) collective-permute-start(bf16[528,128]{1,0:T(8,128)(2,1)S(1)} %get-tuple-element.38), channel_id=1, source_target_pairs={{0,24},{4,28},{8,16},{12,20},{16,8},{20,12},{24,0},{28,4},{1,25},{... | collective-permute-start | bytes 405512 | tf_op jit(solution)/shard_map/ppermute | solution.py:360
  8.7 0.0 collective-permute-start.1
  8.7 2.0 %collective-permute-start.2 = (bf16[528,128]{1,0:T(8,128)(2,1)S(1)}, bf16[528,128]{1,0:T(8,128)(2,1)S(1)}, u32[]{:S(2)}, u32[]{:S(2)}) collective-permute-start(bf16[528,128]{1,0:T(8,128)(2,1)S(1)} %get-tuple-element.35), channel_id=1, source_target_pairs={{0,12},{4,8},{8,4},{12,0},{16,28},{20,24},{24,20},{28,16},{1,13},{... | collective-permute-start | bytes 405512 | tf_op jit(solution)/shard_map/ppermute | solution.py:360
  10.6 0.0 collective-permute-start.3
  10.6 0.0 collective-permute-done.refs_1_
  10.6 2.4 %collective-permute-start.4 = (bf16[528,128]{1,0:T(8,128)(2,1)S(1)}, bf16[528,128]{1,0:T(8,128)(2,1)S(1)}, u32[]{:S(2)}, u32[]{:S(2)}) collective-permute-start(bf16[528,128]{1,0:T(8,128)(2,1)S(1)} %get-tuple-element.37), channel_id=1, source_target_pairs={{0,20},{4,16},{8,28},{12,24},{16,4},{20,0},{24,12},{28,8},{1,21},{... | collective-permute-start | bytes 405512 | tf_op jit(solution)/shard_map/ppermute | solution.py:360
  13.1 0.0 collective-permute-done.5.refs_6_.refs_0_
  13.1 3.8 %collective-permute-start.6 = (bf16[528,128]{1,0:T(8,128)(2,1)S(1)}, bf16[528,128]{1,0:T(8,128)(2,1)S(1)}, u32[]{:S(2)}, u32[]{:S(2)}) collective-permute-start(bf16[528,128]{1,0:T(8,128)(2,1)S(1)} %get-tuple-element.39), channel_id=1, source_target_pairs={{0,28},{4,24},{8,20},{12,16},{16,12},{20,8},{24,4},{28,0},{1,29},{... | collective-permute-start | bytes 405512 | tf_op jit(solution)/shard_map/ppermute | solution.py:360
  16.8 2.2 %split.3 = (bf16[512,128]{1,0:T(8,128)(2,1)S(1)}, bf16[512,128]{1,0:T(8,128)(2,1)S(1)}, bf16[512,128]{1,0:T(8,128)(2,1)S(1)}, bf16[512,128]{1,0:T(8,128)(2,1)S(1...) custom-call(bf16[4096,256]{1,0:T(8,128)(2,1)} %bitcast.3, ...), custom_call_target="tpu_custom_call" | custom-call | flops 1000000 | bytes 4194304 | tf_op jit(solution)/shard_map/split/pallas_call | solution.py:80
  19.0 0.5 collective-permute-done.1.refs_2_
  19.5 0.5 collective-permute-start.9
  20.1 2.4 %collective-permute-done.2.refs_3_ = bf16[528,128]{1,0:T(8,128)(2,1)S(1)} collective-permute-done((bf16[528,128]{1,0:T(8,128)(2,1)S(1)}, bf16[528,128]{1,0:T(8,128)(2,1)S(1)}, u32[]{:S(2)}, u32[]{:S(2)}) %collective-permute-start.2) | collective-permute-done | bytes 135200 | tf_op jit(solution)/shard_map/ppermute | solution.py:360
  22.5 0.0 collective-permute-start.10
  22.5 0.0 collective-permute-done.3.refs_4_
  22.5 1.9 %collective-permute-start.11 = (bf16[512,128]{1,0:T(8,128)(2,1)S(1)}, bf16[512,128]{1,0:T(8,128)(2,1)S(1)}, u32[]{:S(2)}, u32[]{:S(2)}) collective-permute-start(bf16[512,128]{1,0:T(8,128)(2,1)S(1)} %get-tuple-element.45), channel_id=1, source_target_pairs={{0,12},{4,8},{8,4},{12,0},{16,28},{20,24},{24,20},{28,16},{1,13},{... | collective-permute-start | bytes 393224 | tf_op jit(solution)/shard_map/ppermute | solution.py:360
  24.5 5.1 %collective-permute-done.4.refs_5_ = bf16[528,128]{1,0:T(8,128)(2,1)S(1)} collective-permute-done((bf16[528,128]{1,0:T(8,128)(2,1)S(1)}, bf16[528,128]{1,0:T(8,128)(2,1)S(1)}, u32[]{:S(2)}, u32[]{:S(2)}) %collective-permute-start.4) | collective-permute-done | bytes 135200 | tf_op jit(solution)/shard_map/ppermute | solution.py:360
  29.6 0.0 collective-permute-start.12
  29.6 0.0 collective-permute-done.6.refs_7_
  29.6 0.0 copy-done
  29.6 1.9 %outer.1 = (bf16[2176,128]{1,0:T(8,128)(2,1)S(1)}, bf16[2176,128]{1,0:T(8,128)(2,1)S(1)}) custom-call(bf16[528,128]{1,0:T(8,128)(2,1)S(1)} %get-tuple-element.32.refs_0_, bf16[528,128]{1,0:T(8,128)(2,1)S(1)} %collective-permute-done.refs_1_, bf16[528,128]{1,0:T(8,128)(2,1)S(1)} %collective-permute-done.1.refs_2_, ...), custom_call_target="tpu_custom_call" | custom-call | flops 1610612736 | bytes 4194304 | tf_op jit(solution)/shard_map/outer/pallas_call | solution.py:152
  31.4 4.7 %collective-permute-start.7 = (bf16[2176,128]{1,0:T(8,128)(2,1)S(1)}, bf16[2176,128]{1,0:T(8,128)(2,1)S(1)}, u32[]{:S(2)}, u32[]{:S(2)}) collective-permute-start(bf16[2176,128]{1,0:T(8,128)(2,1)S(1)} %get-tuple-element.40.refs_2_), channel_id=1, source_target_pairs={{0,4},{4,8},{8,12},{12,13},{13,9},{9,5},{5,1},{1,2},{2,6},{6,10},{... | collective-permute-start | bytes 1671176 | tf_op jit(solution)/shard_map/ppermute | solution.py:377
  36.2 0.0 collective-permute-done.9.refs_1_
  36.2 1.9 %collective-permute-start.8 = (bf16[2176,128]{1,0:T(8,128)(2,1)S(1)}, bf16[2176,128]{1,0:T(8,128)(2,1)S(1)}, u32[]{:S(2)}, u32[]{:S(2)}) collective-permute-start(bf16[2176,128]{1,0:T(8,128)(2,1)S(1)} %get-tuple-element.41.refs_1_), channel_id=1, source_target_pairs={{4,0},{8,4},{12,8},{13,12},{9,13},{5,9},{1,5},{2,1},{6,2},{10,6},{... | collective-permute-start | bytes 1671176 | tf_op jit(solution)/shard_map/ppermute | solution.py:378
  38.1 0.0 collective-permute-done.10.refs_2_
  38.1 0.8 collective-permute-start.13
  38.9 0.0 collective-permute-done.11.refs_3_
  38.9 3.1 %collective-permute-start.14 = (bf16[512,128]{1,0:T(8,128)(2,1)S(1)}, bf16[512,128]{1,0:T(8,128)(2,1)S(1)}, u32[]{:S(2)}, u32[]{:S(2)}) collective-permute-start(bf16[512,128]{1,0:T(8,128)(2,1)S(1)} %get-tuple-element.48), channel_id=1, source_target_pairs={{0,24},{4,28},{8,16},{12,20},{16,8},{20,12},{24,0},{28,4},{1,25},{... | collective-permute-start | bytes 393224 | tf_op jit(solution)/shard_map/ppermute | solution.py:360
  42.0 0.0 collective-permute-done.12.refs_4_
  42.1 1.4 %collective-permute-start.15 = (bf16[512,128]{1,0:T(8,128)(2,1)S(1)}, bf16[512,128]{1,0:T(8,128)(2,1)S(1)}, u32[]{:S(2)}, u32[]{:S(2)}) collective-permute-start(bf16[512,128]{1,0:T(8,128)(2,1)S(1)} %get-tuple-element.49), channel_id=1, source_target_pairs={{0,28},{4,24},{8,20},{12,16},{16,12},{20,8},{24,4},{28,0},{1,29},{... | collective-permute-start | bytes 393224 | tf_op jit(solution)/shard_map/ppermute | solution.py:360
  43.5 3.9 %collective-permute-done.13.refs_5_ = bf16[512,128]{1,0:T(8,128)(2,1)S(1)} collective-permute-done((bf16[512,128]{1,0:T(8,128)(2,1)S(1)}, bf16[512,128]{1,0:T(8,128)(2,1)S(1)}, u32[]{:S(2)}, u32[]{:S(2)}) %collective-permute-start.13) | collective-permute-done | bytes 131104 | tf_op jit(solution)/shard_map/ppermute | solution.py:360
  47.4 2.3 %collective-permute-done.14.refs_6_ = bf16[512,128]{1,0:T(8,128)(2,1)S(1)} collective-permute-done((bf16[512,128]{1,0:T(8,128)(2,1)S(1)}, bf16[512,128]{1,0:T(8,128)(2,1)S(1)}, u32[]{:S(2)}, u32[]{:S(2)}) %collective-permute-start.14) | collective-permute-done | bytes 131104 | tf_op jit(solution)/shard_map/ppermute | solution.py:360
  49.7 6.5 %collective-permute-done.15.refs_7_ = bf16[512,128]{1,0:T(8,128)(2,1)S(1)} collective-permute-done((bf16[512,128]{1,0:T(8,128)(2,1)S(1)}, bf16[512,128]{1,0:T(8,128)(2,1)S(1)}, u32[]{:S(2)}, u32[]{:S(2)}) %collective-permute-start.15) | collective-permute-done | bytes 131104 | tf_op jit(solution)/shard_map/ppermute | solution.py:360
  56.2 0.7 inner.2.refs_4_
  57.0 0.0 collective-permute-done.7.refs_0_
  57.0 0.0 collective-permute-done.8.refs_3_
  57.0 2.6 %boxed.2 = (bf16[256,128]{1,0:T(8,128)(2,1)S(1)}, bf16[256,128]{1,0:T(8,128)(2,1)S(1)}, bf16[256,128]{1,0:T(8,128)(2,1)S(1)}, bf16[256,128]{1,0:T(8,128)(2,1)S(1)}, f32[3,528,128]{2,1,0:T(8,128)S(1)}) custom-call(bf16[2176,128]{1,0:T(8,128)(2,1)S(1)} %collective-permute-done.7.refs_0_, bf16[2176,128]{1,0:T(8,128)(2,1)S(1)} %get-tuple-element.41.refs_1_, ...), custom_call_target="tpu_custom_call" | custom-call | flops 10000000 | bytes 6291456 | tf_op jit(solution)/shard_map/boxed/pallas_call | solution.py:292
  59.6 2.9 %collective-permute-start.19 = (bf16[256,128]{1,0:T(8,128)(2,1)S(1)}, bf16[256,128]{1,0:T(8,128)(2,1)S(1)}, u32[]{:S(2)}, u32[]{:S(2)}) collective-permute-start(bf16[256,128]{1,0:T(8,128)(2,1)S(1)} %get-tuple-element.55), channel_id=1, source_target_pairs={{0,16},{4,20},{8,24},{12,28},{16,0},{20,4},{24,8},{28,12},{1,17},{... | collective-permute-start | bytes 196616 | tf_op jit(solution)/shard_map/ppermute | solution.py:360
  62.5 0.9 %collective-permute-start.20 = (bf16[256,128]{1,0:T(8,128)(2,1)S(1)}, bf16[256,128]{1,0:T(8,128)(2,1)S(1)}, u32[]{:S(2)}, u32[]{:S(2)}) collective-permute-start(bf16[256,128]{1,0:T(8,128)(2,1)S(1)} %get-tuple-element.56), channel_id=1, source_target_pairs={{0,20},{4,16},{8,28},{12,24},{16,4},{20,0},{24,12},{28,8},{1,21},{... | collective-permute-start | bytes 196616 | tf_op jit(solution)/shard_map/ppermute | solution.py:360
  63.4 0.1 collective-permute-start.21
  63.5 3.6 %collective-permute-start.22 = (bf16[256,128]{1,0:T(8,128)(2,1)S(1)}, bf16[256,128]{1,0:T(8,128)(2,1)S(1)}, u32[]{:S(2)}, u32[]{:S(2)}) collective-permute-start(bf16[256,128]{1,0:T(8,128)(2,1)S(1)} %get-tuple-element.58), channel_id=1, source_target_pairs={{0,28},{4,24},{8,20},{12,16},{16,12},{20,8},{24,4},{28,0},{1,29},{... | collective-permute-start | bytes 196616 | tf_op jit(solution)/shard_map/ppermute | solution.py:360
  67.1 0.7 inner.3.refs_5_
  67.9 2.1 %boxed.3 = (bf16[256,128]{1,0:T(8,128)(2,1)S(1)}, bf16[256,128]{1,0:T(8,128)(2,1)S(1)}, bf16[256,128]{1,0:T(8,128)(2,1)S(1)}, bf16[256,128]{1,0:T(8,128)(2,1)S(1)}) custom-call(bf16[2176,128]{1,0:T(8,128)(2,1)S(1)} %collective-permute-done.7.refs_0_, bf16[2176,128]{1,0:T(8,128)(2,1)S(1)} %get-tuple-element.41.refs_1_, ...), custom_call_target="tpu_custom_call" | custom-call | flops 10000000 | bytes 6291456 | tf_op jit(solution)/shard_map/boxed/pallas_call | solution.py:292
  69.9 0.1 collective-permute-start.16
  70.0 0.0 collective-permute-done.19.refs_0_
  70.0 0.1 collective-permute-start.17
  70.1 2.5 %collective-permute-done.20.refs_1_ = bf16[256,128]{1,0:T(8,128)(2,1)S(1)} collective-permute-done((bf16[256,128]{1,0:T(8,128)(2,1)S(1)}, bf16[256,128]{1,0:T(8,128)(2,1)S(1)}, u32[]{:S(2)}, u32[]{:S(2)}) %collective-permute-start.20) | collective-permute-done | bytes 65568 | tf_op jit(solution)/shard_map/ppermute | solution.py:360
  72.6 0.9 %collective-permute-start.18 = (bf16[256,128]{1,0:T(8,128)(2,1)S(1)}, bf16[256,128]{1,0:T(8,128)(2,1)S(1)}, u32[]{:S(2)}, u32[]{:S(2)}) collective-permute-start(bf16[256,128]{1,0:T(8,128)(2,1)S(1)} %get-tuple-element.54), channel_id=1, source_target_pairs={{0,12},{4,8},{8,4},{12,0},{16,28},{20,24},{24,20},{28,16},{1,13},{... | collective-permute-start | bytes 196616 | tf_op jit(solution)/shard_map/ppermute | solution.py:360
  73.5 0.0 collective-permute-done.21.refs_2_
  73.5 0.0 collective-permute-done.22.refs_3_
  73.5 1.2 %join.2.refs_4_ = f32[1024,256]{1,0:T(8,128)} custom-call(bf16[256,128]{1,0:T(8,128)(2,1)S(1)} %collective-permute-done.19.refs_0_, bf16[256,128]{1,0:T(8,128)(2,1)S(1)} %collective-permute-done.20.refs_1_, bf16[256,128]{1,0:T(8,128)(2,1)S(1)} %collective-permute-done.21.refs_2_, bf16[256,128]{1,0:T(8,128)(2,1)S(1)} %collective-permute-done.22.refs_3_), custom_call_target="tpu_custom_call" | custom-call | flops 1000000000 | bytes 2097152 | tf_op jit(solution)/shard_map/join/pallas_call | solution.py:331
  74.8 0.0 collective-permute-done.16.refs_1_
  74.8 0.0 collective-permute-done.17.refs_2_
  74.8 1.7 %collective-permute-done.18.refs_3_ = bf16[256,128]{1,0:T(8,128)(2,1)S(1)} collective-permute-done((bf16[256,128]{1,0:T(8,128)(2,1)S(1)}, bf16[256,128]{1,0:T(8,128)(2,1)S(1)}, u32[]{:S(2)}, u32[]{:S(2)}) %collective-permute-start.18) | collective-permute-done | bytes 65568 | tf_op jit(solution)/shard_map/ppermute | solution.py:360
  76.5 1.2 %join.3 = f32[1024,256]{1,0:T(8,128)} custom-call(bf16[256,128]{1,0:T(8,128)(2,1)S(1)} %get-tuple-element.51.refs_0_, bf16[256,128]{1,0:T(8,128)(2,1)S(1)} %collective-permute-done.16.refs_1_, bf16[256,128]{1,0:T(8,128)(2,1)S(1)} %collective-permute-done.17.refs_2_, ...), custom_call_target="tpu_custom_call", output_to_operand_aliasing={{}: (4, {})} | custom-call | flops 1000000 | bytes 2097152 | tf_op jit(solution)/shard_map/join/pallas_call | solution.py:331
Async XLA Ops:
  0.0 29.6 %copy-start = (bf16[8,1024,128]{2,1,0:T(8,128)(2,1)S(1)}, bf16[8,1024,128]{2,1,0:T(8,128)(2,1)}, u32[]{:S(2)}) copy-start(bf16[8,1024,128]{2,1,0:T(8,128)(2,1)} %constant.2.clone.refs_8_) | copy-start | bytes 6291460
  3.8 6.8 %collective-permute-start = (bf16[528,128]{1,0:T(8,128)(2,1)S(1)}, bf16[528,128]{1,0:T(8,128)(2,1)S(1)}, u32[]{:S(2)}, u32[]{:S(2)}) collective-permute-start(bf16[528,128]{1,0:T(8,128)(2,1)S(1)} %get-tuple-element.33), channel_id=1, source_target_pairs={{0,4},{4,0},{8,12},{12,8},{16,20},{20,16},{24,28},{28,24},{1,5},{5... | collective-permute-start | bytes 405512 | tf_op jit(solution)/shard_map/ppermute | solution.py:360
  3.9 9.1 %collective-permute-start.5 = (bf16[528,128]{1,0:T(8,128)(2,1)S(1)}, bf16[528,128]{1,0:T(8,128)(2,1)S(1)}, u32[]{:S(2)}, u32[]{:S(2)}) collective-permute-start(bf16[528,128]{1,0:T(8,128)(2,1)S(1)} %get-tuple-element.38), channel_id=1, source_target_pairs={{0,24},{4,28},{8,16},{12,20},{16,8},{20,12},{24,0},{28,4},{1,25},{... | collective-permute-start | bytes 405512 | tf_op jit(solution)/shard_map/ppermute | solution.py:360
  8.7 10.9 %collective-permute-start.1 = (bf16[528,128]{1,0:T(8,128)(2,1)S(1)}, bf16[528,128]{1,0:T(8,128)(2,1)S(1)}, u32[]{:S(2)}, u32[]{:S(2)}) collective-permute-start(bf16[528,128]{1,0:T(8,128)(2,1)S(1)} %get-tuple-element.34), channel_id=1, source_target_pairs={{0,8},{4,12},{8,0},{12,4},{16,24},{20,28},{24,16},{28,20},{1,9},{5... | collective-permute-start | bytes 405512 | tf_op jit(solution)/shard_map/ppermute | solution.py:360
  8.7 13.8 %collective-permute-start.2 = (bf16[528,128]{1,0:T(8,128)(2,1)S(1)}, bf16[528,128]{1,0:T(8,128)(2,1)S(1)}, u32[]{:S(2)}, u32[]{:S(2)}) collective-permute-start(bf16[528,128]{1,0:T(8,128)(2,1)S(1)} %get-tuple-element.35), channel_id=1, source_target_pairs={{0,12},{4,8},{8,4},{12,0},{16,28},{20,24},{24,20},{28,16},{1,13},{... | collective-permute-start | bytes 405512 | tf_op jit(solution)/shard_map/ppermute | solution.py:360
  10.6 11.9 %collective-permute-start.3 = (bf16[528,128]{1,0:T(8,128)(2,1)S(1)}, bf16[528,128]{1,0:T(8,128)(2,1)S(1)}, u32[]{:S(2)}, u32[]{:S(2)}) collective-permute-start(bf16[528,128]{1,0:T(8,128)(2,1)S(1)} %get-tuple-element.36), channel_id=1, source_target_pairs={{0,16},{4,20},{8,24},{12,28},{16,0},{20,4},{24,8},{28,12},{1,17},{... | collective-permute-start | bytes 405512 | tf_op jit(solution)/shard_map/ppermute | solution.py:360
  10.6 18.9 %collective-permute-start.4 = (bf16[528,128]{1,0:T(8,128)(2,1)S(1)}, bf16[528,128]{1,0:T(8,128)(2,1)S(1)}, u32[]{:S(2)}, u32[]{:S(2)}) collective-permute-start(bf16[528,128]{1,0:T(8,128)(2,1)S(1)} %get-tuple-element.37), channel_id=1, source_target_pairs={{0,20},{4,16},{8,28},{12,24},{16,4},{20,0},{24,12},{28,8},{1,21},{... | collective-permute-start | bytes 405512 | tf_op jit(solution)/shard_map/ppermute | solution.py:360
  13.1 16.5 %collective-permute-start.6 = (bf16[528,128]{1,0:T(8,128)(2,1)S(1)}, bf16[528,128]{1,0:T(8,128)(2,1)S(1)}, u32[]{:S(2)}, u32[]{:S(2)}) collective-permute-start(bf16[528,128]{1,0:T(8,128)(2,1)S(1)} %get-tuple-element.39), channel_id=1, source_target_pairs={{0,28},{4,24},{8,20},{12,16},{16,12},{20,8},{24,4},{28,0},{1,29},{... | collective-permute-start | bytes 405512 | tf_op jit(solution)/shard_map/ppermute | solution.py:360
  19.5 16.7 %collective-permute-start.9 = (bf16[512,128]{1,0:T(8,128)(2,1)S(1)}, bf16[512,128]{1,0:T(8,128)(2,1)S(1)}, u32[]{:S(2)}, u32[]{:S(2)}) collective-permute-start(bf16[512,128]{1,0:T(8,128)(2,1)S(1)} %get-tuple-element.43), channel_id=1, source_target_pairs={{0,4},{4,0},{8,12},{12,8},{16,20},{20,16},{24,28},{28,24},{1,5},{5... | collective-permute-start | bytes 393224 | tf_op jit(solution)/shard_map/ppermute | solution.py:360
  22.5 15.6 %collective-permute-start.10 = (bf16[512,128]{1,0:T(8,128)(2,1)S(1)}, bf16[512,128]{1,0:T(8,128)(2,1)S(1)}, u32[]{:S(2)}, u32[]{:S(2)}) collective-permute-start(bf16[512,128]{1,0:T(8,128)(2,1)S(1)} %get-tuple-element.44), channel_id=1, source_target_pairs={{0,8},{4,12},{8,0},{12,4},{16,24},{20,28},{24,16},{28,20},{1,9},{5... | collective-permute-start | bytes 393224 | tf_op jit(solution)/shard_map/ppermute | solution.py:360
  22.5 16.4 %collective-permute-start.11 = (bf16[512,128]{1,0:T(8,128)(2,1)S(1)}, bf16[512,128]{1,0:T(8,128)(2,1)S(1)}, u32[]{:S(2)}, u32[]{:S(2)}) collective-permute-start(bf16[512,128]{1,0:T(8,128)(2,1)S(1)} %get-tuple-element.45), channel_id=1, source_target_pairs={{0,12},{4,8},{8,4},{12,0},{16,28},{20,24},{24,20},{28,16},{1,13},{... | collective-permute-start | bytes 393224 | tf_op jit(solution)/shard_map/ppermute | solution.py:360
  29.6 12.5 %collective-permute-start.12 = (bf16[512,128]{1,0:T(8,128)(2,1)S(1)}, bf16[512,128]{1,0:T(8,128)(2,1)S(1)}, u32[]{:S(2)}, u32[]{:S(2)}) collective-permute-start(bf16[512,128]{1,0:T(8,128)(2,1)S(1)} %get-tuple-element.46), channel_id=1, source_target_pairs={{0,16},{4,20},{8,24},{12,28},{16,0},{20,4},{24,8},{28,12},{1,17},{... | collective-permute-start | bytes 393224 | tf_op jit(solution)/shard_map/ppermute | solution.py:360
  31.4 25.5 %collective-permute-start.7 = (bf16[2176,128]{1,0:T(8,128)(2,1)S(1)}, bf16[2176,128]{1,0:T(8,128)(2,1)S(1)}, u32[]{:S(2)}, u32[]{:S(2)}) collective-permute-start(bf16[2176,128]{1,0:T(8,128)(2,1)S(1)} %get-tuple-element.40.refs_2_), channel_id=1, source_target_pairs={{0,4},{4,8},{8,12},{12,13},{13,9},{9,5},{5,1},{1,2},{2,6},{6,10},{... | collective-permute-start | bytes 1671176 | tf_op jit(solution)/shard_map/ppermute | solution.py:377
  36.2 20.8 %collective-permute-start.8 = (bf16[2176,128]{1,0:T(8,128)(2,1)S(1)}, bf16[2176,128]{1,0:T(8,128)(2,1)S(1)}, u32[]{:S(2)}, u32[]{:S(2)}) collective-permute-start(bf16[2176,128]{1,0:T(8,128)(2,1)S(1)} %get-tuple-element.41.refs_1_), channel_id=1, source_target_pairs={{4,0},{8,4},{12,8},{13,12},{9,13},{5,9},{1,5},{2,1},{6,2},{10,6},{... | collective-permute-start | bytes 1671176 | tf_op jit(solution)/shard_map/ppermute | solution.py:378
  38.1 9.2 %collective-permute-start.13 = (bf16[512,128]{1,0:T(8,128)(2,1)S(1)}, bf16[512,128]{1,0:T(8,128)(2,1)S(1)}, u32[]{:S(2)}, u32[]{:S(2)}) collective-permute-start(bf16[512,128]{1,0:T(8,128)(2,1)S(1)} %get-tuple-element.47), channel_id=1, source_target_pairs={{0,20},{4,16},{8,28},{12,24},{16,4},{20,0},{24,12},{28,8},{1,21},{... | collective-permute-start | bytes 393224 | tf_op jit(solution)/shard_map/ppermute | solution.py:360
  38.9 10.8 %collective-permute-start.14 = (bf16[512,128]{1,0:T(8,128)(2,1)S(1)}, bf16[512,128]{1,0:T(8,128)(2,1)S(1)}, u32[]{:S(2)}, u32[]{:S(2)}) collective-permute-start(bf16[512,128]{1,0:T(8,128)(2,1)S(1)} %get-tuple-element.48), channel_id=1, source_target_pairs={{0,24},{4,28},{8,16},{12,20},{16,8},{20,12},{24,0},{28,4},{1,25},{... | collective-permute-start | bytes 393224 | tf_op jit(solution)/shard_map/ppermute | solution.py:360
  42.1 14.2 %collective-permute-start.15 = (bf16[512,128]{1,0:T(8,128)(2,1)S(1)}, bf16[512,128]{1,0:T(8,128)(2,1)S(1)}, u32[]{:S(2)}, u32[]{:S(2)}) collective-permute-start(bf16[512,128]{1,0:T(8,128)(2,1)S(1)} %get-tuple-element.49), channel_id=1, source_target_pairs={{0,28},{4,24},{8,20},{12,16},{16,12},{20,8},{24,4},{28,0},{1,29},{... | collective-permute-start | bytes 393224 | tf_op jit(solution)/shard_map/ppermute | solution.py:360
  59.6 10.4 %collective-permute-start.19 = (bf16[256,128]{1,0:T(8,128)(2,1)S(1)}, bf16[256,128]{1,0:T(8,128)(2,1)S(1)}, u32[]{:S(2)}, u32[]{:S(2)}) collective-permute-start(bf16[256,128]{1,0:T(8,128)(2,1)S(1)} %get-tuple-element.55), channel_id=1, source_target_pairs={{0,16},{4,20},{8,24},{12,28},{16,0},{20,4},{24,8},{28,12},{1,17},{... | collective-permute-start | bytes 196616 | tf_op jit(solution)/shard_map/ppermute | solution.py:360
  62.5 10.2 %collective-permute-start.20 = (bf16[256,128]{1,0:T(8,128)(2,1)S(1)}, bf16[256,128]{1,0:T(8,128)(2,1)S(1)}, u32[]{:S(2)}, u32[]{:S(2)}) collective-permute-start(bf16[256,128]{1,0:T(8,128)(2,1)S(1)} %get-tuple-element.56), channel_id=1, source_target_pairs={{0,20},{4,16},{8,28},{12,24},{16,4},{20,0},{24,12},{28,8},{1,21},{... | collective-permute-start | bytes 196616 | tf_op jit(solution)/shard_map/ppermute | solution.py:360
  63.4 10.2 %collective-permute-start.21 = (bf16[256,128]{1,0:T(8,128)(2,1)S(1)}, bf16[256,128]{1,0:T(8,128)(2,1)S(1)}, u32[]{:S(2)}, u32[]{:S(2)}) collective-permute-start(bf16[256,128]{1,0:T(8,128)(2,1)S(1)} %get-tuple-element.57), channel_id=1, source_target_pairs={{0,24},{4,28},{8,16},{12,20},{16,8},{20,12},{24,0},{28,4},{1,25},{... | collective-permute-start | bytes 196616 | tf_op jit(solution)/shard_map/ppermute | solution.py:360
  63.5 10.1 %collective-permute-start.22 = (bf16[256,128]{1,0:T(8,128)(2,1)S(1)}, bf16[256,128]{1,0:T(8,128)(2,1)S(1)}, u32[]{:S(2)}, u32[]{:S(2)}) collective-permute-start(bf16[256,128]{1,0:T(8,128)(2,1)S(1)} %get-tuple-element.58), channel_id=1, source_target_pairs={{0,28},{4,24},{8,20},{12,16},{16,12},{20,8},{24,4},{28,0},{1,29},{... | collective-permute-start | bytes 196616 | tf_op jit(solution)/shard_map/ppermute | solution.py:360
  69.9 4.8 %collective-permute-start.16 = (bf16[256,128]{1,0:T(8,128)(2,1)S(1)}, bf16[256,128]{1,0:T(8,128)(2,1)S(1)}, u32[]{:S(2)}, u32[]{:S(2)}) collective-permute-start(bf16[256,128]{1,0:T(8,128)(2,1)S(1)} %get-tuple-element.52), channel_id=1, source_target_pairs={{0,4},{4,0},{8,12},{12,8},{16,20},{20,16},{24,28},{28,24},{1,5},{5... | collective-permute-start | bytes 196616 | tf_op jit(solution)/shard_map/ppermute | solution.py:360
  70.0 4.8 %collective-permute-start.17 = (bf16[256,128]{1,0:T(8,128)(2,1)S(1)}, bf16[256,128]{1,0:T(8,128)(2,1)S(1)}, u32[]{:S(2)}, u32[]{:S(2)}) collective-permute-start(bf16[256,128]{1,0:T(8,128)(2,1)S(1)} %get-tuple-element.53), channel_id=1, source_target_pairs={{0,8},{4,12},{8,0},{12,4},{16,24},{20,28},{24,16},{28,20},{1,9},{5... | collective-permute-start | bytes 196616 | tf_op jit(solution)/shard_map/ppermute | solution.py:360
  72.6 3.9 %collective-permute-start.18 = (bf16[256,128]{1,0:T(8,128)(2,1)S(1)}, bf16[256,128]{1,0:T(8,128)(2,1)S(1)}, u32[]{:S(2)}, u32[]{:S(2)}) collective-permute-start(bf16[256,128]{1,0:T(8,128)(2,1)S(1)} %get-tuple-element.54), channel_id=1, source_target_pairs={{0,12},{4,8},{8,4},{12,0},{16,28},{20,24},{24,20},{28,16},{1,13},{... | collective-permute-start | bytes 196616 | tf_op jit(solution)/shard_map/ppermute | solution.py:360

commit v7 on v6

--- a/solution.py
+++ b/solution.py
@@ -247,7 +247,7 @@
             pair = [x + y for x, y in zip(here, after)]
             here = after
 
-    @pl.loop(0, span // STEP, unroll=4)
+    @pl.loop(0, span // STEP, unroll=8)
     def _(i):
         z = pl.multiple_of(i * STEP, STEP)
         over_rows(pl.multiple_of(base + z, STEP), pl.multiple_of(z + STEP, STEP), z)
@@ -264,7 +264,7 @@
     def deep(x):
         return x[0] + x[1] + x[2]
 
-    @pl.loop(0, span // STEP, unroll=8)
+    @pl.loop(0, span // STEP, unroll=16)
     def _(i):
         z = pl.multiple_of(i * STEP, STEP)
         rim = [deep([edge[t, pl.ds(base + z + j, STEP), :] for j in (7, 8, 9)]) for t in range(3)]

time: 77.9 us -> 78.1 us (level)
  no operation moved by 1% of the time
where the time goes in v7:
time: 78.1 us; the launch traced here: 77.9 us
  starting transfers between devices  36.4 us (47%)
  waiting for transfers between devices  25.1 us (32%)
  Pallas kernels  16.1 us (21%)
    ppermute x21, starting transfers between devices, exchange(): out[s] = lax.ppermute(pieces[s], 'ka', [(i, i ^ s) for i in range(n)])  29.6 us
    ppermute x21, waiting for transfers between devices, exchange(): out[s] = lax.ppermute(pieces[s], 'ka', [(i, i ^ s) for i in range(n)])  25.1 us
    pallas_call x2, Pallas kernels, split(): pl.pallas_call(functools.partial(split_kernel, n, rows, kl, rb, group, ed...  5.96 us
    ppermute x1, starting transfers between devices, body(): above = lax.ppermute(bottom, ('ka', 'row'), down)  4.74 us
    pallas_call x2, Pallas kernels, boxed(): pl.pallas_call(functools.partial(box_kernel, n, kl, rb, far), out_shape=[...  4.37 us
    pallas_call x2, Pallas kernels, join(): pl.pallas_call(functools.partial(join_kernel, n, rows, rb, far), out_shap...  2.39 us
    ppermute x1, starting transfers between devices, body(): below = lax.ppermute(top, ('ka', 'row'), [(j, i) for i, j in down])  2.1 us
    pallas_call x1, Pallas kernels, outer(): pl.pallas_call(functools.partial(outer_kernel, n, kl, first), out_shape=[...  1.86 us
  transfers between devices with their start and end apart: 23, of which 8 were waited for; matrix products, arithmetic and copies ran while one was open for 0% of the time, Pallas kernels for 11%

profile of v7, /device:TPU:1, one launch (start us, length us, event | category | flops | bytes accessed | tf_op | source)
XLA Modules:
  0.0 77.9 jit_solution(8043604600711327514)
XLA Ops:
  0.0 0.0 copy-start
  0.0 3.8 %split.2 = (bf16[528,128]{1,0:T(8,128)(2,1)S(1)}, bf16[528,128]{1,0:T(8,128)(2,1)S(1)}, bf16[528,128]{1,0:T(8,128)(2,1)S(1)}, bf16[528,128]{1,0:T(8,128)(2,1)S(1...) custom-call(bf16[4096,256]{1,0:T(8,128)(2,1)} %bitcast.2), custom_call_target="tpu_custom_call" | custom-call | flops 1000000 | bytes 4194304 | tf_op jit(solution)/shard_map/split/pallas_call | solution.py:80
  3.8 0.1 collective-permute-start
  3.9 4.7 %collective-permute-start.5 = (bf16[528,128]{1,0:T(8,128)(2,1)S(1)}, bf16[528,128]{1,0:T(8,128)(2,1)S(1)}, u32[]{:S(2)}, u32[]{:S(2)}) collective-permute-start(bf16[528,128]{1,0:T(8,128)(2,1)S(1)} %get-tuple-element.38), channel_id=1, source_target_pairs={{0,24},{4,28},{8,16},{12,20},{16,8},{20,12},{24,0},{28,4},{1,25},{... | collective-permute-start | bytes 405512 | tf_op jit(solution)/shard_map/ppermute | solution.py:360
  8.7 0.0 collective-permute-start.1
  8.7 2.0 %collective-permute-start.2 = (bf16[528,128]{1,0:T(8,128)(2,1)S(1)}, bf16[528,128]{1,0:T(8,128)(2,1)S(1)}, u32[]{:S(2)}, u32[]{:S(2)}) collective-permute-start(bf16[528,128]{1,0:T(8,128)(2,1)S(1)} %get-tuple-element.35), channel_id=1, source_target_pairs={{0,12},{4,8},{8,4},{12,0},{16,28},{20,24},{24,20},{28,16},{1,13},{... | collective-permute-start | bytes 405512 | tf_op jit(solution)/shard_map/ppermute | solution.py:360
  10.6 0.0 collective-permute-start.3
  10.6 0.0 collective-permute-done.refs_1_
  10.6 2.4 %collective-permute-start.4 = (bf16[528,128]{1,0:T(8,128)(2,1)S(1)}, bf16[528,128]{1,0:T(8,128)(2,1)S(1)}, u32[]{:S(2)}, u32[]{:S(2)}) collective-permute-start(bf16[528,128]{1,0:T(8,128)(2,1)S(1)} %get-tuple-element.37), channel_id=1, source_target_pairs={{0,20},{4,16},{8,28},{12,24},{16,4},{20,0},{24,12},{28,8},{1,21},{... | collective-permute-start | bytes 405512 | tf_op jit(solution)/shard_map/ppermute | solution.py:360
  13.1 0.0 collective-permute-done.5.refs_6_.refs_0_
  13.1 3.8 %collective-permute-start.6 = (bf16[528,128]{1,0:T(8,128)(2,1)S(1)}, bf16[528,128]{1,0:T(8,128)(2,1)S(1)}, u32[]{:S(2)}, u32[]{:S(2)}) collective-permute-start(bf16[528,128]{1,0:T(8,128)(2,1)S(1)} %get-tuple-element.39), channel_id=1, source_target_pairs={{0,28},{4,24},{8,20},{12,16},{16,12},{20,8},{24,4},{28,0},{1,29},{... | collective-permute-start | bytes 405512 | tf_op jit(solution)/shard_map/ppermute | solution.py:360
  16.8 2.2 %split.3 = (bf16[512,128]{1,0:T(8,128)(2,1)S(1)}, bf16[512,128]{1,0:T(8,128)(2,1)S(1)}, bf16[512,128]{1,0:T(8,128)(2,1)S(1)}, bf16[512,128]{1,0:T(8,128)(2,1)S(1...) custom-call(bf16[4096,256]{1,0:T(8,128)(2,1)} %bitcast.3, ...), custom_call_target="tpu_custom_call" | custom-call | flops 1000000 | bytes 4194304 | tf_op jit(solution)/shard_map/split/pallas_call | solution.py:80
  19.0 0.5 collective-permute-done.1.refs_2_
  19.5 0.5 collective-permute-start.9
  20.1 2.4 %collective-permute-done.2.refs_3_ = bf16[528,128]{1,0:T(8,128)(2,1)S(1)} collective-permute-done((bf16[528,128]{1,0:T(8,128)(2,1)S(1)}, bf16[528,128]{1,0:T(8,128)(2,1)S(1)}, u32[]{:S(2)}, u32[]{:S(2)}) %collective-permute-start.2) | collective-permute-done | bytes 135200 | tf_op jit(solution)/shard_map/ppermute | solution.py:360
  22.5 0.0 collective-permute-start.10
  22.5 0.0 collective-permute-done.3.refs_4_
  22.5 1.9 %collective-permute-start.11 = (bf16[512,128]{1,0:T(8,128)(2,1)S(1)}, bf16[512,128]{1,0:T(8,128)(2,1)S(1)}, u32[]{:S(2)}, u32[]{:S(2)}) collective-permute-start(bf16[512,128]{1,0:T(8,128)(2,1)S(1)} %get-tuple-element.45), channel_id=1, source_target_pairs={{0,12},{4,8},{8,4},{12,0},{16,28},{20,24},{24,20},{28,16},{1,13},{... | collective-permute-start | bytes 393224 | tf_op jit(solution)/shard_map/ppermute | solution.py:360
  24.5 5.1 %collective-permute-done.4.refs_5_ = bf16[528,128]{1,0:T(8,128)(2,1)S(1)} collective-permute-done((bf16[528,128]{1,0:T(8,128)(2,1)S(1)}, bf16[528,128]{1,0:T(8,128)(2,1)S(1)}, u32[]{:S(2)}, u32[]{:S(2)}) %collective-permute-start.4) | collective-permute-done | bytes 135200 | tf_op jit(solution)/shard_map/ppermute | solution.py:360
  29.6 0.0 collective-permute-start.12
  29.6 0.0 collective-permute-done.6.refs_7_
  29.6 0.0 copy-done
  29.6 1.9 %outer.1 = (bf16[2176,128]{1,0:T(8,128)(2,1)S(1)}, bf16[2176,128]{1,0:T(8,128)(2,1)S(1)}) custom-call(bf16[528,128]{1,0:T(8,128)(2,1)S(1)} %get-tuple-element.32.refs_0_, bf16[528,128]{1,0:T(8,128)(2,1)S(1)} %collective-permute-done.refs_1_, bf16[528,128]{1,0:T(8,128)(2,1)S(1)} %collective-permute-done.1.refs_2_, ...), custom_call_target="tpu_custom_call" | custom-call | flops 1610612736 | bytes 4194304 | tf_op jit(solution)/shard_map/outer/pallas_call | solution.py:152
  31.4 4.7 %collective-permute-start.7 = (bf16[2176,128]{1,0:T(8,128)(2,1)S(1)}, bf16[2176,128]{1,0:T(8,128)(2,1)S(1)}, u32[]{:S(2)}, u32[]{:S(2)}) collective-permute-start(bf16[2176,128]{1,0:T(8,128)(2,1)S(1)} %get-tuple-element.40.refs_2_), channel_id=1, source_target_pairs={{0,4},{4,8},{8,12},{12,13},{13,9},{9,5},{5,1},{1,2},{2,6},{6,10},{... | collective-permute-start | bytes 1671176 | tf_op jit(solution)/shard_map/ppermute | solution.py:377
  36.2 0.0 collective-permute-done.9.refs_1_
  36.2 2.1 %collective-permute-start.8 = (bf16[2176,128]{1,0:T(8,128)(2,1)S(1)}, bf16[2176,128]{1,0:T(8,128)(2,1)S(1)}, u32[]{:S(2)}, u32[]{:S(2)}) collective-permute-start(bf16[2176,128]{1,0:T(8,128)(2,1)S(1)} %get-tuple-element.41.refs_1_), channel_id=1, source_target_pairs={{4,0},{8,4},{12,8},{13,12},{9,13},{5,9},{1,5},{2,1},{6,2},{10,6},{... | collective-permute-start | bytes 1671176 | tf_op jit(solution)/shard_map/ppermute | solution.py:378
  38.3 0.0 collective-permute-done.10.refs_2_
  38.3 0.8 collective-permute-start.13
  39.1 0.0 collective-permute-done.11.refs_3_
  39.1 3.1 %collective-permute-start.14 = (bf16[512,128]{1,0:T(8,128)(2,1)S(1)}, bf16[512,128]{1,0:T(8,128)(2,1)S(1)}, u32[]{:S(2)}, u32[]{:S(2)}) collective-permute-start(bf16[512,128]{1,0:T(8,128)(2,1)S(1)} %get-tuple-element.48), channel_id=1, source_target_pairs={{0,24},{4,28},{8,16},{12,20},{16,8},{20,12},{24,0},{28,4},{1,25},{... | collective-permute-start | bytes 393224 | tf_op jit(solution)/shard_map/ppermute | solution.py:360
  42.2 0.0 collective-permute-done.12.refs_4_
  42.2 1.4 %collective-permute-start.15 = (bf16[512,128]{1,0:T(8,128)(2,1)S(1)}, bf16[512,128]{1,0:T(8,128)(2,1)S(1)}, u32[]{:S(2)}, u32[]{:S(2)}) collective-permute-start(bf16[512,128]{1,0:T(8,128)(2,1)S(1)} %get-tuple-element.49), channel_id=1, source_target_pairs={{0,28},{4,24},{8,20},{12,16},{16,12},{20,8},{24,4},{28,0},{1,29},{... | collective-permute-start | bytes 393224 | tf_op jit(solution)/shard_map/ppermute | solution.py:360
  43.6 3.6 %collective-permute-done.13.refs_5_ = bf16[512,128]{1,0:T(8,128)(2,1)S(1)} collective-permute-done((bf16[512,128]{1,0:T(8,128)(2,1)S(1)}, bf16[512,128]{1,0:T(8,128)(2,1)S(1)}, u32[]{:S(2)}, u32[]{:S(2)}) %collective-permute-start.13) | collective-permute-done | bytes 131104 | tf_op jit(solution)/shard_map/ppermute | solution.py:360
  47.2 2.5 %collective-permute-done.14.refs_6_ = bf16[512,128]{1,0:T(8,128)(2,1)S(1)} collective-permute-done((bf16[512,128]{1,0:T(8,128)(2,1)S(1)}, bf16[512,128]{1,0:T(8,128)(2,1)S(1)}, u32[]{:S(2)}, u32[]{:S(2)}) %collective-permute-start.14) | collective-permute-done | bytes 131104 | tf_op jit(solution)/shard_map/ppermute | solution.py:360
  49.7 6.5 %collective-permute-done.15.refs_7_ = bf16[512,128]{1,0:T(8,128)(2,1)S(1)} collective-permute-done((bf16[512,128]{1,0:T(8,128)(2,1)S(1)}, bf16[512,128]{1,0:T(8,128)(2,1)S(1)}, u32[]{:S(2)}, u32[]{:S(2)}) %collective-permute-start.15) | collective-permute-done | bytes 131104 | tf_op jit(solution)/shard_map/ppermute | solution.py:360
  56.2 0.8 inner.2.refs_4_
  57.0 0.0 collective-permute-done.7.refs_0_
  57.0 0.0 collective-permute-done.8.refs_3_
  57.0 2.5 %boxed.2 = (bf16[256,128]{1,0:T(8,128)(2,1)S(1)}, bf16[256,128]{1,0:T(8,128)(2,1)S(1)}, bf16[256,128]{1,0:T(8,128)(2,1)S(1)}, bf16[256,128]{1,0:T(8,128)(2,1)S(1)}, f32[3,528,128]{2,1,0:T(8,128)S(1)}) custom-call(bf16[2176,128]{1,0:T(8,128)(2,1)S(1)} %collective-permute-done.7.refs_0_, bf16[2176,128]{1,0:T(8,128)(2,1)S(1)} %get-tuple-element.41.refs_1_, ...), custom_call_target="tpu_custom_call" | custom-call | flops 10000000 | bytes 6291456 | tf_op jit(solution)/shard_map/boxed/pallas_call | solution.py:292
  59.5 3.0 %collective-permute-start.19 = (bf16[256,128]{1,0:T(8,128)(2,1)S(1)}, bf16[256,128]{1,0:T(8,128)(2,1)S(1)}, u32[]{:S(2)}, u32[]{:S(2)}) collective-permute-start(bf16[256,128]{1,0:T(8,128)(2,1)S(1)} %get-tuple-element.55), channel_id=1, source_target_pairs={{0,16},{4,20},{8,24},{12,28},{16,0},{20,4},{24,8},{28,12},{1,17},{... | collective-permute-start | bytes 196616 | tf_op jit(solution)/shard_map/ppermute | solution.py:360
  62.5 0.9 %collective-permute-start.20 = (bf16[256,128]{1,0:T(8,128)(2,1)S(1)}, bf16[256,128]{1,0:T(8,128)(2,1)S(1)}, u32[]{:S(2)}, u32[]{:S(2)}) collective-permute-start(bf16[256,128]{1,0:T(8,128)(2,1)S(1)} %get-tuple-element.56), channel_id=1, source_target_pairs={{0,20},{4,16},{8,28},{12,24},{16,4},{20,0},{24,12},{28,8},{1,21},{... | collective-permute-start | bytes 196616 | tf_op jit(solution)/shard_map/ppermute | solution.py:360
  63.4 0.1 collective-permute-start.21
  63.5 3.6 %collective-permute-start.22 = (bf16[256,128]{1,0:T(8,128)(2,1)S(1)}, bf16[256,128]{1,0:T(8,128)(2,1)S(1)}, u32[]{:S(2)}, u32[]{:S(2)}) collective-permute-start(bf16[256,128]{1,0:T(8,128)(2,1)S(1)} %get-tuple-element.58), channel_id=1, source_target_pairs={{0,28},{4,24},{8,20},{12,16},{16,12},{20,8},{24,4},{28,0},{1,29},{... | collective-permute-start | bytes 196616 | tf_op jit(solution)/shard_map/ppermute | solution.py:360
  67.2 0.7 inner.3.refs_5_
  67.9 1.9 %boxed.3 = (bf16[256,128]{1,0:T(8,128)(2,1)S(1)}, bf16[256,128]{1,0:T(8,128)(2,1)S(1)}, bf16[256,128]{1,0:T(8,128)(2,1)S(1)}, bf16[256,128]{1,0:T(8,128)(2,1)S(1)}) custom-call(bf16[2176,128]{1,0:T(8,128)(2,1)S(1)} %collective-permute-done.7.refs_0_, bf16[2176,128]{1,0:T(8,128)(2,1)S(1)} %get-tuple-element.41.refs_1_, ...), custom_call_target="tpu_custom_call" | custom-call | flops 10000000 | bytes 6291456 | tf_op jit(solution)/shard_map/boxed/pallas_call | solution.py:292
  69.8 0.1 collective-permute-start.16
  69.9 0.0 collective-permute-done.19.refs_0_
  69.9 0.1 collective-permute-start.17
  70.0 2.7 %collective-permute-done.20.refs_1_ = bf16[256,128]{1,0:T(8,128)(2,1)S(1)} collective-permute-done((bf16[256,128]{1,0:T(8,128)(2,1)S(1)}, bf16[256,128]{1,0:T(8,128)(2,1)S(1)}, u32[]{:S(2)}, u32[]{:S(2)}) %collective-permute-start.20) | collective-permute-done | bytes 65568 | tf_op jit(solution)/shard_map/ppermute | solution.py:360
  72.7 0.9 %collective-permute-start.18 = (bf16[256,128]{1,0:T(8,128)(2,1)S(1)}, bf16[256,128]{1,0:T(8,128)(2,1)S(1)}, u32[]{:S(2)}, u32[]{:S(2)}) collective-permute-start(bf16[256,128]{1,0:T(8,128)(2,1)S(1)} %get-tuple-element.54), channel_id=1, source_target_pairs={{0,12},{4,8},{8,4},{12,0},{16,28},{20,24},{24,20},{28,16},{1,13},{... | collective-permute-start | bytes 196616 | tf_op jit(solution)/shard_map/ppermute | solution.py:360
  73.6 0.0 collective-permute-done.21.refs_2_
  73.6 0.0 collective-permute-done.22.refs_3_
  73.6 1.2 %join.2.refs_4_ = f32[1024,256]{1,0:T(8,128)} custom-call(bf16[256,128]{1,0:T(8,128)(2,1)S(1)} %collective-permute-done.19.refs_0_, bf16[256,128]{1,0:T(8,128)(2,1)S(1)} %collective-permute-done.20.refs_1_, bf16[256,128]{1,0:T(8,128)(2,1)S(1)} %collective-permute-done.21.refs_2_, bf16[256,128]{1,0:T(8,128)(2,1)S(1)} %collective-permute-done.22.refs_3_), custom_call_target="tpu_custom_call" | custom-call | flops 1000000000 | bytes 2097152 | tf_op jit(solution)/shard_map/join/pallas_call | solution.py:331
  74.8 0.0 collective-permute-done.16.refs_1_
  74.8 0.0 collective-permute-done.17.refs_2_
  74.8 1.7 %collective-permute-done.18.refs_3_ = bf16[256,128]{1,0:T(8,128)(2,1)S(1)} collective-permute-done((bf16[256,128]{1,0:T(8,128)(2,1)S(1)}, bf16[256,128]{1,0:T(8,128)(2,1)S(1)}, u32[]{:S(2)}, u32[]{:S(2)}) %collective-permute-start.18) | collective-permute-done | bytes 65568 | tf_op jit(solution)/shard_map/ppermute | solution.py:360
  76.6 1.2 %join.3 = f32[1024,256]{1,0:T(8,128)} custom-call(bf16[256,128]{1,0:T(8,128)(2,1)S(1)} %get-tuple-element.51.refs_0_, bf16[256,128]{1,0:T(8,128)(2,1)S(1)} %collective-permute-done.16.refs_1_, bf16[256,128]{1,0:T(8,128)(2,1)S(1)} %collective-permute-done.17.refs_2_, ...), custom_call_target="tpu_custom_call", output_to_operand_aliasing={{}: (4, {})} | custom-call | flops 1000000 | bytes 2097152 | tf_op jit(solution)/shard_map/join/pallas_call | solution.py:331
Async XLA Ops:
  0.0 29.6 %copy-start = (bf16[8,1024,128]{2,1,0:T(8,128)(2,1)S(1)}, bf16[8,1024,128]{2,1,0:T(8,128)(2,1)}, u32[]{:S(2)}) copy-start(bf16[8,1024,128]{2,1,0:T(8,128)(2,1)} %constant.2.clone.refs_8_) | copy-start | bytes 6291460
  3.8 6.8 %collective-permute-start = (bf16[528,128]{1,0:T(8,128)(2,1)S(1)}, bf16[528,128]{1,0:T(8,128)(2,1)S(1)}, u32[]{:S(2)}, u32[]{:S(2)}) collective-permute-start(bf16[528,128]{1,0:T(8,128)(2,1)S(1)} %get-tuple-element.33), channel_id=1, source_target_pairs={{0,4},{4,0},{8,12},{12,8},{16,20},{20,16},{24,28},{28,24},{1,5},{5... | collective-permute-start | bytes 405512 | tf_op jit(solution)/shard_map/ppermute | solution.py:360
  3.9 9.1 %collective-permute-start.5 = (bf16[528,128]{1,0:T(8,128)(2,1)S(1)}, bf16[528,128]{1,0:T(8,128)(2,1)S(1)}, u32[]{:S(2)}, u32[]{:S(2)}) collective-permute-start(bf16[528,128]{1,0:T(8,128)(2,1)S(1)} %get-tuple-element.38), channel_id=1, source_target_pairs={{0,24},{4,28},{8,16},{12,20},{16,8},{20,12},{24,0},{28,4},{1,25},{... | collective-permute-start | bytes 405512 | tf_op jit(solution)/shard_map/ppermute | solution.py:360
  8.7 10.9 %collective-permute-start.1 = (bf16[528,128]{1,0:T(8,128)(2,1)S(1)}, bf16[528,128]{1,0:T(8,128)(2,1)S(1)}, u32[]{:S(2)}, u32[]{:S(2)}) collective-permute-start(bf16[528,128]{1,0:T(8,128)(2,1)S(1)} %get-tuple-element.34), channel_id=1, source_target_pairs={{0,8},{4,12},{8,0},{12,4},{16,24},{20,28},{24,16},{28,20},{1,9},{5... | collective-permute-start | bytes 405512 | tf_op jit(solution)/shard_map/ppermute | solution.py:360
  8.7 13.8 %collective-permute-start.2 = (bf16[528,128]{1,0:T(8,128)(2,1)S(1)}, bf16[528,128]{1,0:T(8,128)(2,1)S(1)}, u32[]{:S(2)}, u32[]{:S(2)}) collective-permute-start(bf16[528,128]{1,0:T(8,128)(2,1)S(1)} %get-tuple-element.35), channel_id=1, source_target_pairs={{0,12},{4,8},{8,4},{12,0},{16,28},{20,24},{24,20},{28,16},{1,13},{... | collective-permute-start | bytes 405512 | tf_op jit(solution)/shard_map/ppermute | solution.py:360
  10.6 11.9 %collective-permute-start.3 = (bf16[528,128]{1,0:T(8,128)(2,1)S(1)}, bf16[528,128]{1,0:T(8,128)(2,1)S(1)}, u32[]{:S(2)}, u32[]{:S(2)}) collective-permute-start(bf16[528,128]{1,0:T(8,128)(2,1)S(1)} %get-tuple-element.36), channel_id=1, source_target_pairs={{0,16},{4,20},{8,24},{12,28},{16,0},{20,4},{24,8},{28,12},{1,17},{... | collective-permute-start | bytes 405512 | tf_op jit(solution)/shard_map/ppermute | solution.py:360
  10.6 18.9 %collective-permute-start.4 = (bf16[528,128]{1,0:T(8,128)(2,1)S(1)}, bf16[528,128]{1,0:T(8,128)(2,1)S(1)}, u32[]{:S(2)}, u32[]{:S(2)}) collective-permute-start(bf16[528,128]{1,0:T(8,128)(2,1)S(1)} %get-tuple-element.37), channel_id=1, source_target_pairs={{0,20},{4,16},{8,28},{12,24},{16,4},{20,0},{24,12},{28,8},{1,21},{... | collective-permute-start | bytes 405512 | tf_op jit(solution)/shard_map/ppermute | solution.py:360
  13.1 16.5 %collective-permute-start.6 = (bf16[528,128]{1,0:T(8,128)(2,1)S(1)}, bf16[528,128]{1,0:T(8,128)(2,1)S(1)}, u32[]{:S(2)}, u32[]{:S(2)}) collective-permute-start(bf16[528,128]{1,0:T(8,128)(2,1)S(1)} %get-tuple-element.39), channel_id=1, source_target_pairs={{0,28},{4,24},{8,20},{12,16},{16,12},{20,8},{24,4},{28,0},{1,29},{... | collective-permute-start | bytes 405512 | tf_op jit(solution)/shard_map/ppermute | solution.py:360
  19.5 16.7 %collective-permute-start.9 = (bf16[512,128]{1,0:T(8,128)(2,1)S(1)}, bf16[512,128]{1,0:T(8,128)(2,1)S(1)}, u32[]{:S(2)}, u32[]{:S(2)}) collective-permute-start(bf16[512,128]{1,0:T(8,128)(2,1)S(1)} %get-tuple-element.43), channel_id=1, source_target_pairs={{0,4},{4,0},{8,12},{12,8},{16,20},{20,16},{24,28},{28,24},{1,5},{5... | collective-permute-start | bytes 393224 | tf_op jit(solution)/shard_map/ppermute | solution.py:360
  22.5 15.8 %collective-permute-start.10 = (bf16[512,128]{1,0:T(8,128)(2,1)S(1)}, bf16[512,128]{1,0:T(8,128)(2,1)S(1)}, u32[]{:S(2)}, u32[]{:S(2)}) collective-permute-start(bf16[512,128]{1,0:T(8,128)(2,1)S(1)} %get-tuple-element.44), channel_id=1, source_target_pairs={{0,8},{4,12},{8,0},{12,4},{16,24},{20,28},{24,16},{28,20},{1,9},{5... | collective-permute-start | bytes 393224 | tf_op jit(solution)/shard_map/ppermute | solution.py:360
  22.5 16.6 %collective-permute-start.11 = (bf16[512,128]{1,0:T(8,128)(2,1)S(1)}, bf16[512,128]{1,0:T(8,128)(2,1)S(1)}, u32[]{:S(2)}, u32[]{:S(2)}) collective-permute-start(bf16[512,128]{1,0:T(8,128)(2,1)S(1)} %get-tuple-element.45), channel_id=1, source_target_pairs={{0,12},{4,8},{8,4},{12,0},{16,28},{20,24},{24,20},{28,16},{1,13},{... | collective-permute-start | bytes 393224 | tf_op jit(solution)/shard_map/ppermute | solution.py:360
  29.6 12.7 %collective-permute-start.12 = (bf16[512,128]{1,0:T(8,128)(2,1)S(1)}, bf16[512,128]{1,0:T(8,128)(2,1)S(1)}, u32[]{:S(2)}, u32[]{:S(2)}) collective-permute-start(bf16[512,128]{1,0:T(8,128)(2,1)S(1)} %get-tuple-element.46), channel_id=1, source_target_pairs={{0,16},{4,20},{8,24},{12,28},{16,0},{20,4},{24,8},{28,12},{1,17},{... | collective-permute-start | bytes 393224 | tf_op jit(solution)/shard_map/ppermute | solution.py:360
  31.4 25.5 %collective-permute-start.7 = (bf16[2176,128]{1,0:T(8,128)(2,1)S(1)}, bf16[2176,128]{1,0:T(8,128)(2,1)S(1)}, u32[]{:S(2)}, u32[]{:S(2)}) collective-permute-start(bf16[2176,128]{1,0:T(8,128)(2,1)S(1)} %get-tuple-element.40.refs_2_), channel_id=1, source_target_pairs={{0,4},{4,8},{8,12},{12,13},{13,9},{9,5},{5,1},{1,2},{2,6},{6,10},{... | collective-permute-start | bytes 1671176 | tf_op jit(solution)/shard_map/ppermute | solution.py:377
  36.2 20.8 %collective-permute-start.8 = (bf16[2176,128]{1,0:T(8,128)(2,1)S(1)}, bf16[2176,128]{1,0:T(8,128)(2,1)S(1)}, u32[]{:S(2)}, u32[]{:S(2)}) collective-permute-start(bf16[2176,128]{1,0:T(8,128)(2,1)S(1)} %get-tuple-element.41.refs_1_), channel_id=1, source_target_pairs={{4,0},{8,4},{12,8},{13,12},{9,13},{5,9},{1,5},{2,1},{6,2},{10,6},{... | collective-permute-start | bytes 1671176 | tf_op jit(solution)/shard_map/ppermute | solution.py:378
  38.3 8.9 %collective-permute-start.13 = (bf16[512,128]{1,0:T(8,128)(2,1)S(1)}, bf16[512,128]{1,0:T(8,128)(2,1)S(1)}, u32[]{:S(2)}, u32[]{:S(2)}) collective-permute-start(bf16[512,128]{1,0:T(8,128)(2,1)S(1)} %get-tuple-element.47), channel_id=1, source_target_pairs={{0,20},{4,16},{8,28},{12,24},{16,4},{20,0},{24,12},{28,8},{1,21},{... | collective-permute-start | bytes 393224 | tf_op jit(solution)/shard_map/ppermute | solution.py:360
  39.1 10.6 %collective-permute-start.14 = (bf16[512,128]{1,0:T(8,128)(2,1)S(1)}, bf16[512,128]{1,0:T(8,128)(2,1)S(1)}, u32[]{:S(2)}, u32[]{:S(2)}) collective-permute-start(bf16[512,128]{1,0:T(8,128)(2,1)S(1)} %get-tuple-element.48), channel_id=1, source_target_pairs={{0,24},{4,28},{8,16},{12,20},{16,8},{20,12},{24,0},{28,4},{1,25},{... | collective-permute-start | bytes 393224 | tf_op jit(solution)/shard_map/ppermute | solution.py:360
  42.2 14.0 %collective-permute-start.15 = (bf16[512,128]{1,0:T(8,128)(2,1)S(1)}, bf16[512,128]{1,0:T(8,128)(2,1)S(1)}, u32[]{:S(2)}, u32[]{:S(2)}) collective-permute-start(bf16[512,128]{1,0:T(8,128)(2,1)S(1)} %get-tuple-element.49), channel_id=1, source_target_pairs={{0,28},{4,24},{8,20},{12,16},{16,12},{20,8},{24,4},{28,0},{1,29},{... | collective-permute-start | bytes 393224 | tf_op jit(solution)/shard_map/ppermute | solution.py:360
  59.5 10.4 %collective-permute-start.19 = (bf16[256,128]{1,0:T(8,128)(2,1)S(1)}, bf16[256,128]{1,0:T(8,128)(2,1)S(1)}, u32[]{:S(2)}, u32[]{:S(2)}) collective-permute-start(bf16[256,128]{1,0:T(8,128)(2,1)S(1)} %get-tuple-element.55), channel_id=1, source_target_pairs={{0,16},{4,20},{8,24},{12,28},{16,0},{20,4},{24,8},{28,12},{1,17},{... | collective-permute-start | bytes 196616 | tf_op jit(solution)/shard_map/ppermute | solution.py:360
  62.5 10.2 %collective-permute-start.20 = (bf16[256,128]{1,0:T(8,128)(2,1)S(1)}, bf16[256,128]{1,0:T(8,128)(2,1)S(1)}, u32[]{:S(2)}, u32[]{:S(2)}) collective-permute-start(bf16[256,128]{1,0:T(8,128)(2,1)S(1)} %get-tuple-element.56), channel_id=1, source_target_pairs={{0,20},{4,16},{8,28},{12,24},{16,4},{20,0},{24,12},{28,8},{1,21},{... | collective-permute-start | bytes 196616 | tf_op jit(solution)/shard_map/ppermute | solution.py:360
  63.4 10.2 %collective-permute-start.21 = (bf16[256,128]{1,0:T(8,128)(2,1)S(1)}, bf16[256,128]{1,0:T(8,128)(2,1)S(1)}, u32[]{:S(2)}, u32[]{:S(2)}) collective-permute-start(bf16[256,128]{1,0:T(8,128)(2,1)S(1)} %get-tuple-element.57), channel_id=1, source_target_pairs={{0,24},{4,28},{8,16},{12,20},{16,8},{20,12},{24,0},{28,4},{1,25},{... | collective-permute-start | bytes 196616 | tf_op jit(solution)/shard_map/ppermute | solution.py:360
  63.5 10.1 %collective-permute-start.22 = (bf16[256,128]{1,0:T(8,128)(2,1)S(1)}, bf16[256,128]{1,0:T(8,128)(2,1)S(1)}, u32[]{:S(2)}, u32[]{:S(2)}) collective-permute-start(bf16[256,128]{1,0:T(8,128)(2,1)S(1)} %get-tuple-element.58), channel_id=1, source_target_pairs={{0,28},{4,24},{8,20},{12,16},{16,12},{20,8},{24,4},{28,0},{1,29},{... | collective-permute-start | bytes 196616 | tf_op jit(solution)/shard_map/ppermute | solution.py:360
  69.8 5.0 %collective-permute-start.16 = (bf16[256,128]{1,0:T(8,128)(2,1)S(1)}, bf16[256,128]{1,0:T(8,128)(2,1)S(1)}, u32[]{:S(2)}, u32[]{:S(2)}) collective-permute-start(bf16[256,128]{1,0:T(8,128)(2,1)S(1)} %get-tuple-element.52), channel_id=1, source_target_pairs={{0,4},{4,0},{8,12},{12,8},{16,20},{20,16},{24,28},{28,24},{1,5},{5... | collective-permute-start | bytes 196616 | tf_op jit(solution)/shard_map/ppermute | solution.py:360
  69.9 4.9 %collective-permute-start.17 = (bf16[256,128]{1,0:T(8,128)(2,1)S(1)}, bf16[256,128]{1,0:T(8,128)(2,1)S(1)}, u32[]{:S(2)}, u32[]{:S(2)}) collective-permute-start(bf16[256,128]{1,0:T(8,128)(2,1)S(1)} %get-tuple-element.53), channel_id=1, source_target_pairs={{0,8},{4,12},{8,0},{12,4},{16,24},{20,28},{24,16},{28,20},{1,9},{5... | collective-permute-start | bytes 196616 | tf_op jit(solution)/shard_map/ppermute | solution.py:360
  72.7 3.9 %collective-permute-start.18 = (bf16[256,128]{1,0:T(8,128)(2,1)S(1)}, bf16[256,128]{1,0:T(8,128)(2,1)S(1)}, u32[]{:S(2)}, u32[]{:S(2)}) collective-permute-start(bf16[256,128]{1,0:T(8,128)(2,1)S(1)} %get-tuple-element.54), channel_id=1, source_target_pairs={{0,12},{4,8},{8,4},{12,0},{16,28},{20,24},{24,20},{28,16},{1,13},{... | collective-permute-start | bytes 196616 | tf_op jit(solution)/shard_map/ppermute | solution.py:360
